TPU v7x, 32 devices: a whole 2x2x4 slice. The times are simulated.
32 devices in a mesh: dp: 4 (over y, core), seq: 8 (over z, x).
Axes of the slice: x: 2, y: 2, z: 4, core: 2. Of those that a mesh axis runs over, the one named last changes fastest.
Arguments:
- queries: bfloat16 [4, 1024, 2048], P('dp', 'seq'), may hold values from -40 to 40, as said below
- keys: bfloat16 [4, 1024, 2048], P('dp', 'seq'), may hold values from -40 to 40, as said below
- values: bfloat16 [4, 1024, 2048], P('dp', 'seq'), may hold values from -40 to 40, as said below
- gain: float32 [2048], replicated, may hold values from 0.1 to 1.9
- cotangent: bfloat16 [4, 1024, 2048], P('dp', 'seq'), may hold values from -240 to 240, as said below
Outputs:
- output: bfloat16 [4, 1024, 2048], P('dp', 'seq')
- grad_query: bfloat16 [4, 1024, 2048], P('dp', 'seq')
- grad_key: bfloat16 [4, 1024, 2048], P('dp', 'seq')
- grad_value: bfloat16 [4, 1024, 2048], P('dp', 'seq')
- gain_grad: float32 [2048], replicated
Inputs may be any that keep to these rules, and one draw needn't show every extreme that they name: queries: independent entries with row and feature scales. keys: independent entries with row and feature scales. values: independent entries with row and feature scales. cotangent: independent entries with row and feature scales.
All inputs are finite; a program needn't handle non-finite values.
Results may differ from a plain program's by a relative error of at most 0.0058.
Values may be sent and summed in bfloat16 or wider, within the bound.
No kernel may reach another device: no remote copies, remote signals or barrier semaphores. Data moves between devices by JAX's collectives and lax.ppermute only.
A program may use at most 64 MiB of HBM per device.

v0:
```python
import functools

import jax
import jax.numpy as jnp
from jax import lax
from jax.experimental import pallas as pl
from jax.experimental.pallas import tpu as pltpu
from jax.sharding import PartitionSpec as P

HEADS = 16

EPSILON = 1e-06

F32 = jnp.float32
HALF = jnp.bfloat16


def dot(lhs, rhs, lhs_dim, rhs_dim):
    return lax.dot_general(
        lhs, rhs, (((lhs_dim,), (rhs_dim,)), ((), ())), preferred_element_type=F32
    )


def causal(size):
    rows = lax.broadcasted_iota(jnp.int32, (size, size), 0)
    columns = lax.broadcasted_iota(jnp.int32, (size, size), 1)
    return rows >= columns


def member_of(group):
    return lax.rem(lax.axis_index("seq"), group)


STATE_ORDERS = (((0, 1, 2, 3), (0, 2, 1, 3)), ((0, 2, 1, 3), (0, 1, 2, 3)))
GRAD_ORDERS = (((0, 3, 1, 2), (0, 3, 1, 2)), ((0, 3, 1, 2), (0, 1, 2, 3)))
NORM_ORDERS = (STATE_ORDERS[1], GRAD_ORDERS[0])


def partner_of(order, slot):
    even, odd = order[0][slot], order[1][slot]
    offset = even
    if even != odd:
        offset = jnp.where(lax.rem(lax.axis_index("dp"), 2) == 1, odd, even)
    return member_of(len(order[0])) ^ offset


def block_at(index, size):
    return pl.ds(pl.multiple_of(index * size, size), size)


def gathered(order, piece_refs, size, whole_ref):
    for j, ref in enumerate(piece_refs):
        whole_ref[block_at(partner_of(order, j), size), :] = ref[0:size, :]


def columns(first, count):
    return slice(first, first + count)


def first_state_kernel(head, slot, k_ref, v_ref, piece_ref, k_buffer, v_buffer, arrived):
    width = piece_ref.shape[0]
    source = block_at(partner_of(STATE_ORDERS[0], slot), width)
    copies = [
        pltpu.make_async_copy(k_ref.at[:, source], k_buffer, arrived.at[0]),
        pltpu.make_async_copy(v_ref.at[:, source], v_buffer, arrived.at[1]),
    ]
    for copy in copies:
        copy.start()
    for copy in copies:
        copy.wait()
    for i in range(width // head):
        part = columns(i * head, head)
        piece_ref[part, :] = dot(k_buffer[:, part], v_buffer[:, part], 0, 0).astype(HALF)


def state_kernel(head, slots, k_ref, v_ref, token_ref, *piece_refs):
    del token_ref
    for slot, piece_ref in zip(slots, piece_refs):
        width = piece_ref.shape[0]
        for i in range(width // head):
            part = features_at(STATE_ORDERS[0], slot, i, width, head)
            piece_ref[columns(i * head, head), :] = dot(
                k_ref[:, part], v_ref[:, part], 0, 0
            ).astype(HALF)


def local_kernel(head, q_ref, k_ref, v_ref, scores_ref, intra_ref):
    rows = q_ref.shape[0]
    mask = causal(rows)
    scaling = head ** (-0.5)
    for h in range(HEADS):
        part = columns(h * head, head)
        scores = dot(q_ref[:, part], k_ref[:, part], 1, 1) * scaling
        scores = jnp.where(mask, scores, 0.0).astype(HALF)
        scores_ref[columns(h * rows, rows), :] = scores
        intra_ref[:, part] = dot(scores, v_ref[:, part], 1, 0)


def features_at(order, slot, i, width, head):
    start = partner_of(order, slot) * width + i * head
    return pl.ds(pl.multiple_of(start, head), head)


def attend(head, order, slot, refs, prefix_ref, attended_ref, at, squares, inner):
    q_ref, intra_ref, gain_ref, cot_ref = refs
    scaling = head ** (-0.5)
    width = prefix_ref.shape[0]
    for i in range(width // head):
        part = features_at(order, slot, i, width, head)
        prefix = prefix_ref[columns(i * head, head), :]
        attended = intra_ref[:, part] + scaling * dot(q_ref[:, part], prefix, 1, 0)
        attended_ref[:, part if at is None else columns(i * head, head)] = attended
        scaled = cot_ref[:, part].astype(F32) * gain_ref[:, part]
        squares += attended * attended
        inner += scaled * attended
    return squares, inner


def early_norm_kernel(head, order, *refs):
    prefix_refs, (attended_ref, squares_ref, inner_ref) = refs[4:-3], refs[-3:]
    squares = jnp.zeros(squares_ref.shape, F32)
    inner = jnp.zeros(squares_ref.shape, F32)
    for slot, prefix_ref in enumerate(prefix_refs):
        squares, inner = attend(
            head, order, slot, refs[:4], prefix_ref, attended_ref, None, squares, inner
        )
    squares_ref[...] = squares
    inner_ref[...] = inner


def norm_kernel(head, group, orders, replicas, *refs):
    q_ref, _, gain_ref, cot_ref = refs[:4]
    early_ref, squares_ref, inner_ref, prefix_ref = refs[4:8]
    late_ref, inverse_ref, grad_ref = refs[8:11]
    piece_refs = refs[11 : 11 + group]
    gain_grad_ref, gain_rows_ref = refs[11 + group :]
    features = q_ref.shape[1]
    width = features // group
    odd = lax.rem(lax.axis_index("dp"), 2) == 1
    squares, inner = attend(
        head,
        orders[0],
        group - 1,
        refs[:4],
        prefix_ref,
        late_ref,
        0,
        squares_ref[...],
        inner_ref[...],
    )
    inverse = lax.rsqrt(
        jnp.sum(squares, axis=1, keepdims=True) * (1.0 / features) + EPSILON
    )
    inner_mean = jnp.sum(inner, axis=1, keepdims=True) * (1.0 / features) * inverse
    inverse_ref[...] = jnp.broadcast_to(inverse, inverse_ref.shape)
    scaling = head ** (-0.5)
    for slot in range(group):
        for i in range(width // head):
            part = features_at(orders[1], slot, i, width, head)
            local = columns(i * head, head)
            late = [order[slot] == before[-1] for before, order in zip(*orders)]
            attended = late_ref[:, local] if late[0] else early_ref[:, part]
            if late[0] != late[1]:
                other = late_ref[:, local] if late[1] else early_ref[:, part]
                attended = jnp.where(odd, other, attended)
            normalized = attended * inverse
            upstream = cot_ref[:, part].astype(F32)
            gain_grad_ref[:, part] = jnp.sum(
                upstream * normalized, axis=0, keepdims=True
            ) * (1.0 / replicas)
            scaled = upstream * gain_ref[:, part]
            grad = ((scaled - normalized * inner_mean) * inverse).astype(HALF)
            grad_ref[:, part] = grad
            piece_refs[slot][local, :] = (
                scaling * dot(q_ref[:, part], grad, 0, 0)
            ).astype(HALF)
    for h in range(HEADS):
        gain_rows_ref[h : h + 1, :] = gain_grad_ref[:, columns(h * head, head)]
    for ref in piece_refs:
        put_wide_rows(ref, width, gain_rows_ref[...])


def backward_kernel(head, group, *refs):
    q_ref, k_ref, v_ref, scores_ref, grad_ref = refs[:5]
    early_ref, late_ref, inverse_ref, gain_ref = refs[5:9]
    prefix_refs = refs[9 : 9 + group]
    out_ref, grad_query_ref, key_part_ref, value_part_ref, token_ref = refs[
        9 + group : 14 + group
    ]
    whole_ref = refs[14 + group]
    rows = q_ref.shape[0]
    mask = causal(rows)
    scaling = head ** (-0.5)
    gathered(STATE_ORDERS[1], prefix_refs, prefix_refs[0].shape[0], whole_ref)
    inverse = inverse_ref[...]
    width = late_ref.shape[1]
    for slot in range(group):
        for i in range(width // head):
            part = features_at(STATE_ORDERS[1], slot, i, width, head)
            if slot == group - 1:
                attended = late_ref[:, columns(i * head, head)]
            else:
                attended = early_ref[:, part]
            out_ref[:, part] = (gain_ref[:, part] * (attended * inverse)).astype(HALF)
    for h in range(HEADS):
        part = columns(h * head, head)
        grad = grad_ref[:, part]
        grad_scores = dot(grad, v_ref[:, part], 1, 1)
        grad_scores = jnp.where(mask, grad_scores, 0.0).astype(HALF)
        grad_query = dot(grad_scores, k_ref[:, part], 1, 0) + dot(
            grad, whole_ref[part, :], 1, 1
        )
        grad_query_ref[:, part] = (scaling * grad_query).astype(HALF)
        key_part_ref[:, part] = scaling * dot(grad_scores, q_ref[:, part], 0, 0)
        value_part_ref[:, part] = dot(
            scores_ref[columns(h * rows, rows), :], grad, 0, 0
        )
    token_ref[...] = jnp.zeros_like(token_ref)


def final_kernel(head, slots, last, *refs):
    k_ref, v_ref, key_part_ref, value_part_ref = refs[:4]
    suffix_refs = refs[4 : 4 + len(slots)]
    refs = refs[4 + len(slots) :]
    copies = []
    if last:
        gain_grad_ref, total_ref, gain_written = refs[-6], refs[-2], refs[-1]
        total_ref[...] = tree_sum([ref[...] for ref in refs[2:-8]])
        copies.append(pltpu.make_async_copy(total_ref, gain_grad_ref, gain_written))
        copies[0].start()
        out_refs, refs = refs[-8:-6], refs[-5:-2]
    else:
        out_refs, refs = refs[-5:-3], refs[-3:]
    key_buffer, value_buffer, written = refs
    width = key_buffer.shape[2]
    for n, slot in enumerate(slots):
        for i in range(width // head):
            part = features_at(GRAD_ORDERS[1], slot, i, width, head)
            local = columns(i * head, head)
            suffix = suffix_refs[n][local, :]
            key_buffer[n, :, local] = (
                key_part_ref[:, part] + dot(v_ref[:, part], suffix, 1, 1)
            ).astype(HALF)
            value_buffer[n, :, local] = (
                value_part_ref[:, part] + dot(k_ref[:, part], suffix, 1, 0)
            ).astype(HALF)
        for i, buffer in enumerate((key_buffer, value_buffer)):
            copy = pltpu.make_async_copy(
                buffer.at[n],
                out_refs[i].at[:, block_at(partner_of(GRAD_ORDERS[1], slot), width)],
                written.at[i, n],
            )
            copy.start()
            copies.append(copy)
    for copy in copies:
        copy.wait()


def tree_sum(terms):
    while len(terms) > 1:
        terms = [a + b for a, b in zip(terms[::2], terms[1::2])]
    return terms[0]


def wide_rows(ref, start):
    rows = (ref.shape[0] - start) // 2
    high = ref[columns(start, rows), :].astype(F32)
    return high + ref[columns(start + rows, rows), :].astype(F32)


def put_wide_rows(ref, start, value):
    rows = value.shape[0]
    high = value.astype(HALF)
    ref[columns(start, rows), :] = high
    ref[columns(start + rows, rows), :] = (value - high.astype(F32)).astype(HALF)


def total_kernel(size, count, *refs):
    refs, out_refs = refs[:count], refs[count + 1 :]
    total = refs[0][0:size, :].astype(F32)
    for ref in refs[1:]:
        total += ref[0:size, :].astype(F32)
    out_refs[0][0:size, :] = total.astype(HALF)
    if len(out_refs) > 1:
        gain = tree_sum([wide_rows(ref, size) for ref in refs])
        put_wide_rows(out_refs[0], size, gain)
        out_refs[1][...] = wide_rows(out_refs[0], size)


def group_flag(group, reverse, distance):
    index = lax.axis_index("seq") // group
    last = lax.axis_size("seq") // group - 1
    known = index + distance <= last if reverse else index >= distance
    return jnp.where(known, 1.0, 0.0)


def carry_kernel(group, reverse, distance, first, own_ref, moved_ref, out_ref):
    own = own_ref[...].astype(F32)
    if first:
        own = own * group_flag(group, reverse, 1)
    moved = moved_ref[...].astype(F32) * group_flag(group, reverse, distance)
    out_ref[...] = (own + moved).astype(HALF)


def scan_kernel(group, orders, slots, reverse, masked, size, riding, *refs):
    sources = [partner_of(orders[0], j) for j in range(group)]
    carry = refs[0][0:size, :].astype(F32)
    if masked:
        carry = carry * group_flag(group, reverse, 1)
    blocks = [ref[0:size, :].astype(F32) for ref in refs[1 : 1 + group]]
    out_refs = refs[-len(slots) - riding :][: len(slots)]
    for slot, out_ref in zip(slots, out_refs):
        target = partner_of(orders[1], slot)
        total = carry
        for i in range(group):
            known = sources[i] > target if reverse else sources[i] < target
            total += jnp.where(known, 1.0, 0.0) * blocks[i]
        out_ref[...] = total.astype(HALF)
    if riding:
        refs[-1][...] = refs[1 + group][...] + wide_rows(refs[0], size)


VMEM = pl.BlockSpec(memory_space=pltpu.VMEM)
ANY = pl.BlockSpec(memory_space=pl.ANY)
HBM = pl.BlockSpec(memory_space=pltpu.HBM)


def call(kernel, outs, args, matmuls, scratch=(), ins=None, out_specs=None, aliases=None):
    size = sum(a.size * a.dtype.itemsize for a in args)
    size += sum(o.size * o.dtype.itemsize for o in outs)
    ins = ins or {}
    out_specs = out_specs or {}
    return pl.pallas_call(
        kernel,
        out_shape=tuple(outs),
        in_specs=[ins.get(i, VMEM) for i in range(len(args))],
        out_specs=tuple(out_specs.get(i, VMEM) for i in range(len(outs))),
        scratch_shapes=list(scratch),
        input_output_aliases=aliases or {},
        compiler_params=pltpu.CompilerParams(vmem_limit_bytes=16 * 1024 * 1024),
        cost_estimate=pl.CostEstimate(
            flops=2 * 128 * 128 * 128 * HEADS * matmuls,
            bytes_accessed=size,
            transcendentals=0,
        ),
    )(*args)


def swap(array, axis, offset):
    count = lax.axis_size(axis)
    return lax.ppermute(array, axis, [(i, i ^ offset) for i in range(count)])


def own_and_swapped(pieces, order):
    count = lax.axis_size("seq")
    results = [pieces[0]]
    for slot in range(1, len(pieces)):
        pairs = []
        for row in range(lax.axis_size("dp")):
            offset = order[row % 2][slot]
            pairs += [(row * count + i, row * count + (i ^ offset)) for i in range(count)]
        results.append(lax.ppermute(pieces[slot], ("dp", "seq"), pairs))
    return results


def exclusive_scan(pieces, orders, size, reverse, token):
    group = len(pieces)
    count, rows = lax.axis_size("seq"), lax.axis_size("dp")
    groups = count // group
    part = functools.partial
    lanes = pieces[0].shape[1]
    extra = pieces[0].shape[0] - size
    piece = jax.ShapeDtypeStruct((size, lanes), HALF)
    gain_shape = jax.ShapeDtypeStruct((extra // 2, lanes), F32)

    def shifted(array, distance):
        step = -distance if reverse else distance
        pairs = [(i, (i + step) % count) for i in range(count)]
        return lax.ppermute(array, "seq", pairs)

    received = own_and_swapped(pieces, orders[0])
    totals = call(
        part(total_kernel, size, group),
        [jax.ShapeDtypeStruct(pieces[0].shape, HALF)] + [gain_shape] * (extra > 0),
        received + [token],
        0,
        ins={group: ANY},
    )
    total, gains = totals[0], list(totals[1:])
    riding = int(extra > 0 and groups == 2 and rows == 4)
    carry = shifted(total if riding else total[:size], group)
    if riding:
        for offset in (0, group):
            pairs = [
                (row * count + i, (row ^ 2) * count + (i ^ offset))
                for row in range(rows)
                for i in range(count)
            ]
            gains.append(lax.ppermute(gains[0], ("dp", "seq"), pairs))
    elif extra:
        gains = [tree_sum(summed_over("seq", group, gains[0]))]
        gains = [tree_sum(summed_over("dp", 2, gains[0]))]
    distance = 1
    while distance < groups - 1:
        moved = shifted(carry, distance * group)
        kernel = part(
            carry_kernel, group, reverse, distance + (distance == 1), distance == 1
        )
        (carry,) = call(kernel, [piece], [carry, moved], 0)
        distance *= 2
    pieces, after = {}, []
    for slots in ((1,), (2,), (3, 0)):
        adding = riding if 0 in slots else 0
        inputs = [carry] + received + gains[:adding] + after
        sums = call(
            part(scan_kernel, group, orders, slots, reverse, groups <= 2, size, adding),
            [piece] * len(slots) + [gain_shape] * adding,
            inputs,
            0,
            ins={len(inputs) - 1: ANY} if after else {},
        )
        pieces.update(zip(slots, sums))
        after = [sums[0]]
    results = own_and_swapped([pieces[slot] for slot in range(group)], orders[1])
    if riding:
        gains = [sums[-1] + (gains[1] + gains[2])]
    return results, (gains[0] if gains else None)


def summed_over(axis, stride, array):
    count = lax.axis_size(axis)
    terms = [array]
    while stride < count:
        array = tree_sum(terms)
        width = 4 if count // stride % 4 == 0 else 2
        order = sorted(range(1, width), key=lambda i: i % 2)
        moved = {i: swap(array, axis, i * stride) for i in order}
        terms = [array] + [moved[i] for i in range(1, width)]
        stride *= width
    return terms


def per_device(queries, keys, values, gain, cotangent):
    q, k, v, cot = queries[0], keys[0], values[0], cotangent[0]
    rows, features = q.shape
    head = features // HEADS
    group = 4
    width = features // group
    part = functools.partial
    wide = jax.ShapeDtypeStruct((rows, features), F32)
    half = jax.ShapeDtypeStruct((rows, features), HALF)
    square = jax.ShapeDtypeStruct((rows, head), F32)
    piece = jax.ShapeDtypeStruct((width, head), HALF)
    scores_shape = jax.ShapeDtypeStruct((HEADS * rows, rows), HALF)
    gain_shape = jax.ShapeDtypeStruct((HEADS, head), F32)
    token_shape = jax.ShapeDtypeStruct((8, head), F32)
    whole = pltpu.VMEM((features, head), HALF)
    gain_row = gain.reshape(1, features)

    (first,) = call(
        part(first_state_kernel, head, 1),
        [piece],
        [pltpu.with_memory_space_constraint(a, pltpu.HBM) for a in (k, v)],
        1,
        [pltpu.VMEM((rows, width), HALF)] * 2 + [pltpu.SemaphoreType.DMA((2,))],
        ins={0: HBM, 1: HBM},
    )
    slots = (2, 3, 0)
    rest = call(
        part(state_kernel, head, slots), [piece] * 3, [k, v, first], 1, ins={2: ANY}
    )
    pieces = dict(zip(slots, rest))
    pieces[1] = first
    pieces = [pieces[slot] for slot in range(group)]
    scores, intra = call(part(local_kernel, head), [scores_shape, wide], [q, k, v], 2)
    prefix, _ = exclusive_scan(pieces, STATE_ORDERS, width, False, intra)
    message = jax.ShapeDtypeStruct((width + 2 * HEADS, head), HALF)
    sources = [q, intra, gain_row, cot]
    early, squares, inner = call(
        part(early_norm_kernel, head, STATE_ORDERS[1]),
        [wide, square, square],
        sources + prefix[:-1],
        1,
    )
    late, inverse, grad, *pieces = call(
        part(norm_kernel, head, group, NORM_ORDERS, lax.axis_size("dp")),
        [jax.ShapeDtypeStruct((rows, width), F32), square, half] + [message] * group,
        sources + [early, squares, inner, prefix[-1]],
        2,
        [pltpu.VMEM((1, features), F32), pltpu.VMEM((HEADS, head), F32)],
    )
    output, grad_query, key_part, value_part, token = call(
        part(backward_kernel, head, group),
        [half, half, wide, wide, token_shape],
        [q, k, v, scores, grad, early, late, inverse, gain_row] + prefix,
        5,
        [whole],
    )
    suffix, gain_grad = exclusive_scan(pieces, GRAD_ORDERS, width, True, token)
    gains = [gain_grad, swap(gain_grad, "dp", 1)]
    inputs = [k, v, key_part, value_part]
    outs = []
    for slots in ((0, 1), (2,), (3,)):
        last = group - 1 in slots
        at = len(inputs) + len(slots)
        results = call(
            part(final_kernel, head, slots, last),
            [half, half] + [gain_shape] * last,
            inputs + [suffix[slot] for slot in slots] + outs + (gains if last else []),
            1,
            [pltpu.VMEM((len(slots), rows, width), HALF)] * 2
            + [pltpu.SemaphoreType.DMA((2, len(slots)))]
            + [pltpu.VMEM((HEADS, head), F32), pltpu.SemaphoreType.DMA(())] * last,
            ins={at + i: HBM for i in range(len(outs))},
            out_specs={0: HBM, 1: HBM, 2: HBM},
            aliases={at + i: i for i in range(len(outs))},
        )
        outs = list(results[:2])
    grad_key, grad_value, gain_grad = results
    return (
        output[None],
        grad_query[None],
        grad_key[None],
        grad_value[None],
        gain_grad.reshape(features),
    )


def solution(mesh):
    spec = P("dp", "seq", None)
    return jax.shard_map(
        per_device,
        mesh=mesh,
        in_specs=(spec, spec, spec, P(), spec),
        out_specs=(spec, spec, spec, spec, P()),
        check_vma=False,
    )
```

profile of v0, /device:TPU:0, one launch (start us, length us, event | category | flops | bytes accessed | tf_op | source)
XLA Modules:
  0.0 55.8 jit_solution(9852861327924299728)
XLA Ops:
  0.7 1.3 %shard_map.93.token_ref = bf16[512,128]{1,0:T(8,128)(2,1)S(1)} custom-call(bf16[128,2048]{1,0:T(8,128)(2,1)} %bitcast.10, bf16[128,2048]{1,0:T(8,128)(2,1)} %bitcast.17), custom_call_target="tpu_custom_call" | custom-call | flops 67108864 | bytes 1179648 | tf_op jit(solution)/shard_map/pallas_call | solution.py:333
  2.0 3.0 %collective-permute-start = (bf16[512,128]{1,0:T(8,128)(2,1)S(1)}, bf16[512,128]{1,0:T(8,128)(2,1)S(1)}, u32[]{:S(2)}, u32[]{:S(2)}) collective-permute-start(bf16[512,128]{1,0:T(8,128)(2,1)S(1)} %shard_map.93.token_ref), channel_id=1, source_target_pairs={{0,1},{1,0},{2,3},{3,2},{4,5},{5,4},{6,7},{7,6},{8,10},{9,11},{10,... | collective-permute-start | bytes 393224 | tf_op jit(solution)/shard_map/ppermute | solution.py:362
  5.0 0.4 shard_map.94
  5.4 1.6 %collective-permute-start.1 = (bf16[512,128]{1,0:T(8,128)(2,1)S(1)}, bf16[512,128]{1,0:T(8,128)(2,1)S(1)}, u32[]{:S(2)}, u32[]{:S(2)}) collective-permute-start(bf16[512,128]{1,0:T(8,128)(2,1)S(1)} %get-tuple-element.42), channel_id=1, source_target_pairs={{0,2},{1,3},{2,0},{3,1},{4,6},{5,7},{6,4},{7,5},{8,9},{9,8},{10,11... | collective-permute-start | bytes 393224 | tf_op jit(solution)/shard_map/ppermute | solution.py:362
  7.1 2.6 %shard_map.92 = (bf16[2048,128]{1,0:T(8,128)(2,1)S(1)}, f32[128,2048]{1,0:T(8,128)S(1)}) custom-call(bf16[128,2048]{1,0:T(8,128)(2,1)S(1)} %bitcast.24, bf16[128,2048]{1,0:T(8,128)(2,1)S(1)} %bitcast.12, bf16[128,2048]{1,0:T(8,128)(2,1)S(1)} %bitcast.19), custom_call_target="tpu_custom_call" | custom-call | flops 134217728 | bytes 3145728 | tf_op jit(solution)/shard_map/pallas_call | solution.py:333
  9.7 2.0 %collective-permute-done.1.refs_2_.refs_3_ = bf16[512,128]{1,0:T(8,128)(2,1)S(1)} collective-permute-done((bf16[512,128]{1,0:T(8,128)(2,1)S(1)}, bf16[512,128]{1,0:T(8,128)(2,1)S(1)}, u32[]{:S(2)}, u32[]{:S(2)}) %collective-permute-start.1) | collective-permute-done | bytes 131104 | tf_op jit(solution)/shard_map/ppermute | solution.py:362
  11.7 1.2 %collective-permute-done.2.refs_3_.refs_4_ = bf16[512,128]{1,0:T(8,128)(2,1)S(1)} collective-permute-done((bf16[512,128]{1,0:T(8,128)(2,1)S(1)}, bf16[512,128]{1,0:T(8,128)(2,1)S(1)}, u32[]{:S(2)}, u32[]{:S(2)}) %collective-permute-start.2) | collective-permute-done | bytes 131104 | tf_op jit(solution)/shard_map/ppermute | solution.py:362
  12.9 3.0 %collective-permute-start.3 = (bf16[512,128]{1,0:T(8,128)(2,1)S(1)}, bf16[512,128]{1,0:T(8,128)(2,1)S(1)}, u32[]{:S(2)}, u32[]{:S(2)}) collective-permute-start(bf16[512,128]{1,0:T(8,128)(2,1)S(1)} %shard_map.95), channel_id=1, source_target_pairs={{0,4},{1,5},{2,6},{3,7},{4,0},{5,1},{6,2},{7,3},{8,12},{9,13},{10,... | collective-permute-start | bytes 393224 | tf_op jit(solution)/shard_map/ppermute | solution.py:379
  15.9 5.3 %collective-permute-done.3.refs_0_ = bf16[512,128]{1,0:T(8,128)(2,1)S(1)} collective-permute-done((bf16[512,128]{1,0:T(8,128)(2,1)S(1)}, bf16[512,128]{1,0:T(8,128)(2,1)S(1)}, u32[]{:S(2)}, u32[]{:S(2)}) %collective-permute-start.3) | collective-permute-done | bytes 131104 | tf_op jit(solution)/shard_map/ppermute | solution.py:379
  21.5 0.9 %collective-permute-start.5 = (bf16[512,128]{1,0:T(8,128)(2,1)S(1)}, bf16[512,128]{1,0:T(8,128)(2,1)S(1)}, u32[]{:S(2)}, u32[]{:S(2)}) collective-permute-start(bf16[512,128]{1,0:T(8,128)(2,1)S(1)} %shard_map.97.refs_5_), channel_id=1, source_target_pairs={{0,1},{1,0},{2,3},{3,2},{4,5},{5,4},{6,7},{7,6},{8,10},{9,11},{10,... | collective-permute-start | bytes 393224 | tf_op jit(solution)/shard_map/ppermute | solution.py:362
  22.7 2.7 %collective-permute-start.6 = (bf16[512,128]{1,0:T(8,128)(2,1)S(1)}, bf16[512,128]{1,0:T(8,128)(2,1)S(1)}, u32[]{:S(2)}, u32[]{:S(2)}) collective-permute-start(bf16[512,128]{1,0:T(8,128)(2,1)S(1)} %get-tuple-element.48), channel_id=1, source_target_pairs={{0,3},{1,2},{2,1},{3,0},{4,7},{5,6},{6,5},{7,4},{8,11},{9,10},{10,... | collective-permute-start | bytes 393224 | tf_op jit(solution)/shard_map/ppermute | solution.py:362
  25.4 2.7 %collective-permute-done.5.refs_6_.refs_11_ = bf16[512,128]{1,0:T(8,128)(2,1)S(1)} collective-permute-done((bf16[512,128]{1,0:T(8,128)(2,1)S(1)}, bf16[512,128]{1,0:T(8,128)(2,1)S(1)}, u32[]{:S(2)}, u32[]{:S(2)}) %collective-permute-start.5) | collective-permute-done | bytes 131104 | tf_op jit(solution)/shard_map/ppermute | solution.py:362
  28.1 0.4 shard_map.99
  28.6 0.9 %collective-permute-done.6.refs_7_.refs_12_ = bf16[512,128]{1,0:T(8,128)(2,1)S(1)} collective-permute-done((bf16[512,128]{1,0:T(8,128)(2,1)S(1)}, bf16[512,128]{1,0:T(8,128)(2,1)S(1)}, u32[]{:S(2)}, u32[]{:S(2)}) %collective-permute-start.6) | collective-permute-done | bytes 131104 | tf_op jit(solution)/shard_map/ppermute | solution.py:362
  29.5 1.0 %shard_map.100 = (f32[128,512]{1,0:T(8,128)S(1)}, f32[128,128]{1,0:T(8,128)S(1)}, bf16[128,2048]{1,0:T(8,128)(2,1)S(1)}, bf16[544,128]{1,0:T(8,128)(2,1)S(1)}, b...) custom-call(bf16[128,2048]{1,0:T(8,128)(2,1)S(1)} %bitcast.26, ...), custom_call_target="tpu_custom_call" | custom-call | flops 134217728 | bytes 4825088 | tf_op jit(solution)/shard_map/pallas_call | solution.py:333
  30.5 1.8 %collective-permute-start.7 = (bf16[544,128]{1,0:T(8,128)(2,1)S(1)}, bf16[544,128]{1,0:T(8,128)(2,1)S(1)}, u32[]{:S(2)}, u32[]{:S(2)}) collective-permute-start(bf16[544,128]{1,0:T(8,128)(2,1)S(1)} %get-tuple-element.57), channel_id=1, source_target_pairs={{0,3},{1,2},{2,1},{3,0},{4,7},{5,6},{6,5},{7,4},{8,11},{9,10},{10,... | collective-permute-start | bytes 417800 | tf_op jit(solution)/shard_map/ppermute | solution.py:362
  32.3 1.0 %collective-permute-start.8 = (bf16[544,128]{1,0:T(8,128)(2,1)S(1)}, bf16[544,128]{1,0:T(8,128)(2,1)S(1)}, u32[]{:S(2)}, u32[]{:S(2)}) collective-permute-start(bf16[544,128]{1,0:T(8,128)(2,1)S(1)} %get-tuple-element.58), channel_id=1, source_target_pairs={{0,1},{1,0},{2,3},{3,2},{4,5},{5,4},{6,7},{7,6},{8,9},{9,8},{10,11... | collective-permute-start | bytes 417800 | tf_op jit(solution)/shard_map/ppermute | solution.py:362
  33.3 0.7 %collective-permute-start.9 = (bf16[544,128]{1,0:T(8,128)(2,1)S(1)}, bf16[544,128]{1,0:T(8,128)(2,1)S(1)}, u32[]{:S(2)}, u32[]{:S(2)}) collective-permute-start(bf16[544,128]{1,0:T(8,128)(2,1)S(1)} %get-tuple-element.59), channel_id=1, source_target_pairs={{0,2},{1,3},{2,0},{3,1},{4,6},{5,7},{6,4},{7,5},{8,10},{9,11},{10,... | collective-permute-start | bytes 417800 | tf_op jit(solution)/shard_map/ppermute | solution.py:362
  34.1 3.5 %shard_map.101 = (bf16[128,2048]{1,0:T(8,128)(2,1)}, bf16[128,2048]{1,0:T(8,128)(2,1)}, f32[128,2048]{1,0:T(8,128)S(1)}, f32[128,2048]{1,0:T(8,128)S(1)}, f32[8,128]{1,0:T(8,128)S(1)}) custom-call(bf16[128,2048]{1,0:T(8,128)(2,1)S(1)} %bitcast.27, bf16[128,2048]{1,0:T(8,128)(2,1)S(1)} %bitcast.13, bf16[128,2048]{1,0:T(8,128)(2,1)S(1)} %bitcast.20, ...), custom_call_target="tpu_custom_call" | custom-call | flops 335544320 | bytes 7680000 | tf_op jit(solution)/shard_map/pallas_call | solution.py:333
  37.6 0.9 %collective-permute-done.8.refs_2_.refs_3_ = bf16[544,128]{1,0:T(8,128)(2,1)S(1)} collective-permute-done((bf16[544,128]{1,0:T(8,128)(2,1)S(1)}, bf16[544,128]{1,0:T(8,128)(2,1)S(1)}, u32[]{:S(2)}, u32[]{:S(2)}) %collective-permute-start.8) | collective-permute-done | bytes 139296 | tf_op jit(solution)/shard_map/ppermute | solution.py:362
  38.8 1.8 %collective-permute-start.10 = (bf16[544,128]{1,0:T(8,128)(2,1)S(1)}, bf16[544,128]{1,0:T(8,128)(2,1)S(1)}, u32[]{:S(2)}, u32[]{:S(2)}) collective-permute-start(bf16[544,128]{1,0:T(8,128)(2,1)S(1)} %get-tuple-element.61), channel_id=1, source_target_pairs={{0,4},{1,5},{2,6},{3,7},{4,0},{5,1},{6,2},{7,3},{8,12},{9,13},{10,... | collective-permute-start | bytes 417800 | tf_op jit(solution)/shard_map/ppermute | solution.py:379
  40.6 2.0 %collective-permute-start.15 = (f32[16,128]{1,0:T(8,128)S(1)}, f32[16,128]{1,0:T(8,128)S(1)}, u32[]{:S(2)}, u32[]{:S(2)}) collective-permute-start(f32[16,128]{1,0:T(8,128)S(1)} %get-tuple-element.62.refs_5_), channel_id=1, source_target_pairs={{0,20},{1,21},{2,22},{3,23},{4,16},{5,17},{6,18},{7,19},{8,28},{9,... | collective-permute-start | bytes 24584 | tf_op jit(solution)/shard_map/ppermute | solution.py:399
  42.6 0.7 %collective-permute-start.14 = (f32[16,128]{1,0:T(8,128)S(1)}, f32[16,128]{1,0:T(8,128)S(1)}, u32[]{:S(2)}, u32[]{:S(2)}) collective-permute-start(f32[16,128]{1,0:T(8,128)S(1)} %get-tuple-element.62.refs_5_), channel_id=1, source_target_pairs={{0,16},{1,17},{2,18},{3,19},{4,20},{5,21},{6,22},{7,23},{8,24},{9,... | collective-permute-start | bytes 24584 | tf_op jit(solution)/shard_map/ppermute | solution.py:399
  43.2 3.1 %collective-permute-done.10.refs_0_ = bf16[544,128]{1,0:T(8,128)(2,1)S(1)} collective-permute-done((bf16[544,128]{1,0:T(8,128)(2,1)S(1)}, bf16[544,128]{1,0:T(8,128)(2,1)S(1)}, u32[]{:S(2)}, u32[]{:S(2)}) %collective-permute-start.10) | collective-permute-done | bytes 139296 | tf_op jit(solution)/shard_map/ppermute | solution.py:379
  46.5 1.2 %collective-permute-start.13 = (bf16[512,128]{1,0:T(8,128)(2,1)S(1)}, bf16[512,128]{1,0:T(8,128)(2,1)S(1)}, u32[]{:S(2)}, u32[]{:S(2)}) collective-permute-start(bf16[512,128]{1,0:T(8,128)(2,1)S(1)} %shard_map.103.refs_5_), channel_id=1, source_target_pairs={{0,3},{1,2},{2,1},{3,0},{4,7},{5,6},{6,5},{7,4},{8,9},{9,8},{10,11... | collective-permute-start | bytes 393224 | tf_op jit(solution)/shard_map/ppermute | solution.py:362
  47.8 0.3 collective-permute-start.12
  48.1 0.3 shard_map.105
  48.3 2.2 %collective-permute-start.11 = (bf16[512,128]{1,0:T(8,128)(2,1)S(1)}, bf16[512,128]{1,0:T(8,128)(2,1)S(1)}, u32[]{:S(2)}, u32[]{:S(2)}) collective-permute-start(bf16[512,128]{1,0:T(8,128)(2,1)S(1)} %get-tuple-element.63), channel_id=1, source_target_pairs={{0,2},{1,3},{2,0},{3,1},{4,6},{5,7},{6,4},{7,5},{8,11},{9,10},{10,... | collective-permute-start | bytes 393224 | tf_op jit(solution)/shard_map/ppermute | solution.py:362
  50.6 1.9 %collective-permute-done.13.refs_5_ = bf16[512,128]{1,0:T(8,128)(2,1)S(1)} collective-permute-done((bf16[512,128]{1,0:T(8,128)(2,1)S(1)}, bf16[512,128]{1,0:T(8,128)(2,1)S(1)}, u32[]{:S(2)}, u32[]{:S(2)}) %collective-permute-start.13) | collective-permute-done | bytes 131104 | tf_op jit(solution)/shard_map/ppermute | solution.py:362
  52.5 1.1 %shard_map.106 = (bf16[128,2048]{1,0:T(8,128)(2,1)}, bf16[128,2048]{1,0:T(8,128)(2,1)}) custom-call(bf16[128,2048]{1,0:T(8,128)(2,1)S(1)} %bitcast.14, bf16[128,2048]{1,0:T(8,128)(2,1)S(1)} %bitcast.21, f32[128,2048]{1,0:T(8,128)S(1)} %get-tuple-element.54.refs_2_, f32[128,2048]{1,0:T(8,128)S(1)} %get-tuple-element.55.refs_3_, ...), custom_call_target="tpu_custom_call" | custom-call | flops 67108864 | bytes 4456448 | tf_op jit(solution)/shard_map/pallas_call | solution.py:333
  53.8 1.0 %shard_map.107 = (bf16[128,2048]{1,0:T(8,128)(2,1)}, bf16[128,2048]{1,0:T(8,128)(2,1)}) custom-call(bf16[128,2048]{1,0:T(8,128)(2,1)S(1)} %bitcast.15, bf16[128,2048]{1,0:T(8,128)(2,1)S(1)} %bitcast.22, f32[128,2048]{1,0:T(8,128)S(1)} %get-tuple-element.54.refs_2_, ...), custom_call_target="tpu_custom_call", output_to_operand_aliasing={{0}: (5, {}), {1}: (6, {})} | custom-call | flops 67108864 | bytes 5373952 | tf_op jit(solution)/shard_map/pallas_call | solution.py:333
  54.8 1.0 %shard_map.108 = (bf16[128,2048]{1,0:T(8,128)(2,1)}, bf16[128,2048]{1,0:T(8,128)(2,1)}, f32[16,128]{1,0:T(8,128)}) custom-call(bf16[128,2048]{1,0:T(8,128)(2,1)S(1)} %bitcast.16, bf16[128,2048]{1,0:T(8,128)(2,1)S(1)} %bitcast.23, f32[128,2048]{1,0:T(8,128)S(1)} %get-tuple-element.54.refs_2_, ...), custom_call_target="tpu_custom_call", output_to_operand_aliasing={{0}: (5, {}), {1}: (6, {})} | custom-call | flops 67108864 | bytes 5398528 | tf_op jit(solution)/shard_map/pallas_call | solution.py:333
  (30 shorter events, 1.7 us)
Async XLA Ops:
  0.6 4.3 %copy-start = (bf16[1,128,2048]{2,1,0:T(8,128)(2,1)S(1)}, bf16[1,128,2048]{2,1,0:T(8,128)(2,1)}, u32[]{:S(2)}) copy-start(bf16[1,128,2048]{2,1,0:T(8,128)(2,1)} %param.6) | copy-start | bytes 1572868
  0.6 4.3 %copy-start.1 = (bf16[1,128,2048]{2,1,0:T(8,128)(2,1)S(1)}, bf16[1,128,2048]{2,1,0:T(8,128)(2,1)}, u32[]{:S(2)}) copy-start(bf16[1,128,2048]{2,1,0:T(8,128)(2,1)} %param.7) | copy-start | bytes 1572868
  2.0 5.1 %copy-start.2 = (bf16[1,128,2048]{2,1,0:T(8,128)(2,1)S(1)}, bf16[1,128,2048]{2,1,0:T(8,128)(2,1)}, u32[]{:S(2)}) copy-start(bf16[1,128,2048]{2,1,0:T(8,128)(2,1)} %param.5) | copy-start | bytes 1572868
  2.0 7.7 %collective-permute-start = (bf16[512,128]{1,0:T(8,128)(2,1)S(1)}, bf16[512,128]{1,0:T(8,128)(2,1)S(1)}, u32[]{:S(2)}, u32[]{:S(2)}) collective-permute-start(bf16[512,128]{1,0:T(8,128)(2,1)S(1)} %shard_map.93.token_ref), channel_id=1, source_target_pairs={{0,1},{1,0},{2,3},{3,2},{4,5},{5,4},{6,7},{7,6},{8,10},{9,11},{10,... | collective-permute-start | bytes 393224 | tf_op jit(solution)/shard_map/ppermute | solution.py:362
  5.4 6.3 %collective-permute-start.1 = (bf16[512,128]{1,0:T(8,128)(2,1)S(1)}, bf16[512,128]{1,0:T(8,128)(2,1)S(1)}, u32[]{:S(2)}, u32[]{:S(2)}) collective-permute-start(bf16[512,128]{1,0:T(8,128)(2,1)S(1)} %get-tuple-element.42), channel_id=1, source_target_pairs={{0,2},{1,3},{2,0},{3,1},{4,6},{5,7},{6,4},{7,5},{8,9},{9,8},{10,11... | collective-permute-start | bytes 393224 | tf_op jit(solution)/shard_map/ppermute | solution.py:362
  7.0 5.9 %collective-permute-start.2 = (bf16[512,128]{1,0:T(8,128)(2,1)S(1)}, bf16[512,128]{1,0:T(8,128)(2,1)S(1)}, u32[]{:S(2)}, u32[]{:S(2)}) collective-permute-start(bf16[512,128]{1,0:T(8,128)(2,1)S(1)} %get-tuple-element.43), channel_id=1, source_target_pairs={{0,3},{1,2},{2,1},{3,0},{4,7},{5,6},{6,5},{7,4},{8,11},{9,10},{10,... | collective-permute-start | bytes 393224 | tf_op jit(solution)/shard_map/ppermute | solution.py:362
  12.9 8.3 %collective-permute-start.3 = (bf16[512,128]{1,0:T(8,128)(2,1)S(1)}, bf16[512,128]{1,0:T(8,128)(2,1)S(1)}, u32[]{:S(2)}, u32[]{:S(2)}) collective-permute-start(bf16[512,128]{1,0:T(8,128)(2,1)S(1)} %shard_map.95), channel_id=1, source_target_pairs={{0,4},{1,5},{2,6},{3,7},{4,0},{5,1},{6,2},{7,3},{8,12},{9,13},{10,... | collective-permute-start | bytes 393224 | tf_op jit(solution)/shard_map/ppermute | solution.py:379
  21.5 6.6 %copy-start.3 = (bf16[1,128,2048]{2,1,0:T(8,128)(2,1)S(1)}, bf16[1,128,2048]{2,1,0:T(8,128)(2,1)}, u32[]{:S(2)}) copy-start(bf16[1,128,2048]{2,1,0:T(8,128)(2,1)} %param.9) | copy-start | bytes 1572868
  21.5 6.5 %collective-permute-start.5 = (bf16[512,128]{1,0:T(8,128)(2,1)S(1)}, bf16[512,128]{1,0:T(8,128)(2,1)S(1)}, u32[]{:S(2)}, u32[]{:S(2)}) collective-permute-start(bf16[512,128]{1,0:T(8,128)(2,1)S(1)} %shard_map.97.refs_5_), channel_id=1, source_target_pairs={{0,1},{1,0},{2,3},{3,2},{4,5},{5,4},{6,7},{7,6},{8,10},{9,11},{10,... | collective-permute-start | bytes 393224 | tf_op jit(solution)/shard_map/ppermute | solution.py:362
  22.4 5.7 %collective-permute-start.4 = (bf16[512,128]{1,0:T(8,128)(2,1)S(1)}, bf16[512,128]{1,0:T(8,128)(2,1)S(1)}, u32[]{:S(2)}, u32[]{:S(2)}) collective-permute-start(bf16[512,128]{1,0:T(8,128)(2,1)S(1)} %shard_map.96.refs_5_), channel_id=1, source_target_pairs={{0,2},{1,3},{2,0},{3,1},{4,6},{5,7},{6,4},{7,5},{8,9},{9,8},{10,11... | collective-permute-start | bytes 393224 | tf_op jit(solution)/shard_map/ppermute | solution.py:362
  22.4 5.7 %copy-start.4 = (f32[2048]{0:T(1024)S(1)}, f32[2048]{0:T(1024)}, u32[]{:S(2)}) copy-start(f32[2048]{0:T(1024)} %param.8) | copy-start | bytes 24580
  22.7 6.9 %collective-permute-start.6 = (bf16[512,128]{1,0:T(8,128)(2,1)S(1)}, bf16[512,128]{1,0:T(8,128)(2,1)S(1)}, u32[]{:S(2)}, u32[]{:S(2)}) collective-permute-start(bf16[512,128]{1,0:T(8,128)(2,1)S(1)} %get-tuple-element.48), channel_id=1, source_target_pairs={{0,3},{1,2},{2,1},{3,0},{4,7},{5,6},{6,5},{7,4},{8,11},{9,10},{10,... | collective-permute-start | bytes 393224 | tf_op jit(solution)/shard_map/ppermute | solution.py:362
  30.5 7.0 %collective-permute-start.7 = (bf16[544,128]{1,0:T(8,128)(2,1)S(1)}, bf16[544,128]{1,0:T(8,128)(2,1)S(1)}, u32[]{:S(2)}, u32[]{:S(2)}) collective-permute-start(bf16[544,128]{1,0:T(8,128)(2,1)S(1)} %get-tuple-element.57), channel_id=1, source_target_pairs={{0,3},{1,2},{2,1},{3,0},{4,7},{5,6},{6,5},{7,4},{8,11},{9,10},{10,... | collective-permute-start | bytes 417800 | tf_op jit(solution)/shard_map/ppermute | solution.py:362
  32.3 6.1 %collective-permute-start.8 = (bf16[544,128]{1,0:T(8,128)(2,1)S(1)}, bf16[544,128]{1,0:T(8,128)(2,1)S(1)}, u32[]{:S(2)}, u32[]{:S(2)}) collective-permute-start(bf16[544,128]{1,0:T(8,128)(2,1)S(1)} %get-tuple-element.58), channel_id=1, source_target_pairs={{0,1},{1,0},{2,3},{3,2},{4,5},{5,4},{6,7},{7,6},{8,9},{9,8},{10,11... | collective-permute-start | bytes 417800 | tf_op jit(solution)/shard_map/ppermute | solution.py:362
  33.3 5.3 %collective-permute-start.9 = (bf16[544,128]{1,0:T(8,128)(2,1)S(1)}, bf16[544,128]{1,0:T(8,128)(2,1)S(1)}, u32[]{:S(2)}, u32[]{:S(2)}) collective-permute-start(bf16[544,128]{1,0:T(8,128)(2,1)S(1)} %get-tuple-element.59), channel_id=1, source_target_pairs={{0,2},{1,3},{2,0},{3,1},{4,6},{5,7},{6,4},{7,5},{8,10},{9,11},{10,... | collective-permute-start | bytes 417800 | tf_op jit(solution)/shard_map/ppermute | solution.py:362
  38.8 7.5 %collective-permute-start.10 = (bf16[544,128]{1,0:T(8,128)(2,1)S(1)}, bf16[544,128]{1,0:T(8,128)(2,1)S(1)}, u32[]{:S(2)}, u32[]{:S(2)}) collective-permute-start(bf16[544,128]{1,0:T(8,128)(2,1)S(1)} %get-tuple-element.61), channel_id=1, source_target_pairs={{0,4},{1,5},{2,6},{3,7},{4,0},{5,1},{6,2},{7,3},{8,12},{9,13},{10,... | collective-permute-start | bytes 417800 | tf_op jit(solution)/shard_map/ppermute | solution.py:379
  40.6 10.0 %collective-permute-start.15 = (f32[16,128]{1,0:T(8,128)S(1)}, f32[16,128]{1,0:T(8,128)S(1)}, u32[]{:S(2)}, u32[]{:S(2)}) collective-permute-start(f32[16,128]{1,0:T(8,128)S(1)} %get-tuple-element.62.refs_5_), channel_id=1, source_target_pairs={{0,20},{1,21},{2,22},{3,23},{4,16},{5,17},{6,18},{7,19},{8,28},{9,... | collective-permute-start | bytes 24584 | tf_op jit(solution)/shard_map/ppermute | solution.py:399
  42.6 8.0 %collective-permute-start.14 = (f32[16,128]{1,0:T(8,128)S(1)}, f32[16,128]{1,0:T(8,128)S(1)}, u32[]{:S(2)}, u32[]{:S(2)}) collective-permute-start(f32[16,128]{1,0:T(8,128)S(1)} %get-tuple-element.62.refs_5_), channel_id=1, source_target_pairs={{0,16},{1,17},{2,18},{3,19},{4,20},{5,21},{6,22},{7,23},{8,24},{9,... | collective-permute-start | bytes 24584 | tf_op jit(solution)/shard_map/ppermute | solution.py:399
  46.5 6.0 %collective-permute-start.13 = (bf16[512,128]{1,0:T(8,128)(2,1)S(1)}, bf16[512,128]{1,0:T(8,128)(2,1)S(1)}, u32[]{:S(2)}, u32[]{:S(2)}) collective-permute-start(bf16[512,128]{1,0:T(8,128)(2,1)S(1)} %shard_map.103.refs_5_), channel_id=1, source_target_pairs={{0,3},{1,2},{2,1},{3,0},{4,7},{5,6},{6,5},{7,4},{8,9},{9,8},{10,11... | collective-permute-start | bytes 393224 | tf_op jit(solution)/shard_map/ppermute | solution.py:362
  47.8 6.0 %collective-permute-start.12 = (bf16[512,128]{1,0:T(8,128)(2,1)S(1)}, bf16[512,128]{1,0:T(8,128)(2,1)S(1)}, u32[]{:S(2)}, u32[]{:S(2)}) collective-permute-start(bf16[512,128]{1,0:T(8,128)(2,1)S(1)} %shard_map.104.refs_6_), channel_id=1, source_target_pairs={{0,1},{1,0},{2,3},{3,2},{4,5},{5,4},{6,7},{7,6},{8,10},{9,11},{10,... | collective-permute-start | bytes 393224 | tf_op jit(solution)/shard_map/ppermute | solution.py:362
  48.3 6.5 %collective-permute-start.11 = (bf16[512,128]{1,0:T(8,128)(2,1)S(1)}, bf16[512,128]{1,0:T(8,128)(2,1)S(1)}, u32[]{:S(2)}, u32[]{:S(2)}) collective-permute-start(bf16[512,128]{1,0:T(8,128)(2,1)S(1)} %get-tuple-element.63), channel_id=1, source_target_pairs={{0,2},{1,3},{2,0},{3,1},{4,6},{5,7},{6,4},{7,5},{8,11},{9,10},{10,... | collective-permute-start | bytes 393224 | tf_op jit(solution)/shard_map/ppermute | solution.py:362
  50.6 4.2 %collective-permute-start.16 = (f32[16,128]{1,0:T(8,128)S(1)}, f32[16,128]{1,0:T(8,128)S(1)}, u32[]{:S(2)}, u32[]{:S(2)}) collective-permute-start(f32[16,128]{1,0:T(8,128)S(1)} %add_add_fusion.refs_7_), channel_id=1, source_target_pairs={{0,8},{8,0},{16,24},{24,16},{1,9},{9,1},{17,25},{25,17},{2,10},{10... | collective-permute-start | bytes 24584 | tf_op jit(solution)/shard_map/ppermute | solution.py:351
where the time goes:
time: 55.9 us; the launch traced here: 55.8 us
  starting transfers between devices  23 us (41%)
  waiting for transfers between devices  18.5 us (33%)
  Pallas kernels  13.5 us (24%)
  between operations  0.78 us (1%)
    ppermute x12, starting transfers between devices, own_and_swapped(): results.append(lax.ppermute(pieces[slot], ('dp', 'seq'), pairs))  15.5 us
    pallas_call x17, Pallas kernels, call(): pl.pallas_call(kernel, out_shape=tuple(outs), in_specs=[ins.get(i, VMEM)...  13.5 us
    ppermute x12, waiting for transfers between devices, own_and_swapped(): results.append(lax.ppermute(pieces[slot], ('dp', 'seq'), pairs))  10.1 us
    ppermute x2, waiting for transfers between devices, shifted(): return lax.ppermute(array, 'seq', pairs)  8.4 us
    ppermute x2, starting transfers between devices, shifted(): return lax.ppermute(array, 'seq', pairs)  4.74 us
    ppermute x2, starting transfers between devices, exclusive_scan(): gains.append(lax.ppermute(gains[0], ('dp', 'seq'), pairs))  2.66 us
  transfers between devices with their start and end apart: 17, of which 11 were waited for; matrix products, arithmetic and copies ran while one was open for 0% of the time, Pallas kernels for 17%

commit v1 on v0

--- a/solution.py
+++ b/solution.py
@@ -31,17 +31,32 @@
     return lax.rem(lax.axis_index("seq"), group)
 
 
-STATE_ORDERS = (((0, 1, 2, 3), (0, 2, 1, 3)), ((0, 2, 1, 3), (0, 1, 2, 3)))
-GRAD_ORDERS = (((0, 3, 1, 2), (0, 3, 1, 2)), ((0, 3, 1, 2), (0, 1, 2, 3)))
+STATE_ORDERS = (
+    (((0, 1, 2, 3), (0, 2, 1, 3)), ((0, 1, 2, 3), (0, 2, 1, 3))),
+    (((0, 2, 1, 3), (0, 1, 2, 3)), ((0, 2, 1, 3), (0, 1, 2, 3))),
+)
+GRAD_ORDERS = (
+    (((0, 1, 2, 3), (0, 2, 1, 3)), ((0, 3, 1, 2), (0, 3, 1, 2))),
+    (((0, 3, 1, 2), (0, 1, 2, 3)), ((0, 3, 1, 2), (0, 1, 2, 3))),
+)
 NORM_ORDERS = (STATE_ORDERS[1], GRAD_ORDERS[0])
 
 
+def picked(table, group):
+    (first, second), (third, fourth) = table
+    if first == second == third == fourth:
+        return first
+    odd = lax.rem(lax.axis_index("dp"), 2) == 1
+    odd_group = lax.rem(lax.axis_index("seq") // group, 2) == 1
+    return jnp.where(
+        odd_group, jnp.where(odd, fourth, third), jnp.where(odd, second, first)
+    )
+
+
 def partner_of(order, slot):
-    even, odd = order[0][slot], order[1][slot]
-    offset = even
-    if even != odd:
-        offset = jnp.where(lax.rem(lax.axis_index("dp"), 2) == 1, odd, even)
-    return member_of(len(order[0])) ^ offset
+    group = len(order[0][0])
+    offset = picked([[row[slot] for row in rows] for rows in order], group)
+    return member_of(group) ^ offset
 
 
 def block_at(index, size):
@@ -136,7 +151,6 @@
     gain_grad_ref, gain_rows_ref = refs[11 + group :]
     features = q_ref.shape[1]
     width = features // group
-    odd = lax.rem(lax.axis_index("dp"), 2) == 1
     squares, inner = attend(
         head,
         orders[0],
@@ -158,11 +172,16 @@
         for i in range(width // head):
             part = features_at(orders[1], slot, i, width, head)
             local = columns(i * head, head)
-            late = [order[slot] == before[-1] for before, order in zip(*orders)]
-            attended = late_ref[:, local] if late[0] else early_ref[:, part]
-            if late[0] != late[1]:
-                other = late_ref[:, local] if late[1] else early_ref[:, part]
-                attended = jnp.where(odd, other, attended)
+            late = [
+                [int(row[slot] == before[-1]) for before, row in zip(*rows)]
+                for rows in zip(*orders)
+            ]
+            if sum(late[0] + late[1]) in (0, 4):
+                attended = late_ref[:, local] if late[0][0] else early_ref[:, part]
+            else:
+                attended = jnp.where(
+                    picked(late, group) == 1, late_ref[:, local], early_ref[:, part]
+                )
             normalized = attended * inverse
             upstream = cot_ref[:, part].astype(F32)
             gain_grad_ref[:, part] = jnp.sum(
@@ -352,13 +371,14 @@
 
 
 def own_and_swapped(pieces, order):
-    count = lax.axis_size("seq")
+    count, group = lax.axis_size("seq"), len(pieces)
     results = [pieces[0]]
-    for slot in range(1, len(pieces)):
+    for slot in range(1, group):
         pairs = []
         for row in range(lax.axis_size("dp")):
-            offset = order[row % 2][slot]
-            pairs += [(row * count + i, row * count + (i ^ offset)) for i in range(count)]
+            for i in range(count):
+                offset = order[i // group % 2][row % 2][slot]
+                pairs.append((row * count + i, row * count + (i ^ offset)))
         results.append(lax.ppermute(pieces[slot], ("dp", "seq"), pairs))
     return results
 

time: 55.9 us -> 56.1 us (level)
  transfers between devices with their start and end apart: 17 -> 17, of which waited for: 11 -> 9; matrix products, arithmetic and copies ran while one was open for 0% -> 0% of each run, Pallas kernels for 17% -> 17%
where the time goes in v1:
time: 56.1 us; the launch traced here: 56 us
  starting transfers between devices  23 us (41%)
  waiting for transfers between devices  18.6 us (33%)
  Pallas kernels  13.5 us (24%)
  between operations  0.79 us (1%)
    ppermute x12, starting transfers between devices, own_and_swapped(): results.append(lax.ppermute(pieces[slot], ('dp', 'seq'), pairs))  15.5 us
    pallas_call x17, Pallas kernels, call(): pl.pallas_call(kernel, out_shape=tuple(outs), in_specs=[ins.get(i, VMEM)...  13.5 us
    ppermute x12, waiting for transfers between devices, own_and_swapped(): results.append(lax.ppermute(pieces[slot], ('dp', 'seq'), pairs))  10.2 us
    ppermute x2, waiting for transfers between devices, shifted(): return lax.ppermute(array, 'seq', pairs)  8.38 us
    ppermute x2, starting transfers between devices, shifted(): return lax.ppermute(array, 'seq', pairs)  4.42 us
    ppermute x2, starting transfers between devices, exclusive_scan(): gains.append(lax.ppermute(gains[0], ('dp', 'seq'), pairs))  2.99 us
  transfers between devices with their start and end apart: 17, of which 9 were waited for; matrix products, arithmetic and copies ran while one was open for 0% of the time, Pallas kernels for 17%

profile of v1, /device:TPU:0, one launch (start us, length us, event | category | flops | bytes accessed | tf_op | source)
XLA Modules:
  0.0 56.0 jit_solution(2178030921047120108)
XLA Ops:
  0.7 1.3 %shard_map.93.token_ref = bf16[512,128]{1,0:T(8,128)(2,1)S(1)} custom-call(bf16[128,2048]{1,0:T(8,128)(2,1)} %bitcast.10, bf16[128,2048]{1,0:T(8,128)(2,1)} %bitcast.17), custom_call_target="tpu_custom_call" | custom-call | flops 67108864 | bytes 1179648 | tf_op jit(solution)/shard_map/pallas_call | solution.py:352
  2.0 3.0 %collective-permute-start = (bf16[512,128]{1,0:T(8,128)(2,1)S(1)}, bf16[512,128]{1,0:T(8,128)(2,1)S(1)}, u32[]{:S(2)}, u32[]{:S(2)}) collective-permute-start(bf16[512,128]{1,0:T(8,128)(2,1)S(1)} %shard_map.93.token_ref), channel_id=1, source_target_pairs={{0,1},{1,0},{2,3},{3,2},{4,5},{5,4},{6,7},{7,6},{8,10},{9,11},{10,... | collective-permute-start | bytes 393224 | tf_op jit(solution)/shard_map/ppermute | solution.py:382
  5.0 0.4 shard_map.94
  5.4 1.6 %collective-permute-start.1 = (bf16[512,128]{1,0:T(8,128)(2,1)S(1)}, bf16[512,128]{1,0:T(8,128)(2,1)S(1)}, u32[]{:S(2)}, u32[]{:S(2)}) collective-permute-start(bf16[512,128]{1,0:T(8,128)(2,1)S(1)} %get-tuple-element.42), channel_id=1, source_target_pairs={{0,2},{1,3},{2,0},{3,1},{4,6},{5,7},{6,4},{7,5},{8,9},{9,8},{10,11... | collective-permute-start | bytes 393224 | tf_op jit(solution)/shard_map/ppermute | solution.py:382
  7.1 2.6 %shard_map.92 = (bf16[2048,128]{1,0:T(8,128)(2,1)S(1)}, f32[128,2048]{1,0:T(8,128)S(1)}) custom-call(bf16[128,2048]{1,0:T(8,128)(2,1)S(1)} %bitcast.24, bf16[128,2048]{1,0:T(8,128)(2,1)S(1)} %bitcast.12, bf16[128,2048]{1,0:T(8,128)(2,1)S(1)} %bitcast.19), custom_call_target="tpu_custom_call" | custom-call | flops 134217728 | bytes 3145728 | tf_op jit(solution)/shard_map/pallas_call | solution.py:352
  9.7 2.0 %collective-permute-done.1.refs_2_.refs_3_ = bf16[512,128]{1,0:T(8,128)(2,1)S(1)} collective-permute-done((bf16[512,128]{1,0:T(8,128)(2,1)S(1)}, bf16[512,128]{1,0:T(8,128)(2,1)S(1)}, u32[]{:S(2)}, u32[]{:S(2)}) %collective-permute-start.1) | collective-permute-done | bytes 131104 | tf_op jit(solution)/shard_map/ppermute | solution.py:382
  11.7 1.2 %collective-permute-done.2.refs_3_.refs_4_ = bf16[512,128]{1,0:T(8,128)(2,1)S(1)} collective-permute-done((bf16[512,128]{1,0:T(8,128)(2,1)S(1)}, bf16[512,128]{1,0:T(8,128)(2,1)S(1)}, u32[]{:S(2)}, u32[]{:S(2)}) %collective-permute-start.2) | collective-permute-done | bytes 131104 | tf_op jit(solution)/shard_map/ppermute | solution.py:382
  12.9 3.0 %collective-permute-start.3 = (bf16[512,128]{1,0:T(8,128)(2,1)S(1)}, bf16[512,128]{1,0:T(8,128)(2,1)S(1)}, u32[]{:S(2)}, u32[]{:S(2)}) collective-permute-start(bf16[512,128]{1,0:T(8,128)(2,1)S(1)} %shard_map.95), channel_id=1, source_target_pairs={{0,4},{1,5},{2,6},{3,7},{4,0},{5,1},{6,2},{7,3},{8,12},{9,13},{10,... | collective-permute-start | bytes 393224 | tf_op jit(solution)/shard_map/ppermute | solution.py:399
  15.9 5.3 %collective-permute-done.3.refs_0_ = bf16[512,128]{1,0:T(8,128)(2,1)S(1)} collective-permute-done((bf16[512,128]{1,0:T(8,128)(2,1)S(1)}, bf16[512,128]{1,0:T(8,128)(2,1)S(1)}, u32[]{:S(2)}, u32[]{:S(2)}) %collective-permute-start.3) | collective-permute-done | bytes 131104 | tf_op jit(solution)/shard_map/ppermute | solution.py:399
  21.5 0.9 %collective-permute-start.5 = (bf16[512,128]{1,0:T(8,128)(2,1)S(1)}, bf16[512,128]{1,0:T(8,128)(2,1)S(1)}, u32[]{:S(2)}, u32[]{:S(2)}) collective-permute-start(bf16[512,128]{1,0:T(8,128)(2,1)S(1)} %shard_map.97.refs_5_), channel_id=1, source_target_pairs={{0,1},{1,0},{2,3},{3,2},{4,5},{5,4},{6,7},{7,6},{8,10},{9,11},{10,... | collective-permute-start | bytes 393224 | tf_op jit(solution)/shard_map/ppermute | solution.py:382
  22.7 2.7 %collective-permute-start.6 = (bf16[512,128]{1,0:T(8,128)(2,1)S(1)}, bf16[512,128]{1,0:T(8,128)(2,1)S(1)}, u32[]{:S(2)}, u32[]{:S(2)}) collective-permute-start(bf16[512,128]{1,0:T(8,128)(2,1)S(1)} %get-tuple-element.48), channel_id=1, source_target_pairs={{0,3},{1,2},{2,1},{3,0},{4,7},{5,6},{6,5},{7,4},{8,11},{9,10},{10,... | collective-permute-start | bytes 393224 | tf_op jit(solution)/shard_map/ppermute | solution.py:382
  25.4 2.7 %collective-permute-done.5.refs_6_.refs_11_ = bf16[512,128]{1,0:T(8,128)(2,1)S(1)} collective-permute-done((bf16[512,128]{1,0:T(8,128)(2,1)S(1)}, bf16[512,128]{1,0:T(8,128)(2,1)S(1)}, u32[]{:S(2)}, u32[]{:S(2)}) %collective-permute-start.5) | collective-permute-done | bytes 131104 | tf_op jit(solution)/shard_map/ppermute | solution.py:382
  28.1 0.4 shard_map.99
  28.6 0.9 %collective-permute-done.6.refs_7_.refs_12_ = bf16[512,128]{1,0:T(8,128)(2,1)S(1)} collective-permute-done((bf16[512,128]{1,0:T(8,128)(2,1)S(1)}, bf16[512,128]{1,0:T(8,128)(2,1)S(1)}, u32[]{:S(2)}, u32[]{:S(2)}) %collective-permute-start.6) | collective-permute-done | bytes 131104 | tf_op jit(solution)/shard_map/ppermute | solution.py:382
  29.5 1.1 %shard_map.100 = (f32[128,512]{1,0:T(8,128)S(1)}, f32[128,128]{1,0:T(8,128)S(1)}, bf16[128,2048]{1,0:T(8,128)(2,1)S(1)}, bf16[544,128]{1,0:T(8,128)(2,1)S(1)}, b...) custom-call(bf16[128,2048]{1,0:T(8,128)(2,1)S(1)} %bitcast.26, ...), custom_call_target="tpu_custom_call" | custom-call | flops 134217728 | bytes 4825088 | tf_op jit(solution)/shard_map/pallas_call | solution.py:352
  30.6 1.5 %collective-permute-start.7 = (bf16[544,128]{1,0:T(8,128)(2,1)S(1)}, bf16[544,128]{1,0:T(8,128)(2,1)S(1)}, u32[]{:S(2)}, u32[]{:S(2)}) collective-permute-start(bf16[544,128]{1,0:T(8,128)(2,1)S(1)} %get-tuple-element.57), channel_id=1, source_target_pairs={{0,1},{1,0},{2,3},{3,2},{4,7},{5,6},{6,5},{7,4},{8,10},{9,11},{10,... | collective-permute-start | bytes 417800 | tf_op jit(solution)/shard_map/ppermute | solution.py:382
  32.1 0.8 %collective-permute-start.8 = (bf16[544,128]{1,0:T(8,128)(2,1)S(1)}, bf16[544,128]{1,0:T(8,128)(2,1)S(1)}, u32[]{:S(2)}, u32[]{:S(2)}) collective-permute-start(bf16[544,128]{1,0:T(8,128)(2,1)S(1)} %get-tuple-element.58), channel_id=1, source_target_pairs={{0,2},{1,3},{2,0},{3,1},{4,5},{5,4},{6,7},{7,6},{8,9},{9,8},{10,11... | collective-permute-start | bytes 417800 | tf_op jit(solution)/shard_map/ppermute | solution.py:382
  32.9 1.2 %collective-permute-start.9 = (bf16[544,128]{1,0:T(8,128)(2,1)S(1)}, bf16[544,128]{1,0:T(8,128)(2,1)S(1)}, u32[]{:S(2)}, u32[]{:S(2)}) collective-permute-start(bf16[544,128]{1,0:T(8,128)(2,1)S(1)} %get-tuple-element.59), channel_id=1, source_target_pairs={{0,3},{1,2},{2,1},{3,0},{4,6},{5,7},{6,4},{7,5},{8,11},{9,10},{10,... | collective-permute-start | bytes 417800 | tf_op jit(solution)/shard_map/ppermute | solution.py:382
  34.1 3.5 %shard_map.101 = (bf16[128,2048]{1,0:T(8,128)(2,1)}, bf16[128,2048]{1,0:T(8,128)(2,1)}, f32[128,2048]{1,0:T(8,128)S(1)}, f32[128,2048]{1,0:T(8,128)S(1)}, f32[8,128]{1,0:T(8,128)S(1)}) custom-call(bf16[128,2048]{1,0:T(8,128)(2,1)S(1)} %bitcast.27, bf16[128,2048]{1,0:T(8,128)(2,1)S(1)} %bitcast.13, bf16[128,2048]{1,0:T(8,128)(2,1)S(1)} %bitcast.20, ...), custom_call_target="tpu_custom_call" | custom-call | flops 335544320 | bytes 7680000 | tf_op jit(solution)/shard_map/pallas_call | solution.py:352
  37.6 1.4 %collective-permute-done.7.refs_1_.refs_2_ = bf16[544,128]{1,0:T(8,128)(2,1)S(1)} collective-permute-done((bf16[544,128]{1,0:T(8,128)(2,1)S(1)}, bf16[544,128]{1,0:T(8,128)(2,1)S(1)}, u32[]{:S(2)}, u32[]{:S(2)}) %collective-permute-start.7) | collective-permute-done | bytes 139296 | tf_op jit(solution)/shard_map/ppermute | solution.py:382
  39.1 1.5 %collective-permute-start.10 = (bf16[544,128]{1,0:T(8,128)(2,1)S(1)}, bf16[544,128]{1,0:T(8,128)(2,1)S(1)}, u32[]{:S(2)}, u32[]{:S(2)}) collective-permute-start(bf16[544,128]{1,0:T(8,128)(2,1)S(1)} %get-tuple-element.61), channel_id=1, source_target_pairs={{0,4},{1,5},{2,6},{3,7},{4,0},{5,1},{6,2},{7,3},{8,12},{9,13},{10,... | collective-permute-start | bytes 417800 | tf_op jit(solution)/shard_map/ppermute | solution.py:399
  40.6 2.3 %collective-permute-start.15 = (f32[16,128]{1,0:T(8,128)S(1)}, f32[16,128]{1,0:T(8,128)S(1)}, u32[]{:S(2)}, u32[]{:S(2)}) collective-permute-start(f32[16,128]{1,0:T(8,128)S(1)} %get-tuple-element.62.refs_5_), channel_id=1, source_target_pairs={{0,20},{1,21},{2,22},{3,23},{4,16},{5,17},{6,18},{7,19},{8,28},{9,... | collective-permute-start | bytes 24584 | tf_op jit(solution)/shard_map/ppermute | solution.py:419
  42.9 0.7 %collective-permute-start.14 = (f32[16,128]{1,0:T(8,128)S(1)}, f32[16,128]{1,0:T(8,128)S(1)}, u32[]{:S(2)}, u32[]{:S(2)}) collective-permute-start(f32[16,128]{1,0:T(8,128)S(1)} %get-tuple-element.62.refs_5_), channel_id=1, source_target_pairs={{0,16},{1,17},{2,18},{3,19},{4,20},{5,21},{6,22},{7,23},{8,24},{9,... | collective-permute-start | bytes 24584 | tf_op jit(solution)/shard_map/ppermute | solution.py:419
  43.6 3.1 %collective-permute-done.10.refs_0_ = bf16[544,128]{1,0:T(8,128)(2,1)S(1)} collective-permute-done((bf16[544,128]{1,0:T(8,128)(2,1)S(1)}, bf16[544,128]{1,0:T(8,128)(2,1)S(1)}, u32[]{:S(2)}, u32[]{:S(2)}) %collective-permute-start.10) | collective-permute-done | bytes 139296 | tf_op jit(solution)/shard_map/ppermute | solution.py:399
  46.8 0.3 collective-permute-start.13
  47.3 1.8 %collective-permute-start.12 = (bf16[512,128]{1,0:T(8,128)(2,1)S(1)}, bf16[512,128]{1,0:T(8,128)(2,1)S(1)}, u32[]{:S(2)}, u32[]{:S(2)}) collective-permute-start(bf16[512,128]{1,0:T(8,128)(2,1)S(1)} %shard_map.104.refs_6_), channel_id=1, source_target_pairs={{0,1},{1,0},{2,3},{3,2},{4,5},{5,4},{6,7},{7,6},{8,10},{9,11},{10,... | collective-permute-start | bytes 393224 | tf_op jit(solution)/shard_map/ppermute | solution.py:382
  49.1 0.3 shard_map.105
  49.4 1.5 %collective-permute-start.11 = (bf16[512,128]{1,0:T(8,128)(2,1)S(1)}, bf16[512,128]{1,0:T(8,128)(2,1)S(1)}, u32[]{:S(2)}, u32[]{:S(2)}) collective-permute-start(bf16[512,128]{1,0:T(8,128)(2,1)S(1)} %get-tuple-element.63), channel_id=1, source_target_pairs={{0,2},{1,3},{2,0},{3,1},{4,6},{5,7},{6,4},{7,5},{8,11},{9,10},{10,... | collective-permute-start | bytes 393224 | tf_op jit(solution)/shard_map/ppermute | solution.py:382
  51.0 1.9 %collective-permute-done.13.refs_5_ = bf16[512,128]{1,0:T(8,128)(2,1)S(1)} collective-permute-done((bf16[512,128]{1,0:T(8,128)(2,1)S(1)}, bf16[512,128]{1,0:T(8,128)(2,1)S(1)}, u32[]{:S(2)}, u32[]{:S(2)}) %collective-permute-start.13) | collective-permute-done | bytes 131104 | tf_op jit(solution)/shard_map/ppermute | solution.py:382
  52.9 1.1 %shard_map.106 = (bf16[128,2048]{1,0:T(8,128)(2,1)}, bf16[128,2048]{1,0:T(8,128)(2,1)}) custom-call(bf16[128,2048]{1,0:T(8,128)(2,1)S(1)} %bitcast.14, bf16[128,2048]{1,0:T(8,128)(2,1)S(1)} %bitcast.21, f32[128,2048]{1,0:T(8,128)S(1)} %get-tuple-element.54.refs_2_, f32[128,2048]{1,0:T(8,128)S(1)} %get-tuple-element.55.refs_3_, ...), custom_call_target="tpu_custom_call" | custom-call | flops 67108864 | bytes 4456448 | tf_op jit(solution)/shard_map/pallas_call | solution.py:352
  54.0 1.0 %shard_map.107 = (bf16[128,2048]{1,0:T(8,128)(2,1)}, bf16[128,2048]{1,0:T(8,128)(2,1)}) custom-call(bf16[128,2048]{1,0:T(8,128)(2,1)S(1)} %bitcast.15, bf16[128,2048]{1,0:T(8,128)(2,1)S(1)} %bitcast.22, f32[128,2048]{1,0:T(8,128)S(1)} %get-tuple-element.54.refs_2_, ...), custom_call_target="tpu_custom_call", output_to_operand_aliasing={{0}: (5, {}), {1}: (6, {})} | custom-call | flops 67108864 | bytes 5373952 | tf_op jit(solution)/shard_map/pallas_call | solution.py:352
  55.0 1.0 %shard_map.108 = (bf16[128,2048]{1,0:T(8,128)(2,1)}, bf16[128,2048]{1,0:T(8,128)(2,1)}, f32[16,128]{1,0:T(8,128)}) custom-call(bf16[128,2048]{1,0:T(8,128)(2,1)S(1)} %bitcast.16, bf16[128,2048]{1,0:T(8,128)(2,1)S(1)} %bitcast.23, f32[128,2048]{1,0:T(8,128)S(1)} %get-tuple-element.54.refs_2_, ...), custom_call_target="tpu_custom_call", output_to_operand_aliasing={{0}: (5, {}), {1}: (6, {})} | custom-call | flops 67108864 | bytes 5398528 | tf_op jit(solution)/shard_map/pallas_call | solution.py:352
  (30 shorter events, 1.3 us)
Async XLA Ops:
  0.6 4.3 %copy-start = (bf16[1,128,2048]{2,1,0:T(8,128)(2,1)S(1)}, bf16[1,128,2048]{2,1,0:T(8,128)(2,1)}, u32[]{:S(2)}) copy-start(bf16[1,128,2048]{2,1,0:T(8,128)(2,1)} %param.6) | copy-start | bytes 1572868
  0.6 4.3 %copy-start.1 = (bf16[1,128,2048]{2,1,0:T(8,128)(2,1)S(1)}, bf16[1,128,2048]{2,1,0:T(8,128)(2,1)}, u32[]{:S(2)}) copy-start(bf16[1,128,2048]{2,1,0:T(8,128)(2,1)} %param.7) | copy-start | bytes 1572868
  2.0 5.1 %copy-start.2 = (bf16[1,128,2048]{2,1,0:T(8,128)(2,1)S(1)}, bf16[1,128,2048]{2,1,0:T(8,128)(2,1)}, u32[]{:S(2)}) copy-start(bf16[1,128,2048]{2,1,0:T(8,128)(2,1)} %param.5) | copy-start | bytes 1572868
  2.0 7.7 %collective-permute-start = (bf16[512,128]{1,0:T(8,128)(2,1)S(1)}, bf16[512,128]{1,0:T(8,128)(2,1)S(1)}, u32[]{:S(2)}, u32[]{:S(2)}) collective-permute-start(bf16[512,128]{1,0:T(8,128)(2,1)S(1)} %shard_map.93.token_ref), channel_id=1, source_target_pairs={{0,1},{1,0},{2,3},{3,2},{4,5},{5,4},{6,7},{7,6},{8,10},{9,11},{10,... | collective-permute-start | bytes 393224 | tf_op jit(solution)/shard_map/ppermute | solution.py:382
  5.4 6.3 %collective-permute-start.1 = (bf16[512,128]{1,0:T(8,128)(2,1)S(1)}, bf16[512,128]{1,0:T(8,128)(2,1)S(1)}, u32[]{:S(2)}, u32[]{:S(2)}) collective-permute-start(bf16[512,128]{1,0:T(8,128)(2,1)S(1)} %get-tuple-element.42), channel_id=1, source_target_pairs={{0,2},{1,3},{2,0},{3,1},{4,6},{5,7},{6,4},{7,5},{8,9},{9,8},{10,11... | collective-permute-start | bytes 393224 | tf_op jit(solution)/shard_map/ppermute | solution.py:382
  7.0 5.9 %collective-permute-start.2 = (bf16[512,128]{1,0:T(8,128)(2,1)S(1)}, bf16[512,128]{1,0:T(8,128)(2,1)S(1)}, u32[]{:S(2)}, u32[]{:S(2)}) collective-permute-start(bf16[512,128]{1,0:T(8,128)(2,1)S(1)} %get-tuple-element.43), channel_id=1, source_target_pairs={{0,3},{1,2},{2,1},{3,0},{4,7},{5,6},{6,5},{7,4},{8,11},{9,10},{10,... | collective-permute-start | bytes 393224 | tf_op jit(solution)/shard_map/ppermute | solution.py:382
  12.9 8.3 %collective-permute-start.3 = (bf16[512,128]{1,0:T(8,128)(2,1)S(1)}, bf16[512,128]{1,0:T(8,128)(2,1)S(1)}, u32[]{:S(2)}, u32[]{:S(2)}) collective-permute-start(bf16[512,128]{1,0:T(8,128)(2,1)S(1)} %shard_map.95), channel_id=1, source_target_pairs={{0,4},{1,5},{2,6},{3,7},{4,0},{5,1},{6,2},{7,3},{8,12},{9,13},{10,... | collective-permute-start | bytes 393224 | tf_op jit(solution)/shard_map/ppermute | solution.py:399
  21.5 6.6 %copy-start.3 = (bf16[1,128,2048]{2,1,0:T(8,128)(2,1)S(1)}, bf16[1,128,2048]{2,1,0:T(8,128)(2,1)}, u32[]{:S(2)}) copy-start(bf16[1,128,2048]{2,1,0:T(8,128)(2,1)} %param.9) | copy-start | bytes 1572868
  21.5 6.5 %collective-permute-start.5 = (bf16[512,128]{1,0:T(8,128)(2,1)S(1)}, bf16[512,128]{1,0:T(8,128)(2,1)S(1)}, u32[]{:S(2)}, u32[]{:S(2)}) collective-permute-start(bf16[512,128]{1,0:T(8,128)(2,1)S(1)} %shard_map.97.refs_5_), channel_id=1, source_target_pairs={{0,1},{1,0},{2,3},{3,2},{4,5},{5,4},{6,7},{7,6},{8,10},{9,11},{10,... | collective-permute-start | bytes 393224 | tf_op jit(solution)/shard_map/ppermute | solution.py:382
  22.4 5.7 %collective-permute-start.4 = (bf16[512,128]{1,0:T(8,128)(2,1)S(1)}, bf16[512,128]{1,0:T(8,128)(2,1)S(1)}, u32[]{:S(2)}, u32[]{:S(2)}) collective-permute-start(bf16[512,128]{1,0:T(8,128)(2,1)S(1)} %shard_map.96.refs_5_), channel_id=1, source_target_pairs={{0,2},{1,3},{2,0},{3,1},{4,6},{5,7},{6,4},{7,5},{8,9},{9,8},{10,11... | collective-permute-start | bytes 393224 | tf_op jit(solution)/shard_map/ppermute | solution.py:382
  22.4 5.7 %copy-start.4 = (f32[2048]{0:T(1024)S(1)}, f32[2048]{0:T(1024)}, u32[]{:S(2)}) copy-start(f32[2048]{0:T(1024)} %param.8) | copy-start | bytes 24580
  22.7 6.9 %collective-permute-start.6 = (bf16[512,128]{1,0:T(8,128)(2,1)S(1)}, bf16[512,128]{1,0:T(8,128)(2,1)S(1)}, u32[]{:S(2)}, u32[]{:S(2)}) collective-permute-start(bf16[512,128]{1,0:T(8,128)(2,1)S(1)} %get-tuple-element.48), channel_id=1, source_target_pairs={{0,3},{1,2},{2,1},{3,0},{4,7},{5,6},{6,5},{7,4},{8,11},{9,10},{10,... | collective-permute-start | bytes 393224 | tf_op jit(solution)/shard_map/ppermute | solution.py:382
  30.6 8.5 %collective-permute-start.7 = (bf16[544,128]{1,0:T(8,128)(2,1)S(1)}, bf16[544,128]{1,0:T(8,128)(2,1)S(1)}, u32[]{:S(2)}, u32[]{:S(2)}) collective-permute-start(bf16[544,128]{1,0:T(8,128)(2,1)S(1)} %get-tuple-element.57), channel_id=1, source_target_pairs={{0,1},{1,0},{2,3},{3,2},{4,7},{5,6},{6,5},{7,4},{8,10},{9,11},{10,... | collective-permute-start | bytes 417800 | tf_op jit(solution)/shard_map/ppermute | solution.py:382
  32.1 6.9 %collective-permute-start.8 = (bf16[544,128]{1,0:T(8,128)(2,1)S(1)}, bf16[544,128]{1,0:T(8,128)(2,1)S(1)}, u32[]{:S(2)}, u32[]{:S(2)}) collective-permute-start(bf16[544,128]{1,0:T(8,128)(2,1)S(1)} %get-tuple-element.58), channel_id=1, source_target_pairs={{0,2},{1,3},{2,0},{3,1},{4,5},{5,4},{6,7},{7,6},{8,9},{9,8},{10,11... | collective-permute-start | bytes 417800 | tf_op jit(solution)/shard_map/ppermute | solution.py:382
  32.9 6.1 %collective-permute-start.9 = (bf16[544,128]{1,0:T(8,128)(2,1)S(1)}, bf16[544,128]{1,0:T(8,128)(2,1)S(1)}, u32[]{:S(2)}, u32[]{:S(2)}) collective-permute-start(bf16[544,128]{1,0:T(8,128)(2,1)S(1)} %get-tuple-element.59), channel_id=1, source_target_pairs={{0,3},{1,2},{2,1},{3,0},{4,6},{5,7},{6,4},{7,5},{8,11},{9,10},{10,... | collective-permute-start | bytes 417800 | tf_op jit(solution)/shard_map/ppermute | solution.py:382
  39.1 7.5 %collective-permute-start.10 = (bf16[544,128]{1,0:T(8,128)(2,1)S(1)}, bf16[544,128]{1,0:T(8,128)(2,1)S(1)}, u32[]{:S(2)}, u32[]{:S(2)}) collective-permute-start(bf16[544,128]{1,0:T(8,128)(2,1)S(1)} %get-tuple-element.61), channel_id=1, source_target_pairs={{0,4},{1,5},{2,6},{3,7},{4,0},{5,1},{6,2},{7,3},{8,12},{9,13},{10,... | collective-permute-start | bytes 417800 | tf_op jit(solution)/shard_map/ppermute | solution.py:399
  40.6 10.3 %collective-permute-start.15 = (f32[16,128]{1,0:T(8,128)S(1)}, f32[16,128]{1,0:T(8,128)S(1)}, u32[]{:S(2)}, u32[]{:S(2)}) collective-permute-start(f32[16,128]{1,0:T(8,128)S(1)} %get-tuple-element.62.refs_5_), channel_id=1, source_target_pairs={{0,20},{1,21},{2,22},{3,23},{4,16},{5,17},{6,18},{7,19},{8,28},{9,... | collective-permute-start | bytes 24584 | tf_op jit(solution)/shard_map/ppermute | solution.py:419
  42.9 8.0 %collective-permute-start.14 = (f32[16,128]{1,0:T(8,128)S(1)}, f32[16,128]{1,0:T(8,128)S(1)}, u32[]{:S(2)}, u32[]{:S(2)}) collective-permute-start(f32[16,128]{1,0:T(8,128)S(1)} %get-tuple-element.62.refs_5_), channel_id=1, source_target_pairs={{0,16},{1,17},{2,18},{3,19},{4,20},{5,21},{6,22},{7,23},{8,24},{9,... | collective-permute-start | bytes 24584 | tf_op jit(solution)/shard_map/ppermute | solution.py:419
  46.8 6.0 %collective-permute-start.13 = (bf16[512,128]{1,0:T(8,128)(2,1)S(1)}, bf16[512,128]{1,0:T(8,128)(2,1)S(1)}, u32[]{:S(2)}, u32[]{:S(2)}) collective-permute-start(bf16[512,128]{1,0:T(8,128)(2,1)S(1)} %shard_map.103.refs_5_), channel_id=1, source_target_pairs={{0,3},{1,2},{2,1},{3,0},{4,7},{5,6},{6,5},{7,4},{8,9},{9,8},{10,11... | collective-permute-start | bytes 393224 | tf_op jit(solution)/shard_map/ppermute | solution.py:382
  47.3 6.7 %collective-permute-start.12 = (bf16[512,128]{1,0:T(8,128)(2,1)S(1)}, bf16[512,128]{1,0:T(8,128)(2,1)S(1)}, u32[]{:S(2)}, u32[]{:S(2)}) collective-permute-start(bf16[512,128]{1,0:T(8,128)(2,1)S(1)} %shard_map.104.refs_6_), channel_id=1, source_target_pairs={{0,1},{1,0},{2,3},{3,2},{4,5},{5,4},{6,7},{7,6},{8,10},{9,11},{10,... | collective-permute-start | bytes 393224 | tf_op jit(solution)/shard_map/ppermute | solution.py:382
  49.4 5.6 %collective-permute-start.11 = (bf16[512,128]{1,0:T(8,128)(2,1)S(1)}, bf16[512,128]{1,0:T(8,128)(2,1)S(1)}, u32[]{:S(2)}, u32[]{:S(2)}) collective-permute-start(bf16[512,128]{1,0:T(8,128)(2,1)S(1)} %get-tuple-element.63), channel_id=1, source_target_pairs={{0,2},{1,3},{2,0},{3,1},{4,6},{5,7},{6,4},{7,5},{8,11},{9,10},{10,... | collective-permute-start | bytes 393224 | tf_op jit(solution)/shard_map/ppermute | solution.py:382
  50.9 4.0 %collective-permute-start.16 = (f32[16,128]{1,0:T(8,128)S(1)}, f32[16,128]{1,0:T(8,128)S(1)}, u32[]{:S(2)}, u32[]{:S(2)}) collective-permute-start(f32[16,128]{1,0:T(8,128)S(1)} %add_add_fusion.refs_7_), channel_id=1, source_target_pairs={{0,8},{8,0},{16,24},{24,16},{1,9},{9,1},{17,25},{25,17},{2,10},{10... | collective-permute-start | bytes 24584 | tf_op jit(solution)/shard_map/ppermute | solution.py:370

commit v2 on v1

--- a/solution.py
+++ b/solution.py
@@ -36,7 +36,7 @@
     (((0, 2, 1, 3), (0, 1, 2, 3)), ((0, 2, 1, 3), (0, 1, 2, 3))),
 )
 GRAD_ORDERS = (
-    (((0, 1, 2, 3), (0, 2, 1, 3)), ((0, 3, 1, 2), (0, 3, 1, 2))),
+    (((0, 3, 1, 2), (0, 3, 1, 2)), ((0, 3, 1, 2), (0, 3, 1, 2))),
     (((0, 3, 1, 2), (0, 1, 2, 3)), ((0, 3, 1, 2), (0, 1, 2, 3))),
 )
 NORM_ORDERS = (STATE_ORDERS[1], GRAD_ORDERS[0])
@@ -429,7 +429,7 @@
         (carry,) = call(kernel, [piece], [carry, moved], 0)
         distance *= 2
     pieces, after = {}, []
-    for slots in ((1,), (2,), (3, 0)):
+    for slots in ((1,), (2,), (3,), (0,)):
         adding = riding if 0 in slots else 0
         inputs = [carry] + received + gains[:adding] + after
         sums = call(
@@ -520,7 +520,7 @@
     gains = [gain_grad, swap(gain_grad, "dp", 1)]
     inputs = [k, v, key_part, value_part]
     outs = []
-    for slots in ((0, 1), (2,), (3,)):
+    for slots in ((0, 1), (2, 3)):
         last = group - 1 in slots
         at = len(inputs) + len(slots)
         results = call(

time: 56.1 us -> 57.3 us (1.021)
  the two profiles are of different devices: /device:TPU:0 before, /device:TPU:4 now
where the time goes in v2:
time: 57.3 us; the launch traced here: 57.2 us
  waiting for transfers between devices  22 us (38%)
  starting transfers between devices  21.6 us (38%)
  Pallas kernels  12.7 us (22%)
  between operations  0.8 us (1%)
    ppermute x12, starting transfers between devices, own_and_swapped(): results.append(lax.ppermute(pieces[slot], ('dp', 'seq'), pairs))  14.5 us
    pallas_call x18, Pallas kernels, call(): pl.pallas_call(kernel, out_shape=tuple(outs), in_specs=[ins.get(i, VMEM)...  12.7 us
    ppermute x12, waiting for transfers between devices, own_and_swapped(): results.append(lax.ppermute(pieces[slot], ('dp', 'seq'), pairs))  11.8 us
    ppermute x2, waiting for transfers between devices, shifted(): return lax.ppermute(array, 'seq', pairs)  10.2 us
    ppermute x2, starting transfers between devices, shifted(): return lax.ppermute(array, 'seq', pairs)  4 us
    ppermute x2, starting transfers between devices, exclusive_scan(): gains.append(lax.ppermute(gains[0], ('dp', 'seq'), pairs))  3.11 us
  transfers between devices with their start and end apart: 17, of which 11 were waited for; matrix products, arithmetic and copies ran while one was open for 0% of the time, Pallas kernels for 15%

profile of v2, /device:TPU:4, one launch (start us, length us, event | category | flops | bytes accessed | tf_op | source)
XLA Modules:
  0.0 57.2 jit_solution(5778704297182448521)
XLA Ops:
  0.7 1.3 %shard_map.93.token_ref = bf16[512,128]{1,0:T(8,128)(2,1)S(1)} custom-call(bf16[128,2048]{1,0:T(8,128)(2,1)} %bitcast.10, bf16[128,2048]{1,0:T(8,128)(2,1)} %bitcast.16), custom_call_target="tpu_custom_call" | custom-call | flops 67108864 | bytes 1179648 | tf_op jit(solution)/shard_map/pallas_call | solution.py:352
  2.0 1.6 %collective-permute-start = (bf16[512,128]{1,0:T(8,128)(2,1)S(1)}, bf16[512,128]{1,0:T(8,128)(2,1)S(1)}, u32[]{:S(2)}, u32[]{:S(2)}) collective-permute-start(bf16[512,128]{1,0:T(8,128)(2,1)S(1)} %shard_map.93.token_ref), channel_id=1, source_target_pairs={{0,1},{1,0},{2,3},{3,2},{4,5},{5,4},{6,7},{7,6},{8,10},{9,11},{10,... | collective-permute-start | bytes 393224 | tf_op jit(solution)/shard_map/ppermute | solution.py:382
  3.5 0.4 shard_map.94
  3.9 1.6 %collective-permute-start.1 = (bf16[512,128]{1,0:T(8,128)(2,1)S(1)}, bf16[512,128]{1,0:T(8,128)(2,1)S(1)}, u32[]{:S(2)}, u32[]{:S(2)}) collective-permute-start(bf16[512,128]{1,0:T(8,128)(2,1)S(1)} %get-tuple-element.37), channel_id=1, source_target_pairs={{0,2},{1,3},{2,0},{3,1},{4,6},{5,7},{6,4},{7,5},{8,9},{9,8},{10,11... | collective-permute-start | bytes 393224 | tf_op jit(solution)/shard_map/ppermute | solution.py:382
  5.6 0.4 collective-permute-start.2
  6.0 2.6 %shard_map.92 = (bf16[2048,128]{1,0:T(8,128)(2,1)S(1)}, f32[128,2048]{1,0:T(8,128)S(1)}) custom-call(bf16[128,2048]{1,0:T(8,128)(2,1)S(1)} %bitcast.22, bf16[128,2048]{1,0:T(8,128)(2,1)S(1)} %bitcast.12, bf16[128,2048]{1,0:T(8,128)(2,1)S(1)} %bitcast.18), custom_call_target="tpu_custom_call" | custom-call | flops 134217728 | bytes 3145728 | tf_op jit(solution)/shard_map/pallas_call | solution.py:352
  8.6 1.6 %collective-permute-done.1.refs_2_.refs_3_ = bf16[512,128]{1,0:T(8,128)(2,1)S(1)} collective-permute-done((bf16[512,128]{1,0:T(8,128)(2,1)S(1)}, bf16[512,128]{1,0:T(8,128)(2,1)S(1)}, u32[]{:S(2)}, u32[]{:S(2)}) %collective-permute-start.1) | collective-permute-done | bytes 131104 | tf_op jit(solution)/shard_map/ppermute | solution.py:382
  10.2 1.5 %collective-permute-done.2.refs_3_.refs_4_ = bf16[512,128]{1,0:T(8,128)(2,1)S(1)} collective-permute-done((bf16[512,128]{1,0:T(8,128)(2,1)S(1)}, bf16[512,128]{1,0:T(8,128)(2,1)S(1)}, u32[]{:S(2)}, u32[]{:S(2)}) %collective-permute-start.2) | collective-permute-done | bytes 131104 | tf_op jit(solution)/shard_map/ppermute | solution.py:382
  11.8 2.7 %collective-permute-start.3 = (bf16[512,128]{1,0:T(8,128)(2,1)S(1)}, bf16[512,128]{1,0:T(8,128)(2,1)S(1)}, u32[]{:S(2)}, u32[]{:S(2)}) collective-permute-start(bf16[512,128]{1,0:T(8,128)(2,1)S(1)} %shard_map.95), channel_id=1, source_target_pairs={{0,4},{1,5},{2,6},{3,7},{4,0},{5,1},{6,2},{7,3},{8,12},{9,13},{10,... | collective-permute-start | bytes 393224 | tf_op jit(solution)/shard_map/ppermute | solution.py:399
  14.5 5.3 %collective-permute-done.3.refs_0_ = bf16[512,128]{1,0:T(8,128)(2,1)S(1)} collective-permute-done((bf16[512,128]{1,0:T(8,128)(2,1)S(1)}, bf16[512,128]{1,0:T(8,128)(2,1)S(1)}, u32[]{:S(2)}, u32[]{:S(2)}) %collective-permute-start.3) | collective-permute-done | bytes 131104 | tf_op jit(solution)/shard_map/ppermute | solution.py:399
  20.1 0.9 %collective-permute-start.5 = (bf16[512,128]{1,0:T(8,128)(2,1)S(1)}, bf16[512,128]{1,0:T(8,128)(2,1)S(1)}, u32[]{:S(2)}, u32[]{:S(2)}) collective-permute-start(bf16[512,128]{1,0:T(8,128)(2,1)S(1)} %shard_map.97.refs_5_), channel_id=1, source_target_pairs={{0,1},{1,0},{2,3},{3,2},{4,5},{5,4},{6,7},{7,6},{8,10},{9,11},{10,... | collective-permute-start | bytes 393224 | tf_op jit(solution)/shard_map/ppermute | solution.py:382
  21.1 2.7 %collective-permute-start.6 = (bf16[512,128]{1,0:T(8,128)(2,1)S(1)}, bf16[512,128]{1,0:T(8,128)(2,1)S(1)}, u32[]{:S(2)}, u32[]{:S(2)}) collective-permute-start(bf16[512,128]{1,0:T(8,128)(2,1)S(1)} %shard_map.98.refs_5_), channel_id=1, source_target_pairs={{0,3},{1,2},{2,1},{3,0},{4,7},{5,6},{6,5},{7,4},{8,11},{9,10},{10,... | collective-permute-start | bytes 393224 | tf_op jit(solution)/shard_map/ppermute | solution.py:382
  24.0 2.3 %collective-permute-done.5.refs_6_.refs_11_ = bf16[512,128]{1,0:T(8,128)(2,1)S(1)} collective-permute-done((bf16[512,128]{1,0:T(8,128)(2,1)S(1)}, bf16[512,128]{1,0:T(8,128)(2,1)S(1)}, u32[]{:S(2)}, u32[]{:S(2)}) %collective-permute-start.5) | collective-permute-done | bytes 131104 | tf_op jit(solution)/shard_map/ppermute | solution.py:382
  26.3 0.4 shard_map.100
  26.8 1.2 %collective-permute-done.6.refs_7_.refs_12_ = bf16[512,128]{1,0:T(8,128)(2,1)S(1)} collective-permute-done((bf16[512,128]{1,0:T(8,128)(2,1)S(1)}, bf16[512,128]{1,0:T(8,128)(2,1)S(1)}, u32[]{:S(2)}, u32[]{:S(2)}) %collective-permute-start.6) | collective-permute-done | bytes 131104 | tf_op jit(solution)/shard_map/ppermute | solution.py:382
  28.0 1.0 %shard_map.101 = (f32[128,512]{1,0:T(8,128)S(1)}, f32[128,128]{1,0:T(8,128)S(1)}, bf16[128,2048]{1,0:T(8,128)(2,1)S(1)}, bf16[544,128]{1,0:T(8,128)(2,1)S(1)}, b...) custom-call(bf16[128,2048]{1,0:T(8,128)(2,1)S(1)} %bitcast.24, ...), custom_call_target="tpu_custom_call" | custom-call | flops 134217728 | bytes 4825088 | tf_op jit(solution)/shard_map/pallas_call | solution.py:352
  29.0 1.8 %collective-permute-start.7 = (bf16[544,128]{1,0:T(8,128)(2,1)S(1)}, bf16[544,128]{1,0:T(8,128)(2,1)S(1)}, u32[]{:S(2)}, u32[]{:S(2)}) collective-permute-start(bf16[544,128]{1,0:T(8,128)(2,1)S(1)} %get-tuple-element.50), channel_id=1, source_target_pairs={{0,3},{1,2},{2,1},{3,0},{4,7},{5,6},{6,5},{7,4},{8,11},{9,10},{10,... | collective-permute-start | bytes 417800 | tf_op jit(solution)/shard_map/ppermute | solution.py:382
  30.7 0.9 %collective-permute-start.8 = (bf16[544,128]{1,0:T(8,128)(2,1)S(1)}, bf16[544,128]{1,0:T(8,128)(2,1)S(1)}, u32[]{:S(2)}, u32[]{:S(2)}) collective-permute-start(bf16[544,128]{1,0:T(8,128)(2,1)S(1)} %get-tuple-element.51), channel_id=1, source_target_pairs={{0,1},{1,0},{2,3},{3,2},{4,5},{5,4},{6,7},{7,6},{8,9},{9,8},{10,11... | collective-permute-start | bytes 417800 | tf_op jit(solution)/shard_map/ppermute | solution.py:382
  31.6 0.9 %collective-permute-start.9 = (bf16[544,128]{1,0:T(8,128)(2,1)S(1)}, bf16[544,128]{1,0:T(8,128)(2,1)S(1)}, u32[]{:S(2)}, u32[]{:S(2)}) collective-permute-start(bf16[544,128]{1,0:T(8,128)(2,1)S(1)} %get-tuple-element.52), channel_id=1, source_target_pairs={{0,2},{1,3},{2,0},{3,1},{4,6},{5,7},{6,4},{7,5},{8,10},{9,11},{10,... | collective-permute-start | bytes 417800 | tf_op jit(solution)/shard_map/ppermute | solution.py:382
  32.5 3.5 %shard_map.102 = (bf16[128,2048]{1,0:T(8,128)(2,1)}, bf16[128,2048]{1,0:T(8,128)(2,1)}, f32[128,2048]{1,0:T(8,128)S(1)}, f32[128,2048]{1,0:T(8,128)S(1)}, f32[8,128]{1,0:T(8,128)S(1)}) custom-call(bf16[128,2048]{1,0:T(8,128)(2,1)S(1)} %bitcast.25, bf16[128,2048]{1,0:T(8,128)(2,1)S(1)} %bitcast.13, bf16[128,2048]{1,0:T(8,128)(2,1)S(1)} %bitcast.19, ...), custom_call_target="tpu_custom_call" | custom-call | flops 335544320 | bytes 7680000 | tf_op jit(solution)/shard_map/pallas_call | solution.py:352
  36.1 1.1 %collective-permute-done.8.refs_2_.refs_3_ = bf16[544,128]{1,0:T(8,128)(2,1)S(1)} collective-permute-done((bf16[544,128]{1,0:T(8,128)(2,1)S(1)}, bf16[544,128]{1,0:T(8,128)(2,1)S(1)}, u32[]{:S(2)}, u32[]{:S(2)}) %collective-permute-start.8) | collective-permute-done | bytes 139296 | tf_op jit(solution)/shard_map/ppermute | solution.py:382
  37.2 0.5 collective-permute-done.9.refs_3_.refs_4_
  37.8 1.3 %collective-permute-start.10 = (bf16[544,128]{1,0:T(8,128)(2,1)S(1)}, bf16[544,128]{1,0:T(8,128)(2,1)S(1)}, u32[]{:S(2)}, u32[]{:S(2)}) collective-permute-start(bf16[544,128]{1,0:T(8,128)(2,1)S(1)} %get-tuple-element.54), channel_id=1, source_target_pairs={{0,4},{1,5},{2,6},{3,7},{4,0},{5,1},{6,2},{7,3},{8,12},{9,13},{10,... | collective-permute-start | bytes 417800 | tf_op jit(solution)/shard_map/ppermute | solution.py:399
  39.2 1.0 %collective-permute-start.15 = (f32[16,128]{1,0:T(8,128)S(1)}, f32[16,128]{1,0:T(8,128)S(1)}, u32[]{:S(2)}, u32[]{:S(2)}) collective-permute-start(f32[16,128]{1,0:T(8,128)S(1)} %get-tuple-element.55.refs_5_), channel_id=1, source_target_pairs={{0,20},{1,21},{2,22},{3,23},{4,16},{5,17},{6,18},{7,19},{8,28},{9,... | collective-permute-start | bytes 24584 | tf_op jit(solution)/shard_map/ppermute | solution.py:419
  40.1 2.1 %collective-permute-start.14 = (f32[16,128]{1,0:T(8,128)S(1)}, f32[16,128]{1,0:T(8,128)S(1)}, u32[]{:S(2)}, u32[]{:S(2)}) collective-permute-start(f32[16,128]{1,0:T(8,128)S(1)} %get-tuple-element.55.refs_5_), channel_id=1, source_target_pairs={{0,16},{1,17},{2,18},{3,19},{4,20},{5,21},{6,22},{7,23},{8,24},{9,... | collective-permute-start | bytes 24584 | tf_op jit(solution)/shard_map/ppermute | solution.py:419
  42.3 4.9 %collective-permute-done.10.refs_0_ = bf16[544,128]{1,0:T(8,128)(2,1)S(1)} collective-permute-done((bf16[544,128]{1,0:T(8,128)(2,1)S(1)}, bf16[544,128]{1,0:T(8,128)(2,1)S(1)}, u32[]{:S(2)}, u32[]{:S(2)}) %collective-permute-start.10) | collective-permute-done | bytes 139296 | tf_op jit(solution)/shard_map/ppermute | solution.py:399
  47.4 0.1 shard_map.105.refs_5_
  47.5 1.6 %collective-permute-start.11 = (bf16[512,128]{1,0:T(8,128)(2,1)S(1)}, bf16[512,128]{1,0:T(8,128)(2,1)S(1)}, u32[]{:S(2)}, u32[]{:S(2)}) collective-permute-start(bf16[512,128]{1,0:T(8,128)(2,1)S(1)} %shard_map.105.refs_5_), channel_id=1, source_target_pairs={{0,1},{1,0},{2,3},{3,2},{4,5},{5,4},{6,7},{7,6},{8,10},{9,11},{10,... | collective-permute-start | bytes 393224 | tf_op jit(solution)/shard_map/ppermute | solution.py:382
  49.3 2.0 %collective-permute-start.12 = (bf16[512,128]{1,0:T(8,128)(2,1)S(1)}, bf16[512,128]{1,0:T(8,128)(2,1)S(1)}, u32[]{:S(2)}, u32[]{:S(2)}) collective-permute-start(bf16[512,128]{1,0:T(8,128)(2,1)S(1)} %shard_map.106.refs_6_), channel_id=1, source_target_pairs={{0,2},{1,3},{2,0},{3,1},{4,6},{5,7},{6,4},{7,5},{8,11},{9,10},{10,... | collective-permute-start | bytes 393224 | tf_op jit(solution)/shard_map/ppermute | solution.py:382
  51.5 3.2 %collective-permute-done.13.refs_5_ = bf16[512,128]{1,0:T(8,128)(2,1)S(1)} collective-permute-done((bf16[512,128]{1,0:T(8,128)(2,1)S(1)}, bf16[512,128]{1,0:T(8,128)(2,1)S(1)}, u32[]{:S(2)}, u32[]{:S(2)}) %collective-permute-start.13) | collective-permute-done | bytes 131104 | tf_op jit(solution)/shard_map/ppermute | solution.py:382
  54.8 1.1 %shard_map.108 = (bf16[128,2048]{1,0:T(8,128)(2,1)}, bf16[128,2048]{1,0:T(8,128)(2,1)}) custom-call(bf16[128,2048]{1,0:T(8,128)(2,1)S(1)} %bitcast.14, bf16[128,2048]{1,0:T(8,128)(2,1)S(1)} %bitcast.20, f32[128,2048]{1,0:T(8,128)S(1)} %get-tuple-element.47.refs_2_, f32[128,2048]{1,0:T(8,128)S(1)} %get-tuple-element.48.refs_3_, ...), custom_call_target="tpu_custom_call" | custom-call | flops 67108864 | bytes 4456448 | tf_op jit(solution)/shard_map/pallas_call | solution.py:352
  56.0 1.1 %shard_map.109 = (bf16[128,2048]{1,0:T(8,128)(2,1)}, bf16[128,2048]{1,0:T(8,128)(2,1)}, f32[16,128]{1,0:T(8,128)}) custom-call(bf16[128,2048]{1,0:T(8,128)(2,1)S(1)} %bitcast.15, bf16[128,2048]{1,0:T(8,128)(2,1)S(1)} %bitcast.21, f32[128,2048]{1,0:T(8,128)S(1)} %get-tuple-element.47.refs_2_, ...), custom_call_target="tpu_custom_call", output_to_operand_aliasing={{0}: (6, {}), {1}: (7, {})} | custom-call | flops 67108864 | bytes 5529600 | tf_op jit(solution)/shard_map/pallas_call | solution.py:352
  (31 shorter events, 1.6 us)
Async XLA Ops:
  0.6 2.9 %copy-start = (bf16[1,128,2048]{2,1,0:T(8,128)(2,1)S(1)}, bf16[1,128,2048]{2,1,0:T(8,128)(2,1)}, u32[]{:S(2)}) copy-start(bf16[1,128,2048]{2,1,0:T(8,128)(2,1)} %param.6) | copy-start | bytes 1572868
  0.6 2.9 %copy-start.1 = (bf16[1,128,2048]{2,1,0:T(8,128)(2,1)S(1)}, bf16[1,128,2048]{2,1,0:T(8,128)(2,1)}, u32[]{:S(2)}) copy-start(bf16[1,128,2048]{2,1,0:T(8,128)(2,1)} %param.7) | copy-start | bytes 1572868
  2.0 4.0 %copy-start.2 = (bf16[1,128,2048]{2,1,0:T(8,128)(2,1)S(1)}, bf16[1,128,2048]{2,1,0:T(8,128)(2,1)}, u32[]{:S(2)}) copy-start(bf16[1,128,2048]{2,1,0:T(8,128)(2,1)} %param.5) | copy-start | bytes 1572868
  2.0 6.6 %collective-permute-start = (bf16[512,128]{1,0:T(8,128)(2,1)S(1)}, bf16[512,128]{1,0:T(8,128)(2,1)S(1)}, u32[]{:S(2)}, u32[]{:S(2)}) collective-permute-start(bf16[512,128]{1,0:T(8,128)(2,1)S(1)} %shard_map.93.token_ref), channel_id=1, source_target_pairs={{0,1},{1,0},{2,3},{3,2},{4,5},{5,4},{6,7},{7,6},{8,10},{9,11},{10,... | collective-permute-start | bytes 393224 | tf_op jit(solution)/shard_map/ppermute | solution.py:382
  3.9 6.3 %collective-permute-start.1 = (bf16[512,128]{1,0:T(8,128)(2,1)S(1)}, bf16[512,128]{1,0:T(8,128)(2,1)S(1)}, u32[]{:S(2)}, u32[]{:S(2)}) collective-permute-start(bf16[512,128]{1,0:T(8,128)(2,1)S(1)} %get-tuple-element.37), channel_id=1, source_target_pairs={{0,2},{1,3},{2,0},{3,1},{4,6},{5,7},{6,4},{7,5},{8,9},{9,8},{10,11... | collective-permute-start | bytes 393224 | tf_op jit(solution)/shard_map/ppermute | solution.py:382
  5.6 6.2 %collective-permute-start.2 = (bf16[512,128]{1,0:T(8,128)(2,1)S(1)}, bf16[512,128]{1,0:T(8,128)(2,1)S(1)}, u32[]{:S(2)}, u32[]{:S(2)}) collective-permute-start(bf16[512,128]{1,0:T(8,128)(2,1)S(1)} %get-tuple-element.38), channel_id=1, source_target_pairs={{0,3},{1,2},{2,1},{3,0},{4,7},{5,6},{6,5},{7,4},{8,11},{9,10},{10,... | collective-permute-start | bytes 393224 | tf_op jit(solution)/shard_map/ppermute | solution.py:382
  11.8 8.0 %collective-permute-start.3 = (bf16[512,128]{1,0:T(8,128)(2,1)S(1)}, bf16[512,128]{1,0:T(8,128)(2,1)S(1)}, u32[]{:S(2)}, u32[]{:S(2)}) collective-permute-start(bf16[512,128]{1,0:T(8,128)(2,1)S(1)} %shard_map.95), channel_id=1, source_target_pairs={{0,4},{1,5},{2,6},{3,7},{4,0},{5,1},{6,2},{7,3},{8,12},{9,13},{10,... | collective-permute-start | bytes 393224 | tf_op jit(solution)/shard_map/ppermute | solution.py:399
  20.1 6.2 %collective-permute-start.5 = (bf16[512,128]{1,0:T(8,128)(2,1)S(1)}, bf16[512,128]{1,0:T(8,128)(2,1)S(1)}, u32[]{:S(2)}, u32[]{:S(2)}) collective-permute-start(bf16[512,128]{1,0:T(8,128)(2,1)S(1)} %shard_map.97.refs_5_), channel_id=1, source_target_pairs={{0,1},{1,0},{2,3},{3,2},{4,5},{5,4},{6,7},{7,6},{8,10},{9,11},{10,... | collective-permute-start | bytes 393224 | tf_op jit(solution)/shard_map/ppermute | solution.py:382
  20.9 5.4 %collective-permute-start.4 = (bf16[512,128]{1,0:T(8,128)(2,1)S(1)}, bf16[512,128]{1,0:T(8,128)(2,1)S(1)}, u32[]{:S(2)}, u32[]{:S(2)}) collective-permute-start(bf16[512,128]{1,0:T(8,128)(2,1)S(1)} %shard_map.96.refs_5_), channel_id=1, source_target_pairs={{0,2},{1,3},{2,0},{3,1},{4,6},{5,7},{6,4},{7,5},{8,9},{9,8},{10,11... | collective-permute-start | bytes 393224 | tf_op jit(solution)/shard_map/ppermute | solution.py:382
  21.1 5.2 %copy-start.3 = (bf16[1,128,2048]{2,1,0:T(8,128)(2,1)S(1)}, bf16[1,128,2048]{2,1,0:T(8,128)(2,1)}, u32[]{:S(2)}) copy-start(bf16[1,128,2048]{2,1,0:T(8,128)(2,1)} %param.9) | copy-start | bytes 1572868
  21.1 6.9 %collective-permute-start.6 = (bf16[512,128]{1,0:T(8,128)(2,1)S(1)}, bf16[512,128]{1,0:T(8,128)(2,1)S(1)}, u32[]{:S(2)}, u32[]{:S(2)}) collective-permute-start(bf16[512,128]{1,0:T(8,128)(2,1)S(1)} %shard_map.98.refs_5_), channel_id=1, source_target_pairs={{0,3},{1,2},{2,1},{3,0},{4,7},{5,6},{6,5},{7,4},{8,11},{9,10},{10,... | collective-permute-start | bytes 393224 | tf_op jit(solution)/shard_map/ppermute | solution.py:382
  23.8 2.5 %copy-start.4 = (f32[2048]{0:T(1024)S(1)}, f32[2048]{0:T(1024)}, u32[]{:S(2)}) copy-start(f32[2048]{0:T(1024)} %param.8) | copy-start | bytes 24580
  29.0 7.2 %collective-permute-start.7 = (bf16[544,128]{1,0:T(8,128)(2,1)S(1)}, bf16[544,128]{1,0:T(8,128)(2,1)S(1)}, u32[]{:S(2)}, u32[]{:S(2)}) collective-permute-start(bf16[544,128]{1,0:T(8,128)(2,1)S(1)} %get-tuple-element.50), channel_id=1, source_target_pairs={{0,3},{1,2},{2,1},{3,0},{4,7},{5,6},{6,5},{7,4},{8,11},{9,10},{10,... | collective-permute-start | bytes 417800 | tf_op jit(solution)/shard_map/ppermute | solution.py:382
  30.7 6.5 %collective-permute-start.8 = (bf16[544,128]{1,0:T(8,128)(2,1)S(1)}, bf16[544,128]{1,0:T(8,128)(2,1)S(1)}, u32[]{:S(2)}, u32[]{:S(2)}) collective-permute-start(bf16[544,128]{1,0:T(8,128)(2,1)S(1)} %get-tuple-element.51), channel_id=1, source_target_pairs={{0,1},{1,0},{2,3},{3,2},{4,5},{5,4},{6,7},{7,6},{8,9},{9,8},{10,11... | collective-permute-start | bytes 417800 | tf_op jit(solution)/shard_map/ppermute | solution.py:382
  31.6 6.1 %collective-permute-start.9 = (bf16[544,128]{1,0:T(8,128)(2,1)S(1)}, bf16[544,128]{1,0:T(8,128)(2,1)S(1)}, u32[]{:S(2)}, u32[]{:S(2)}) collective-permute-start(bf16[544,128]{1,0:T(8,128)(2,1)S(1)} %get-tuple-element.52), channel_id=1, source_target_pairs={{0,2},{1,3},{2,0},{3,1},{4,6},{5,7},{6,4},{7,5},{8,10},{9,11},{10,... | collective-permute-start | bytes 417800 | tf_op jit(solution)/shard_map/ppermute | solution.py:382
  37.8 9.3 %collective-permute-start.10 = (bf16[544,128]{1,0:T(8,128)(2,1)S(1)}, bf16[544,128]{1,0:T(8,128)(2,1)S(1)}, u32[]{:S(2)}, u32[]{:S(2)}) collective-permute-start(bf16[544,128]{1,0:T(8,128)(2,1)S(1)} %get-tuple-element.54), channel_id=1, source_target_pairs={{0,4},{1,5},{2,6},{3,7},{4,0},{5,1},{6,2},{7,3},{8,12},{9,13},{10,... | collective-permute-start | bytes 417800 | tf_op jit(solution)/shard_map/ppermute | solution.py:399
  39.2 12.3 %collective-permute-start.15 = (f32[16,128]{1,0:T(8,128)S(1)}, f32[16,128]{1,0:T(8,128)S(1)}, u32[]{:S(2)}, u32[]{:S(2)}) collective-permute-start(f32[16,128]{1,0:T(8,128)S(1)} %get-tuple-element.55.refs_5_), channel_id=1, source_target_pairs={{0,20},{1,21},{2,22},{3,23},{4,16},{5,17},{6,18},{7,19},{8,28},{9,... | collective-permute-start | bytes 24584 | tf_op jit(solution)/shard_map/ppermute | solution.py:419
  40.1 11.3 %collective-permute-start.14 = (f32[16,128]{1,0:T(8,128)S(1)}, f32[16,128]{1,0:T(8,128)S(1)}, u32[]{:S(2)}, u32[]{:S(2)}) collective-permute-start(f32[16,128]{1,0:T(8,128)S(1)} %get-tuple-element.55.refs_5_), channel_id=1, source_target_pairs={{0,16},{1,17},{2,18},{3,19},{4,20},{5,21},{6,22},{7,23},{8,24},{9,... | collective-permute-start | bytes 24584 | tf_op jit(solution)/shard_map/ppermute | solution.py:419
  47.3 7.5 %collective-permute-start.13 = (bf16[512,128]{1,0:T(8,128)(2,1)S(1)}, bf16[512,128]{1,0:T(8,128)(2,1)S(1)}, u32[]{:S(2)}, u32[]{:S(2)}) collective-permute-start(bf16[512,128]{1,0:T(8,128)(2,1)S(1)} %shard_map.104.refs_5_), channel_id=1, source_target_pairs={{0,3},{1,2},{2,1},{3,0},{4,7},{5,6},{6,5},{7,4},{8,9},{9,8},{10,11... | collective-permute-start | bytes 393224 | tf_op jit(solution)/shard_map/ppermute | solution.py:382
  47.5 8.5 %collective-permute-start.11 = (bf16[512,128]{1,0:T(8,128)(2,1)S(1)}, bf16[512,128]{1,0:T(8,128)(2,1)S(1)}, u32[]{:S(2)}, u32[]{:S(2)}) collective-permute-start(bf16[512,128]{1,0:T(8,128)(2,1)S(1)} %shard_map.105.refs_5_), channel_id=1, source_target_pairs={{0,1},{1,0},{2,3},{3,2},{4,5},{5,4},{6,7},{7,6},{8,10},{9,11},{10,... | collective-permute-start | bytes 393224 | tf_op jit(solution)/shard_map/ppermute | solution.py:382
  49.3 6.7 %collective-permute-start.12 = (bf16[512,128]{1,0:T(8,128)(2,1)S(1)}, bf16[512,128]{1,0:T(8,128)(2,1)S(1)}, u32[]{:S(2)}, u32[]{:S(2)}) collective-permute-start(bf16[512,128]{1,0:T(8,128)(2,1)S(1)} %shard_map.106.refs_6_), channel_id=1, source_target_pairs={{0,2},{1,3},{2,0},{3,1},{4,6},{5,7},{6,4},{7,5},{8,11},{9,10},{10,... | collective-permute-start | bytes 393224 | tf_op jit(solution)/shard_map/ppermute | solution.py:382
  51.5 4.4 %collective-permute-start.16 = (f32[16,128]{1,0:T(8,128)S(1)}, f32[16,128]{1,0:T(8,128)S(1)}, u32[]{:S(2)}, u32[]{:S(2)}) collective-permute-start(f32[16,128]{1,0:T(8,128)S(1)} %add_add_fusion.refs_8_), channel_id=1, source_target_pairs={{0,8},{8,0},{16,24},{24,16},{1,9},{9,1},{17,25},{25,17},{2,10},{10... | collective-permute-start | bytes 24584 | tf_op jit(solution)/shard_map/ppermute | solution.py:370

commit v3 on v0

--- a/solution.py
+++ b/solution.py
@@ -500,7 +500,7 @@
     gains = [gain_grad, swap(gain_grad, "dp", 1)]
     inputs = [k, v, key_part, value_part]
     outs = []
-    for slots in ((0, 1), (2,), (3,)):
+    for slots in ((0, 1), (2, 3)):
         last = group - 1 in slots
         at = len(inputs) + len(slots)
         results = call(

time: 55.9 us -> 55.1 us (0.986)
  Pallas kernels: 13.5 us -> 12.6 us
    pallas_call x17 -> x16, Pallas kernels: 13.5 us -> 12.6 us  [call(): pl.pallas_call(kernel, out_shape=tuple(outs), in_specs=[ins.get(i, VMEM)...]
  transfers between devices with their start and end apart: 17 -> 17, of which waited for: 11 -> 11; matrix products, arithmetic and copies ran while one was open for 0% -> 0% of each run, Pallas kernels for 17% -> 16%
where the time goes in v3:
time: 55.1 us; the launch traced here: 54.9 us
  starting transfers between devices  23 us (42%)
  waiting for transfers between devices  18.5 us (34%)
  Pallas kernels  12.6 us (23%)
  between operations  0.77 us (1%)
    ppermute x12, starting transfers between devices, own_and_swapped(): results.append(lax.ppermute(pieces[slot], ('dp', 'seq'), pairs))  15.5 us
    pallas_call x16, Pallas kernels, call(): pl.pallas_call(kernel, out_shape=tuple(outs), in_specs=[ins.get(i, VMEM)...  12.6 us
    ppermute x12, waiting for transfers between devices, own_and_swapped(): results.append(lax.ppermute(pieces[slot], ('dp', 'seq'), pairs))  10 us
    ppermute x2, waiting for transfers between devices, shifted(): return lax.ppermute(array, 'seq', pairs)  8.4 us
    ppermute x2, starting transfers between devices, shifted(): return lax.ppermute(array, 'seq', pairs)  4.74 us
    ppermute x2, starting transfers between devices, exclusive_scan(): gains.append(lax.ppermute(gains[0], ('dp', 'seq'), pairs))  2.66 us
  transfers between devices with their start and end apart: 17, of which 11 were waited for; matrix products, arithmetic and copies ran while one was open for 0% of the time, Pallas kernels for 16%

profile of v3, /device:TPU:0, one launch (start us, length us, event | category | flops | bytes accessed | tf_op | source)
XLA Modules:
  0.0 54.9 jit_solution(14907766583942764486)
XLA Ops:
  0.7 1.3 %shard_map.93.token_ref = bf16[512,128]{1,0:T(8,128)(2,1)S(1)} custom-call(bf16[128,2048]{1,0:T(8,128)(2,1)} %bitcast.10, bf16[128,2048]{1,0:T(8,128)(2,1)} %bitcast.16), custom_call_target="tpu_custom_call" | custom-call | flops 67108864 | bytes 1179648 | tf_op jit(solution)/shard_map/pallas_call | solution.py:333
  2.0 3.0 %collective-permute-start = (bf16[512,128]{1,0:T(8,128)(2,1)S(1)}, bf16[512,128]{1,0:T(8,128)(2,1)S(1)}, u32[]{:S(2)}, u32[]{:S(2)}) collective-permute-start(bf16[512,128]{1,0:T(8,128)(2,1)S(1)} %shard_map.93.token_ref), channel_id=1, source_target_pairs={{0,1},{1,0},{2,3},{3,2},{4,5},{5,4},{6,7},{7,6},{8,10},{9,11},{10,... | collective-permute-start | bytes 393224 | tf_op jit(solution)/shard_map/ppermute | solution.py:362
  5.0 0.4 shard_map.94
  5.4 1.6 %collective-permute-start.1 = (bf16[512,128]{1,0:T(8,128)(2,1)S(1)}, bf16[512,128]{1,0:T(8,128)(2,1)S(1)}, u32[]{:S(2)}, u32[]{:S(2)}) collective-permute-start(bf16[512,128]{1,0:T(8,128)(2,1)S(1)} %get-tuple-element.40), channel_id=1, source_target_pairs={{0,2},{1,3},{2,0},{3,1},{4,6},{5,7},{6,4},{7,5},{8,9},{9,8},{10,11... | collective-permute-start | bytes 393224 | tf_op jit(solution)/shard_map/ppermute | solution.py:362
  7.1 2.6 %shard_map.92 = (bf16[2048,128]{1,0:T(8,128)(2,1)S(1)}, f32[128,2048]{1,0:T(8,128)S(1)}) custom-call(bf16[128,2048]{1,0:T(8,128)(2,1)S(1)} %bitcast.22, bf16[128,2048]{1,0:T(8,128)(2,1)S(1)} %bitcast.12, bf16[128,2048]{1,0:T(8,128)(2,1)S(1)} %bitcast.18), custom_call_target="tpu_custom_call" | custom-call | flops 134217728 | bytes 3145728 | tf_op jit(solution)/shard_map/pallas_call | solution.py:333
  9.7 2.0 %collective-permute-done.1.refs_2_.refs_3_ = bf16[512,128]{1,0:T(8,128)(2,1)S(1)} collective-permute-done((bf16[512,128]{1,0:T(8,128)(2,1)S(1)}, bf16[512,128]{1,0:T(8,128)(2,1)S(1)}, u32[]{:S(2)}, u32[]{:S(2)}) %collective-permute-start.1) | collective-permute-done | bytes 131104 | tf_op jit(solution)/shard_map/ppermute | solution.py:362
  11.7 1.2 %collective-permute-done.2.refs_3_.refs_4_ = bf16[512,128]{1,0:T(8,128)(2,1)S(1)} collective-permute-done((bf16[512,128]{1,0:T(8,128)(2,1)S(1)}, bf16[512,128]{1,0:T(8,128)(2,1)S(1)}, u32[]{:S(2)}, u32[]{:S(2)}) %collective-permute-start.2) | collective-permute-done | bytes 131104 | tf_op jit(solution)/shard_map/ppermute | solution.py:362
  12.9 3.0 %collective-permute-start.3 = (bf16[512,128]{1,0:T(8,128)(2,1)S(1)}, bf16[512,128]{1,0:T(8,128)(2,1)S(1)}, u32[]{:S(2)}, u32[]{:S(2)}) collective-permute-start(bf16[512,128]{1,0:T(8,128)(2,1)S(1)} %shard_map.95), channel_id=1, source_target_pairs={{0,4},{1,5},{2,6},{3,7},{4,0},{5,1},{6,2},{7,3},{8,12},{9,13},{10,... | collective-permute-start | bytes 393224 | tf_op jit(solution)/shard_map/ppermute | solution.py:379
  15.9 5.3 %collective-permute-done.3.refs_0_ = bf16[512,128]{1,0:T(8,128)(2,1)S(1)} collective-permute-done((bf16[512,128]{1,0:T(8,128)(2,1)S(1)}, bf16[512,128]{1,0:T(8,128)(2,1)S(1)}, u32[]{:S(2)}, u32[]{:S(2)}) %collective-permute-start.3) | collective-permute-done | bytes 131104 | tf_op jit(solution)/shard_map/ppermute | solution.py:379
  21.5 0.9 %collective-permute-start.5 = (bf16[512,128]{1,0:T(8,128)(2,1)S(1)}, bf16[512,128]{1,0:T(8,128)(2,1)S(1)}, u32[]{:S(2)}, u32[]{:S(2)}) collective-permute-start(bf16[512,128]{1,0:T(8,128)(2,1)S(1)} %shard_map.97.refs_5_), channel_id=1, source_target_pairs={{0,1},{1,0},{2,3},{3,2},{4,5},{5,4},{6,7},{7,6},{8,10},{9,11},{10,... | collective-permute-start | bytes 393224 | tf_op jit(solution)/shard_map/ppermute | solution.py:362
  22.4 0.2 shard_map.98
  22.7 2.7 %collective-permute-start.6 = (bf16[512,128]{1,0:T(8,128)(2,1)S(1)}, bf16[512,128]{1,0:T(8,128)(2,1)S(1)}, u32[]{:S(2)}, u32[]{:S(2)}) collective-permute-start(bf16[512,128]{1,0:T(8,128)(2,1)S(1)} %get-tuple-element.46), channel_id=1, source_target_pairs={{0,3},{1,2},{2,1},{3,0},{4,7},{5,6},{6,5},{7,4},{8,11},{9,10},{10,... | collective-permute-start | bytes 393224 | tf_op jit(solution)/shard_map/ppermute | solution.py:362
  25.4 2.7 %collective-permute-done.5.refs_6_.refs_11_ = bf16[512,128]{1,0:T(8,128)(2,1)S(1)} collective-permute-done((bf16[512,128]{1,0:T(8,128)(2,1)S(1)}, bf16[512,128]{1,0:T(8,128)(2,1)S(1)}, u32[]{:S(2)}, u32[]{:S(2)}) %collective-permute-start.5) | collective-permute-done | bytes 131104 | tf_op jit(solution)/shard_map/ppermute | solution.py:362
  28.1 0.4 shard_map.99
  28.6 0.9 %collective-permute-done.6.refs_7_.refs_12_ = bf16[512,128]{1,0:T(8,128)(2,1)S(1)} collective-permute-done((bf16[512,128]{1,0:T(8,128)(2,1)S(1)}, bf16[512,128]{1,0:T(8,128)(2,1)S(1)}, u32[]{:S(2)}, u32[]{:S(2)}) %collective-permute-start.6) | collective-permute-done | bytes 131104 | tf_op jit(solution)/shard_map/ppermute | solution.py:362
  29.5 1.0 %shard_map.100 = (f32[128,512]{1,0:T(8,128)S(1)}, f32[128,128]{1,0:T(8,128)S(1)}, bf16[128,2048]{1,0:T(8,128)(2,1)S(1)}, bf16[544,128]{1,0:T(8,128)(2,1)S(1)}, b...) custom-call(bf16[128,2048]{1,0:T(8,128)(2,1)S(1)} %bitcast.24, ...), custom_call_target="tpu_custom_call" | custom-call | flops 134217728 | bytes 4825088 | tf_op jit(solution)/shard_map/pallas_call | solution.py:333
  30.5 1.8 %collective-permute-start.7 = (bf16[544,128]{1,0:T(8,128)(2,1)S(1)}, bf16[544,128]{1,0:T(8,128)(2,1)S(1)}, u32[]{:S(2)}, u32[]{:S(2)}) collective-permute-start(bf16[544,128]{1,0:T(8,128)(2,1)S(1)} %get-tuple-element.55), channel_id=1, source_target_pairs={{0,3},{1,2},{2,1},{3,0},{4,7},{5,6},{6,5},{7,4},{8,11},{9,10},{10,... | collective-permute-start | bytes 417800 | tf_op jit(solution)/shard_map/ppermute | solution.py:362
  32.3 1.0 %collective-permute-start.8 = (bf16[544,128]{1,0:T(8,128)(2,1)S(1)}, bf16[544,128]{1,0:T(8,128)(2,1)S(1)}, u32[]{:S(2)}, u32[]{:S(2)}) collective-permute-start(bf16[544,128]{1,0:T(8,128)(2,1)S(1)} %get-tuple-element.56), channel_id=1, source_target_pairs={{0,1},{1,0},{2,3},{3,2},{4,5},{5,4},{6,7},{7,6},{8,9},{9,8},{10,11... | collective-permute-start | bytes 417800 | tf_op jit(solution)/shard_map/ppermute | solution.py:362
  33.3 0.7 %collective-permute-start.9 = (bf16[544,128]{1,0:T(8,128)(2,1)S(1)}, bf16[544,128]{1,0:T(8,128)(2,1)S(1)}, u32[]{:S(2)}, u32[]{:S(2)}) collective-permute-start(bf16[544,128]{1,0:T(8,128)(2,1)S(1)} %get-tuple-element.57), channel_id=1, source_target_pairs={{0,2},{1,3},{2,0},{3,1},{4,6},{5,7},{6,4},{7,5},{8,10},{9,11},{10,... | collective-permute-start | bytes 417800 | tf_op jit(solution)/shard_map/ppermute | solution.py:362
  34.1 3.5 %shard_map.101 = (bf16[128,2048]{1,0:T(8,128)(2,1)}, bf16[128,2048]{1,0:T(8,128)(2,1)}, f32[128,2048]{1,0:T(8,128)S(1)}, f32[128,2048]{1,0:T(8,128)S(1)}, f32[8,128]{1,0:T(8,128)S(1)}) custom-call(bf16[128,2048]{1,0:T(8,128)(2,1)S(1)} %bitcast.25, bf16[128,2048]{1,0:T(8,128)(2,1)S(1)} %bitcast.13, bf16[128,2048]{1,0:T(8,128)(2,1)S(1)} %bitcast.19, ...), custom_call_target="tpu_custom_call" | custom-call | flops 335544320 | bytes 7680000 | tf_op jit(solution)/shard_map/pallas_call | solution.py:333
  37.6 0.9 %collective-permute-done.8.refs_2_.refs_3_ = bf16[544,128]{1,0:T(8,128)(2,1)S(1)} collective-permute-done((bf16[544,128]{1,0:T(8,128)(2,1)S(1)}, bf16[544,128]{1,0:T(8,128)(2,1)S(1)}, u32[]{:S(2)}, u32[]{:S(2)}) %collective-permute-start.8) | collective-permute-done | bytes 139296 | tf_op jit(solution)/shard_map/ppermute | solution.py:362
  38.8 1.8 %collective-permute-start.10 = (bf16[544,128]{1,0:T(8,128)(2,1)S(1)}, bf16[544,128]{1,0:T(8,128)(2,1)S(1)}, u32[]{:S(2)}, u32[]{:S(2)}) collective-permute-start(bf16[544,128]{1,0:T(8,128)(2,1)S(1)} %get-tuple-element.59), channel_id=1, source_target_pairs={{0,4},{1,5},{2,6},{3,7},{4,0},{5,1},{6,2},{7,3},{8,12},{9,13},{10,... | collective-permute-start | bytes 417800 | tf_op jit(solution)/shard_map/ppermute | solution.py:379
  40.6 2.0 %collective-permute-start.15 = (f32[16,128]{1,0:T(8,128)S(1)}, f32[16,128]{1,0:T(8,128)S(1)}, u32[]{:S(2)}, u32[]{:S(2)}) collective-permute-start(f32[16,128]{1,0:T(8,128)S(1)} %get-tuple-element.60.refs_5_), channel_id=1, source_target_pairs={{0,20},{1,21},{2,22},{3,23},{4,16},{5,17},{6,18},{7,19},{8,28},{9,... | collective-permute-start | bytes 24584 | tf_op jit(solution)/shard_map/ppermute | solution.py:399
  42.6 0.7 %collective-permute-start.14 = (f32[16,128]{1,0:T(8,128)S(1)}, f32[16,128]{1,0:T(8,128)S(1)}, u32[]{:S(2)}, u32[]{:S(2)}) collective-permute-start(f32[16,128]{1,0:T(8,128)S(1)} %get-tuple-element.60.refs_5_), channel_id=1, source_target_pairs={{0,16},{1,17},{2,18},{3,19},{4,20},{5,21},{6,22},{7,23},{8,24},{9,... | collective-permute-start | bytes 24584 | tf_op jit(solution)/shard_map/ppermute | solution.py:399
  43.2 3.1 %collective-permute-done.10.refs_0_ = bf16[544,128]{1,0:T(8,128)(2,1)S(1)} collective-permute-done((bf16[544,128]{1,0:T(8,128)(2,1)S(1)}, bf16[544,128]{1,0:T(8,128)(2,1)S(1)}, u32[]{:S(2)}, u32[]{:S(2)}) %collective-permute-start.10) | collective-permute-done | bytes 139296 | tf_op jit(solution)/shard_map/ppermute | solution.py:379
  46.5 1.2 %collective-permute-start.13 = (bf16[512,128]{1,0:T(8,128)(2,1)S(1)}, bf16[512,128]{1,0:T(8,128)(2,1)S(1)}, u32[]{:S(2)}, u32[]{:S(2)}) collective-permute-start(bf16[512,128]{1,0:T(8,128)(2,1)S(1)} %shard_map.103.refs_5_), channel_id=1, source_target_pairs={{0,3},{1,2},{2,1},{3,0},{4,7},{5,6},{6,5},{7,4},{8,9},{9,8},{10,11... | collective-permute-start | bytes 393224 | tf_op jit(solution)/shard_map/ppermute | solution.py:362
  47.8 0.3 collective-permute-start.11
  48.1 0.3 shard_map.105
  48.3 2.2 %collective-permute-start.12 = (bf16[512,128]{1,0:T(8,128)(2,1)S(1)}, bf16[512,128]{1,0:T(8,128)(2,1)S(1)}, u32[]{:S(2)}, u32[]{:S(2)}) collective-permute-start(bf16[512,128]{1,0:T(8,128)(2,1)S(1)} %get-tuple-element.61), channel_id=1, source_target_pairs={{0,2},{1,3},{2,0},{3,1},{4,6},{5,7},{6,4},{7,5},{8,11},{9,10},{10,... | collective-permute-start | bytes 393224 | tf_op jit(solution)/shard_map/ppermute | solution.py:362
  50.6 1.9 %collective-permute-done.13.refs_5_ = bf16[512,128]{1,0:T(8,128)(2,1)S(1)} collective-permute-done((bf16[512,128]{1,0:T(8,128)(2,1)S(1)}, bf16[512,128]{1,0:T(8,128)(2,1)S(1)}, u32[]{:S(2)}, u32[]{:S(2)}) %collective-permute-start.13) | collective-permute-done | bytes 131104 | tf_op jit(solution)/shard_map/ppermute | solution.py:362
  52.5 1.1 %shard_map.106 = (bf16[128,2048]{1,0:T(8,128)(2,1)}, bf16[128,2048]{1,0:T(8,128)(2,1)}) custom-call(bf16[128,2048]{1,0:T(8,128)(2,1)S(1)} %bitcast.14, bf16[128,2048]{1,0:T(8,128)(2,1)S(1)} %bitcast.20, f32[128,2048]{1,0:T(8,128)S(1)} %get-tuple-element.52.refs_2_, f32[128,2048]{1,0:T(8,128)S(1)} %get-tuple-element.53.refs_3_, ...), custom_call_target="tpu_custom_call" | custom-call | flops 67108864 | bytes 4456448 | tf_op jit(solution)/shard_map/pallas_call | solution.py:333
  53.8 1.1 %shard_map.107 = (bf16[128,2048]{1,0:T(8,128)(2,1)}, bf16[128,2048]{1,0:T(8,128)(2,1)}, f32[16,128]{1,0:T(8,128)}) custom-call(bf16[128,2048]{1,0:T(8,128)(2,1)S(1)} %bitcast.15, bf16[128,2048]{1,0:T(8,128)(2,1)S(1)} %bitcast.21, f32[128,2048]{1,0:T(8,128)S(1)} %get-tuple-element.52.refs_2_, ...), custom_call_target="tpu_custom_call", output_to_operand_aliasing={{0}: (6, {}), {1}: (7, {})} | custom-call | flops 67108864 | bytes 5529600 | tf_op jit(solution)/shard_map/pallas_call | solution.py:333
  (29 shorter events, 1.4 us)
Async XLA Ops:
  0.6 4.3 %copy-start = (bf16[1,128,2048]{2,1,0:T(8,128)(2,1)S(1)}, bf16[1,128,2048]{2,1,0:T(8,128)(2,1)}, u32[]{:S(2)}) copy-start(bf16[1,128,2048]{2,1,0:T(8,128)(2,1)} %param.6) | copy-start | bytes 1572868
  0.6 4.3 %copy-start.1 = (bf16[1,128,2048]{2,1,0:T(8,128)(2,1)S(1)}, bf16[1,128,2048]{2,1,0:T(8,128)(2,1)}, u32[]{:S(2)}) copy-start(bf16[1,128,2048]{2,1,0:T(8,128)(2,1)} %param.7) | copy-start | bytes 1572868
  2.0 5.1 %copy-start.2 = (bf16[1,128,2048]{2,1,0:T(8,128)(2,1)S(1)}, bf16[1,128,2048]{2,1,0:T(8,128)(2,1)}, u32[]{:S(2)}) copy-start(bf16[1,128,2048]{2,1,0:T(8,128)(2,1)} %param.5) | copy-start | bytes 1572868
  2.0 7.7 %collective-permute-start = (bf16[512,128]{1,0:T(8,128)(2,1)S(1)}, bf16[512,128]{1,0:T(8,128)(2,1)S(1)}, u32[]{:S(2)}, u32[]{:S(2)}) collective-permute-start(bf16[512,128]{1,0:T(8,128)(2,1)S(1)} %shard_map.93.token_ref), channel_id=1, source_target_pairs={{0,1},{1,0},{2,3},{3,2},{4,5},{5,4},{6,7},{7,6},{8,10},{9,11},{10,... | collective-permute-start | bytes 393224 | tf_op jit(solution)/shard_map/ppermute | solution.py:362
  5.4 6.3 %collective-permute-start.1 = (bf16[512,128]{1,0:T(8,128)(2,1)S(1)}, bf16[512,128]{1,0:T(8,128)(2,1)S(1)}, u32[]{:S(2)}, u32[]{:S(2)}) collective-permute-start(bf16[512,128]{1,0:T(8,128)(2,1)S(1)} %get-tuple-element.40), channel_id=1, source_target_pairs={{0,2},{1,3},{2,0},{3,1},{4,6},{5,7},{6,4},{7,5},{8,9},{9,8},{10,11... | collective-permute-start | bytes 393224 | tf_op jit(solution)/shard_map/ppermute | solution.py:362
  7.0 5.9 %collective-permute-start.2 = (bf16[512,128]{1,0:T(8,128)(2,1)S(1)}, bf16[512,128]{1,0:T(8,128)(2,1)S(1)}, u32[]{:S(2)}, u32[]{:S(2)}) collective-permute-start(bf16[512,128]{1,0:T(8,128)(2,1)S(1)} %get-tuple-element.41), channel_id=1, source_target_pairs={{0,3},{1,2},{2,1},{3,0},{4,7},{5,6},{6,5},{7,4},{8,11},{9,10},{10,... | collective-permute-start | bytes 393224 | tf_op jit(solution)/shard_map/ppermute | solution.py:362
  12.9 8.3 %collective-permute-start.3 = (bf16[512,128]{1,0:T(8,128)(2,1)S(1)}, bf16[512,128]{1,0:T(8,128)(2,1)S(1)}, u32[]{:S(2)}, u32[]{:S(2)}) collective-permute-start(bf16[512,128]{1,0:T(8,128)(2,1)S(1)} %shard_map.95), channel_id=1, source_target_pairs={{0,4},{1,5},{2,6},{3,7},{4,0},{5,1},{6,2},{7,3},{8,12},{9,13},{10,... | collective-permute-start | bytes 393224 | tf_op jit(solution)/shard_map/ppermute | solution.py:379
  21.5 6.6 %copy-start.3 = (bf16[1,128,2048]{2,1,0:T(8,128)(2,1)S(1)}, bf16[1,128,2048]{2,1,0:T(8,128)(2,1)}, u32[]{:S(2)}) copy-start(bf16[1,128,2048]{2,1,0:T(8,128)(2,1)} %param.9) | copy-start | bytes 1572868
  21.5 6.5 %collective-permute-start.5 = (bf16[512,128]{1,0:T(8,128)(2,1)S(1)}, bf16[512,128]{1,0:T(8,128)(2,1)S(1)}, u32[]{:S(2)}, u32[]{:S(2)}) collective-permute-start(bf16[512,128]{1,0:T(8,128)(2,1)S(1)} %shard_map.97.refs_5_), channel_id=1, source_target_pairs={{0,1},{1,0},{2,3},{3,2},{4,5},{5,4},{6,7},{7,6},{8,10},{9,11},{10,... | collective-permute-start | bytes 393224 | tf_op jit(solution)/shard_map/ppermute | solution.py:362
  22.4 5.7 %collective-permute-start.4 = (bf16[512,128]{1,0:T(8,128)(2,1)S(1)}, bf16[512,128]{1,0:T(8,128)(2,1)S(1)}, u32[]{:S(2)}, u32[]{:S(2)}) collective-permute-start(bf16[512,128]{1,0:T(8,128)(2,1)S(1)} %shard_map.96.refs_5_), channel_id=1, source_target_pairs={{0,2},{1,3},{2,0},{3,1},{4,6},{5,7},{6,4},{7,5},{8,9},{9,8},{10,11... | collective-permute-start | bytes 393224 | tf_op jit(solution)/shard_map/ppermute | solution.py:362
  22.4 5.7 %copy-start.4 = (f32[2048]{0:T(1024)S(1)}, f32[2048]{0:T(1024)}, u32[]{:S(2)}) copy-start(f32[2048]{0:T(1024)} %param.8) | copy-start | bytes 24580
  22.7 6.9 %collective-permute-start.6 = (bf16[512,128]{1,0:T(8,128)(2,1)S(1)}, bf16[512,128]{1,0:T(8,128)(2,1)S(1)}, u32[]{:S(2)}, u32[]{:S(2)}) collective-permute-start(bf16[512,128]{1,0:T(8,128)(2,1)S(1)} %get-tuple-element.46), channel_id=1, source_target_pairs={{0,3},{1,2},{2,1},{3,0},{4,7},{5,6},{6,5},{7,4},{8,11},{9,10},{10,... | collective-permute-start | bytes 393224 | tf_op jit(solution)/shard_map/ppermute | solution.py:362
  30.5 7.0 %collective-permute-start.7 = (bf16[544,128]{1,0:T(8,128)(2,1)S(1)}, bf16[544,128]{1,0:T(8,128)(2,1)S(1)}, u32[]{:S(2)}, u32[]{:S(2)}) collective-permute-start(bf16[544,128]{1,0:T(8,128)(2,1)S(1)} %get-tuple-element.55), channel_id=1, source_target_pairs={{0,3},{1,2},{2,1},{3,0},{4,7},{5,6},{6,5},{7,4},{8,11},{9,10},{10,... | collective-permute-start | bytes 417800 | tf_op jit(solution)/shard_map/ppermute | solution.py:362
  32.3 6.1 %collective-permute-start.8 = (bf16[544,128]{1,0:T(8,128)(2,1)S(1)}, bf16[544,128]{1,0:T(8,128)(2,1)S(1)}, u32[]{:S(2)}, u32[]{:S(2)}) collective-permute-start(bf16[544,128]{1,0:T(8,128)(2,1)S(1)} %get-tuple-element.56), channel_id=1, source_target_pairs={{0,1},{1,0},{2,3},{3,2},{4,5},{5,4},{6,7},{7,6},{8,9},{9,8},{10,11... | collective-permute-start | bytes 417800 | tf_op jit(solution)/shard_map/ppermute | solution.py:362
  33.3 5.3 %collective-permute-start.9 = (bf16[544,128]{1,0:T(8,128)(2,1)S(1)}, bf16[544,128]{1,0:T(8,128)(2,1)S(1)}, u32[]{:S(2)}, u32[]{:S(2)}) collective-permute-start(bf16[544,128]{1,0:T(8,128)(2,1)S(1)} %get-tuple-element.57), channel_id=1, source_target_pairs={{0,2},{1,3},{2,0},{3,1},{4,6},{5,7},{6,4},{7,5},{8,10},{9,11},{10,... | collective-permute-start | bytes 417800 | tf_op jit(solution)/shard_map/ppermute | solution.py:362
  38.8 7.5 %collective-permute-start.10 = (bf16[544,128]{1,0:T(8,128)(2,1)S(1)}, bf16[544,128]{1,0:T(8,128)(2,1)S(1)}, u32[]{:S(2)}, u32[]{:S(2)}) collective-permute-start(bf16[544,128]{1,0:T(8,128)(2,1)S(1)} %get-tuple-element.59), channel_id=1, source_target_pairs={{0,4},{1,5},{2,6},{3,7},{4,0},{5,1},{6,2},{7,3},{8,12},{9,13},{10,... | collective-permute-start | bytes 417800 | tf_op jit(solution)/shard_map/ppermute | solution.py:379
  40.6 10.0 %collective-permute-start.15 = (f32[16,128]{1,0:T(8,128)S(1)}, f32[16,128]{1,0:T(8,128)S(1)}, u32[]{:S(2)}, u32[]{:S(2)}) collective-permute-start(f32[16,128]{1,0:T(8,128)S(1)} %get-tuple-element.60.refs_5_), channel_id=1, source_target_pairs={{0,20},{1,21},{2,22},{3,23},{4,16},{5,17},{6,18},{7,19},{8,28},{9,... | collective-permute-start | bytes 24584 | tf_op jit(solution)/shard_map/ppermute | solution.py:399
  42.6 8.0 %collective-permute-start.14 = (f32[16,128]{1,0:T(8,128)S(1)}, f32[16,128]{1,0:T(8,128)S(1)}, u32[]{:S(2)}, u32[]{:S(2)}) collective-permute-start(f32[16,128]{1,0:T(8,128)S(1)} %get-tuple-element.60.refs_5_), channel_id=1, source_target_pairs={{0,16},{1,17},{2,18},{3,19},{4,20},{5,21},{6,22},{7,23},{8,24},{9,... | collective-permute-start | bytes 24584 | tf_op jit(solution)/shard_map/ppermute | solution.py:399
  46.5 6.0 %collective-permute-start.13 = (bf16[512,128]{1,0:T(8,128)(2,1)S(1)}, bf16[512,128]{1,0:T(8,128)(2,1)S(1)}, u32[]{:S(2)}, u32[]{:S(2)}) collective-permute-start(bf16[512,128]{1,0:T(8,128)(2,1)S(1)} %shard_map.103.refs_5_), channel_id=1, source_target_pairs={{0,3},{1,2},{2,1},{3,0},{4,7},{5,6},{6,5},{7,4},{8,9},{9,8},{10,11... | collective-permute-start | bytes 393224 | tf_op jit(solution)/shard_map/ppermute | solution.py:362
  47.8 6.0 %collective-permute-start.11 = (bf16[512,128]{1,0:T(8,128)(2,1)S(1)}, bf16[512,128]{1,0:T(8,128)(2,1)S(1)}, u32[]{:S(2)}, u32[]{:S(2)}) collective-permute-start(bf16[512,128]{1,0:T(8,128)(2,1)S(1)} %shard_map.104.refs_6_), channel_id=1, source_target_pairs={{0,1},{1,0},{2,3},{3,2},{4,5},{5,4},{6,7},{7,6},{8,10},{9,11},{10,... | collective-permute-start | bytes 393224 | tf_op jit(solution)/shard_map/ppermute | solution.py:362
  48.3 5.3 %collective-permute-start.12 = (bf16[512,128]{1,0:T(8,128)(2,1)S(1)}, bf16[512,128]{1,0:T(8,128)(2,1)S(1)}, u32[]{:S(2)}, u32[]{:S(2)}) collective-permute-start(bf16[512,128]{1,0:T(8,128)(2,1)S(1)} %get-tuple-element.61), channel_id=1, source_target_pairs={{0,2},{1,3},{2,0},{3,1},{4,6},{5,7},{6,4},{7,5},{8,11},{9,10},{10,... | collective-permute-start | bytes 393224 | tf_op jit(solution)/shard_map/ppermute | solution.py:362
  50.6 3.0 %collective-permute-start.16 = (f32[16,128]{1,0:T(8,128)S(1)}, f32[16,128]{1,0:T(8,128)S(1)}, u32[]{:S(2)}, u32[]{:S(2)}) collective-permute-start(f32[16,128]{1,0:T(8,128)S(1)} %add_add_fusion.refs_8_), channel_id=1, source_target_pairs={{0,8},{8,0},{16,24},{24,16},{1,9},{9,1},{17,25},{25,17},{2,10},{10... | collective-permute-start | bytes 24584 | tf_op jit(solution)/shard_map/ppermute | solution.py:351

commit v4 on v3

--- a/solution.py
+++ b/solution.py
@@ -32,7 +32,7 @@
 
 
 STATE_ORDERS = (((0, 1, 2, 3), (0, 2, 1, 3)), ((0, 2, 1, 3), (0, 1, 2, 3)))
-GRAD_ORDERS = (((0, 3, 1, 2), (0, 3, 1, 2)), ((0, 3, 1, 2), (0, 1, 2, 3)))
+GRAD_ORDERS = (((0, 3, 1, 2), (0, 3, 1, 2)), ((0, 1, 3, 2), (0, 1, 2, 3)))
 NORM_ORDERS = (STATE_ORDERS[1], GRAD_ORDERS[0])
 
 

time: 55.1 us -> 55.8 us (1.013)
  waiting for transfers between devices: 18.5 us -> 19.2 us
    ppermute x12, waiting for transfers between devices: 10 us -> 10.8 us  [own_and_swapped(): results.append(lax.ppermute(pieces[slot], ('dp', 'seq'), pairs))]
where the time goes in v4:
time: 55.8 us; the launch traced here: 55.7 us
  starting transfers between devices  23 us (41%)
  waiting for transfers between devices  19.2 us (34%)
  Pallas kernels  12.6 us (23%)
  between operations  0.78 us (1%)
    ppermute x12, starting transfers between devices, own_and_swapped(): results.append(lax.ppermute(pieces[slot], ('dp', 'seq'), pairs))  15.5 us
    pallas_call x16, Pallas kernels, call(): pl.pallas_call(kernel, out_shape=tuple(outs), in_specs=[ins.get(i, VMEM)...  12.6 us
    ppermute x12, waiting for transfers between devices, own_and_swapped(): results.append(lax.ppermute(pieces[slot], ('dp', 'seq'), pairs))  10.8 us
    ppermute x2, waiting for transfers between devices, shifted(): return lax.ppermute(array, 'seq', pairs)  8.4 us
    ppermute x2, starting transfers between devices, shifted(): return lax.ppermute(array, 'seq', pairs)  4.74 us
    ppermute x2, starting transfers between devices, exclusive_scan(): gains.append(lax.ppermute(gains[0], ('dp', 'seq'), pairs))  2.66 us
  transfers between devices with their start and end apart: 17, of which 11 were waited for; matrix products, arithmetic and copies ran while one was open for 0% of the time, Pallas kernels for 16%

profile of v4, /device:TPU:0, one launch (start us, length us, event | category | flops | bytes accessed | tf_op | source)
XLA Modules:
  0.0 55.7 jit_solution(12805165911016230916)
XLA Ops:
  0.7 1.3 %shard_map.93.token_ref = bf16[512,128]{1,0:T(8,128)(2,1)S(1)} custom-call(bf16[128,2048]{1,0:T(8,128)(2,1)} %bitcast.10, bf16[128,2048]{1,0:T(8,128)(2,1)} %bitcast.16), custom_call_target="tpu_custom_call" | custom-call | flops 67108864 | bytes 1179648 | tf_op jit(solution)/shard_map/pallas_call | solution.py:333
  2.0 3.0 %collective-permute-start = (bf16[512,128]{1,0:T(8,128)(2,1)S(1)}, bf16[512,128]{1,0:T(8,128)(2,1)S(1)}, u32[]{:S(2)}, u32[]{:S(2)}) collective-permute-start(bf16[512,128]{1,0:T(8,128)(2,1)S(1)} %shard_map.93.token_ref), channel_id=1, source_target_pairs={{0,1},{1,0},{2,3},{3,2},{4,5},{5,4},{6,7},{7,6},{8,10},{9,11},{10,... | collective-permute-start | bytes 393224 | tf_op jit(solution)/shard_map/ppermute | solution.py:362
  5.0 0.4 shard_map.94
  5.4 1.6 %collective-permute-start.1 = (bf16[512,128]{1,0:T(8,128)(2,1)S(1)}, bf16[512,128]{1,0:T(8,128)(2,1)S(1)}, u32[]{:S(2)}, u32[]{:S(2)}) collective-permute-start(bf16[512,128]{1,0:T(8,128)(2,1)S(1)} %get-tuple-element.40), channel_id=1, source_target_pairs={{0,2},{1,3},{2,0},{3,1},{4,6},{5,7},{6,4},{7,5},{8,9},{9,8},{10,11... | collective-permute-start | bytes 393224 | tf_op jit(solution)/shard_map/ppermute | solution.py:362
  7.1 2.6 %shard_map.92 = (bf16[2048,128]{1,0:T(8,128)(2,1)S(1)}, f32[128,2048]{1,0:T(8,128)S(1)}) custom-call(bf16[128,2048]{1,0:T(8,128)(2,1)S(1)} %bitcast.22, bf16[128,2048]{1,0:T(8,128)(2,1)S(1)} %bitcast.12, bf16[128,2048]{1,0:T(8,128)(2,1)S(1)} %bitcast.18), custom_call_target="tpu_custom_call" | custom-call | flops 134217728 | bytes 3145728 | tf_op jit(solution)/shard_map/pallas_call | solution.py:333
  9.7 2.0 %collective-permute-done.1.refs_2_.refs_3_ = bf16[512,128]{1,0:T(8,128)(2,1)S(1)} collective-permute-done((bf16[512,128]{1,0:T(8,128)(2,1)S(1)}, bf16[512,128]{1,0:T(8,128)(2,1)S(1)}, u32[]{:S(2)}, u32[]{:S(2)}) %collective-permute-start.1) | collective-permute-done | bytes 131104 | tf_op jit(solution)/shard_map/ppermute | solution.py:362
  11.7 1.2 %collective-permute-done.2.refs_3_.refs_4_ = bf16[512,128]{1,0:T(8,128)(2,1)S(1)} collective-permute-done((bf16[512,128]{1,0:T(8,128)(2,1)S(1)}, bf16[512,128]{1,0:T(8,128)(2,1)S(1)}, u32[]{:S(2)}, u32[]{:S(2)}) %collective-permute-start.2) | collective-permute-done | bytes 131104 | tf_op jit(solution)/shard_map/ppermute | solution.py:362
  12.9 3.0 %collective-permute-start.3 = (bf16[512,128]{1,0:T(8,128)(2,1)S(1)}, bf16[512,128]{1,0:T(8,128)(2,1)S(1)}, u32[]{:S(2)}, u32[]{:S(2)}) collective-permute-start(bf16[512,128]{1,0:T(8,128)(2,1)S(1)} %shard_map.95), channel_id=1, source_target_pairs={{0,4},{1,5},{2,6},{3,7},{4,0},{5,1},{6,2},{7,3},{8,12},{9,13},{10,... | collective-permute-start | bytes 393224 | tf_op jit(solution)/shard_map/ppermute | solution.py:379
  15.9 5.3 %collective-permute-done.3.refs_0_ = bf16[512,128]{1,0:T(8,128)(2,1)S(1)} collective-permute-done((bf16[512,128]{1,0:T(8,128)(2,1)S(1)}, bf16[512,128]{1,0:T(8,128)(2,1)S(1)}, u32[]{:S(2)}, u32[]{:S(2)}) %collective-permute-start.3) | collective-permute-done | bytes 131104 | tf_op jit(solution)/shard_map/ppermute | solution.py:379
  21.5 0.9 %collective-permute-start.5 = (bf16[512,128]{1,0:T(8,128)(2,1)S(1)}, bf16[512,128]{1,0:T(8,128)(2,1)S(1)}, u32[]{:S(2)}, u32[]{:S(2)}) collective-permute-start(bf16[512,128]{1,0:T(8,128)(2,1)S(1)} %shard_map.97.refs_5_), channel_id=1, source_target_pairs={{0,1},{1,0},{2,3},{3,2},{4,5},{5,4},{6,7},{7,6},{8,10},{9,11},{10,... | collective-permute-start | bytes 393224 | tf_op jit(solution)/shard_map/ppermute | solution.py:362
  22.4 0.2 shard_map.98
  22.7 2.7 %collective-permute-start.6 = (bf16[512,128]{1,0:T(8,128)(2,1)S(1)}, bf16[512,128]{1,0:T(8,128)(2,1)S(1)}, u32[]{:S(2)}, u32[]{:S(2)}) collective-permute-start(bf16[512,128]{1,0:T(8,128)(2,1)S(1)} %get-tuple-element.46), channel_id=1, source_target_pairs={{0,3},{1,2},{2,1},{3,0},{4,7},{5,6},{6,5},{7,4},{8,11},{9,10},{10,... | collective-permute-start | bytes 393224 | tf_op jit(solution)/shard_map/ppermute | solution.py:362
  25.4 2.7 %collective-permute-done.5.refs_6_.refs_11_ = bf16[512,128]{1,0:T(8,128)(2,1)S(1)} collective-permute-done((bf16[512,128]{1,0:T(8,128)(2,1)S(1)}, bf16[512,128]{1,0:T(8,128)(2,1)S(1)}, u32[]{:S(2)}, u32[]{:S(2)}) %collective-permute-start.5) | collective-permute-done | bytes 131104 | tf_op jit(solution)/shard_map/ppermute | solution.py:362
  28.1 0.4 shard_map.99
  28.6 0.9 %collective-permute-done.6.refs_7_.refs_12_ = bf16[512,128]{1,0:T(8,128)(2,1)S(1)} collective-permute-done((bf16[512,128]{1,0:T(8,128)(2,1)S(1)}, bf16[512,128]{1,0:T(8,128)(2,1)S(1)}, u32[]{:S(2)}, u32[]{:S(2)}) %collective-permute-start.6) | collective-permute-done | bytes 131104 | tf_op jit(solution)/shard_map/ppermute | solution.py:362
  29.5 1.0 %shard_map.100 = (f32[128,512]{1,0:T(8,128)S(1)}, f32[128,128]{1,0:T(8,128)S(1)}, bf16[128,2048]{1,0:T(8,128)(2,1)S(1)}, bf16[544,128]{1,0:T(8,128)(2,1)S(1)}, b...) custom-call(bf16[128,2048]{1,0:T(8,128)(2,1)S(1)} %bitcast.24, ...), custom_call_target="tpu_custom_call" | custom-call | flops 134217728 | bytes 4825088 | tf_op jit(solution)/shard_map/pallas_call | solution.py:333
  30.5 1.8 %collective-permute-start.7 = (bf16[544,128]{1,0:T(8,128)(2,1)S(1)}, bf16[544,128]{1,0:T(8,128)(2,1)S(1)}, u32[]{:S(2)}, u32[]{:S(2)}) collective-permute-start(bf16[544,128]{1,0:T(8,128)(2,1)S(1)} %get-tuple-element.55), channel_id=1, source_target_pairs={{0,3},{1,2},{2,1},{3,0},{4,7},{5,6},{6,5},{7,4},{8,11},{9,10},{10,... | collective-permute-start | bytes 417800 | tf_op jit(solution)/shard_map/ppermute | solution.py:362
  32.3 1.0 %collective-permute-start.8 = (bf16[544,128]{1,0:T(8,128)(2,1)S(1)}, bf16[544,128]{1,0:T(8,128)(2,1)S(1)}, u32[]{:S(2)}, u32[]{:S(2)}) collective-permute-start(bf16[544,128]{1,0:T(8,128)(2,1)S(1)} %get-tuple-element.56), channel_id=1, source_target_pairs={{0,1},{1,0},{2,3},{3,2},{4,5},{5,4},{6,7},{7,6},{8,9},{9,8},{10,11... | collective-permute-start | bytes 417800 | tf_op jit(solution)/shard_map/ppermute | solution.py:362
  33.3 0.7 %collective-permute-start.9 = (bf16[544,128]{1,0:T(8,128)(2,1)S(1)}, bf16[544,128]{1,0:T(8,128)(2,1)S(1)}, u32[]{:S(2)}, u32[]{:S(2)}) collective-permute-start(bf16[544,128]{1,0:T(8,128)(2,1)S(1)} %get-tuple-element.57), channel_id=1, source_target_pairs={{0,2},{1,3},{2,0},{3,1},{4,6},{5,7},{6,4},{7,5},{8,10},{9,11},{10,... | collective-permute-start | bytes 417800 | tf_op jit(solution)/shard_map/ppermute | solution.py:362
  34.1 3.5 %shard_map.101 = (bf16[128,2048]{1,0:T(8,128)(2,1)}, bf16[128,2048]{1,0:T(8,128)(2,1)}, f32[128,2048]{1,0:T(8,128)S(1)}, f32[128,2048]{1,0:T(8,128)S(1)}, f32[8,128]{1,0:T(8,128)S(1)}) custom-call(bf16[128,2048]{1,0:T(8,128)(2,1)S(1)} %bitcast.25, bf16[128,2048]{1,0:T(8,128)(2,1)S(1)} %bitcast.13, bf16[128,2048]{1,0:T(8,128)(2,1)S(1)} %bitcast.19, ...), custom_call_target="tpu_custom_call" | custom-call | flops 335544320 | bytes 7680000 | tf_op jit(solution)/shard_map/pallas_call | solution.py:333
  37.6 0.9 %collective-permute-done.8.refs_2_.refs_3_ = bf16[544,128]{1,0:T(8,128)(2,1)S(1)} collective-permute-done((bf16[544,128]{1,0:T(8,128)(2,1)S(1)}, bf16[544,128]{1,0:T(8,128)(2,1)S(1)}, u32[]{:S(2)}, u32[]{:S(2)}) %collective-permute-start.8) | collective-permute-done | bytes 139296 | tf_op jit(solution)/shard_map/ppermute | solution.py:362
  38.8 1.8 %collective-permute-start.10 = (bf16[544,128]{1,0:T(8,128)(2,1)S(1)}, bf16[544,128]{1,0:T(8,128)(2,1)S(1)}, u32[]{:S(2)}, u32[]{:S(2)}) collective-permute-start(bf16[544,128]{1,0:T(8,128)(2,1)S(1)} %get-tuple-element.59), channel_id=1, source_target_pairs={{0,4},{1,5},{2,6},{3,7},{4,0},{5,1},{6,2},{7,3},{8,12},{9,13},{10,... | collective-permute-start | bytes 417800 | tf_op jit(solution)/shard_map/ppermute | solution.py:379
  40.6 2.0 %collective-permute-start.15 = (f32[16,128]{1,0:T(8,128)S(1)}, f32[16,128]{1,0:T(8,128)S(1)}, u32[]{:S(2)}, u32[]{:S(2)}) collective-permute-start(f32[16,128]{1,0:T(8,128)S(1)} %get-tuple-element.60.refs_5_), channel_id=1, source_target_pairs={{0,20},{1,21},{2,22},{3,23},{4,16},{5,17},{6,18},{7,19},{8,28},{9,... | collective-permute-start | bytes 24584 | tf_op jit(solution)/shard_map/ppermute | solution.py:399
  42.6 0.7 %collective-permute-start.14 = (f32[16,128]{1,0:T(8,128)S(1)}, f32[16,128]{1,0:T(8,128)S(1)}, u32[]{:S(2)}, u32[]{:S(2)}) collective-permute-start(f32[16,128]{1,0:T(8,128)S(1)} %get-tuple-element.60.refs_5_), channel_id=1, source_target_pairs={{0,16},{1,17},{2,18},{3,19},{4,20},{5,21},{6,22},{7,23},{8,24},{9,... | collective-permute-start | bytes 24584 | tf_op jit(solution)/shard_map/ppermute | solution.py:399
  43.2 3.1 %collective-permute-done.10.refs_0_ = bf16[544,128]{1,0:T(8,128)(2,1)S(1)} collective-permute-done((bf16[544,128]{1,0:T(8,128)(2,1)S(1)}, bf16[544,128]{1,0:T(8,128)(2,1)S(1)}, u32[]{:S(2)}, u32[]{:S(2)}) %collective-permute-start.10) | collective-permute-done | bytes 139296 | tf_op jit(solution)/shard_map/ppermute | solution.py:379
  46.7 1.4 %collective-permute-start.11 = (bf16[512,128]{1,0:T(8,128)(2,1)S(1)}, bf16[512,128]{1,0:T(8,128)(2,1)S(1)}, u32[]{:S(2)}, u32[]{:S(2)}) collective-permute-start(bf16[512,128]{1,0:T(8,128)(2,1)S(1)} %shard_map.104.refs_6_), channel_id=1, source_target_pairs={{0,3},{1,2},{2,1},{3,0},{4,7},{5,6},{6,5},{7,4},{8,10},{9,11},{10,... | collective-permute-start | bytes 393224 | tf_op jit(solution)/shard_map/ppermute | solution.py:362
  48.1 0.3 shard_map.105
  48.3 2.2 %collective-permute-start.12 = (bf16[512,128]{1,0:T(8,128)(2,1)S(1)}, bf16[512,128]{1,0:T(8,128)(2,1)S(1)}, u32[]{:S(2)}, u32[]{:S(2)}) collective-permute-start(bf16[512,128]{1,0:T(8,128)(2,1)S(1)} %get-tuple-element.61), channel_id=1, source_target_pairs={{0,2},{1,3},{2,0},{3,1},{4,6},{5,7},{6,4},{7,5},{8,11},{9,10},{10,... | collective-permute-start | bytes 393224 | tf_op jit(solution)/shard_map/ppermute | solution.py:362
  50.6 2.3 %collective-permute-done.13.refs_5_ = bf16[512,128]{1,0:T(8,128)(2,1)S(1)} collective-permute-done((bf16[512,128]{1,0:T(8,128)(2,1)S(1)}, bf16[512,128]{1,0:T(8,128)(2,1)S(1)}, u32[]{:S(2)}, u32[]{:S(2)}) %collective-permute-start.13) | collective-permute-done | bytes 131104 | tf_op jit(solution)/shard_map/ppermute | solution.py:362
  52.9 1.1 %shard_map.106 = (bf16[128,2048]{1,0:T(8,128)(2,1)}, bf16[128,2048]{1,0:T(8,128)(2,1)}) custom-call(bf16[128,2048]{1,0:T(8,128)(2,1)S(1)} %bitcast.14, bf16[128,2048]{1,0:T(8,128)(2,1)S(1)} %bitcast.20, f32[128,2048]{1,0:T(8,128)S(1)} %get-tuple-element.52.refs_2_, f32[128,2048]{1,0:T(8,128)S(1)} %get-tuple-element.53.refs_3_, ...), custom_call_target="tpu_custom_call" | custom-call | flops 67108864 | bytes 4456448 | tf_op jit(solution)/shard_map/pallas_call | solution.py:333
  54.0 0.6 collective-permute-done.12.refs_5_
  54.6 1.1 %shard_map.107 = (bf16[128,2048]{1,0:T(8,128)(2,1)}, bf16[128,2048]{1,0:T(8,128)(2,1)}, f32[16,128]{1,0:T(8,128)}) custom-call(bf16[128,2048]{1,0:T(8,128)(2,1)S(1)} %bitcast.15, bf16[128,2048]{1,0:T(8,128)(2,1)S(1)} %bitcast.21, f32[128,2048]{1,0:T(8,128)S(1)} %get-tuple-element.52.refs_2_, ...), custom_call_target="tpu_custom_call", output_to_operand_aliasing={{0}: (6, {}), {1}: (7, {})} | custom-call | flops 67108864 | bytes 5529600 | tf_op jit(solution)/shard_map/pallas_call | solution.py:333
  (29 shorter events, 1.3 us)
Async XLA Ops:
  0.6 4.3 %copy-start = (bf16[1,128,2048]{2,1,0:T(8,128)(2,1)S(1)}, bf16[1,128,2048]{2,1,0:T(8,128)(2,1)}, u32[]{:S(2)}) copy-start(bf16[1,128,2048]{2,1,0:T(8,128)(2,1)} %param.6) | copy-start | bytes 1572868
  0.6 4.3 %copy-start.1 = (bf16[1,128,2048]{2,1,0:T(8,128)(2,1)S(1)}, bf16[1,128,2048]{2,1,0:T(8,128)(2,1)}, u32[]{:S(2)}) copy-start(bf16[1,128,2048]{2,1,0:T(8,128)(2,1)} %param.7) | copy-start | bytes 1572868
  2.0 5.1 %copy-start.2 = (bf16[1,128,2048]{2,1,0:T(8,128)(2,1)S(1)}, bf16[1,128,2048]{2,1,0:T(8,128)(2,1)}, u32[]{:S(2)}) copy-start(bf16[1,128,2048]{2,1,0:T(8,128)(2,1)} %param.5) | copy-start | bytes 1572868
  2.0 7.7 %collective-permute-start = (bf16[512,128]{1,0:T(8,128)(2,1)S(1)}, bf16[512,128]{1,0:T(8,128)(2,1)S(1)}, u32[]{:S(2)}, u32[]{:S(2)}) collective-permute-start(bf16[512,128]{1,0:T(8,128)(2,1)S(1)} %shard_map.93.token_ref), channel_id=1, source_target_pairs={{0,1},{1,0},{2,3},{3,2},{4,5},{5,4},{6,7},{7,6},{8,10},{9,11},{10,... | collective-permute-start | bytes 393224 | tf_op jit(solution)/shard_map/ppermute | solution.py:362
  5.4 6.3 %collective-permute-start.1 = (bf16[512,128]{1,0:T(8,128)(2,1)S(1)}, bf16[512,128]{1,0:T(8,128)(2,1)S(1)}, u32[]{:S(2)}, u32[]{:S(2)}) collective-permute-start(bf16[512,128]{1,0:T(8,128)(2,1)S(1)} %get-tuple-element.40), channel_id=1, source_target_pairs={{0,2},{1,3},{2,0},{3,1},{4,6},{5,7},{6,4},{7,5},{8,9},{9,8},{10,11... | collective-permute-start | bytes 393224 | tf_op jit(solution)/shard_map/ppermute | solution.py:362
  7.0 5.9 %collective-permute-start.2 = (bf16[512,128]{1,0:T(8,128)(2,1)S(1)}, bf16[512,128]{1,0:T(8,128)(2,1)S(1)}, u32[]{:S(2)}, u32[]{:S(2)}) collective-permute-start(bf16[512,128]{1,0:T(8,128)(2,1)S(1)} %get-tuple-element.41), channel_id=1, source_target_pairs={{0,3},{1,2},{2,1},{3,0},{4,7},{5,6},{6,5},{7,4},{8,11},{9,10},{10,... | collective-permute-start | bytes 393224 | tf_op jit(solution)/shard_map/ppermute | solution.py:362
  12.9 8.3 %collective-permute-start.3 = (bf16[512,128]{1,0:T(8,128)(2,1)S(1)}, bf16[512,128]{1,0:T(8,128)(2,1)S(1)}, u32[]{:S(2)}, u32[]{:S(2)}) collective-permute-start(bf16[512,128]{1,0:T(8,128)(2,1)S(1)} %shard_map.95), channel_id=1, source_target_pairs={{0,4},{1,5},{2,6},{3,7},{4,0},{5,1},{6,2},{7,3},{8,12},{9,13},{10,... | collective-permute-start | bytes 393224 | tf_op jit(solution)/shard_map/ppermute | solution.py:379
  21.5 6.6 %copy-start.3 = (bf16[1,128,2048]{2,1,0:T(8,128)(2,1)S(1)}, bf16[1,128,2048]{2,1,0:T(8,128)(2,1)}, u32[]{:S(2)}) copy-start(bf16[1,128,2048]{2,1,0:T(8,128)(2,1)} %param.9) | copy-start | bytes 1572868
  21.5 6.5 %collective-permute-start.5 = (bf16[512,128]{1,0:T(8,128)(2,1)S(1)}, bf16[512,128]{1,0:T(8,128)(2,1)S(1)}, u32[]{:S(2)}, u32[]{:S(2)}) collective-permute-start(bf16[512,128]{1,0:T(8,128)(2,1)S(1)} %shard_map.97.refs_5_), channel_id=1, source_target_pairs={{0,1},{1,0},{2,3},{3,2},{4,5},{5,4},{6,7},{7,6},{8,10},{9,11},{10,... | collective-permute-start | bytes 393224 | tf_op jit(solution)/shard_map/ppermute | solution.py:362
  22.4 5.7 %collective-permute-start.4 = (bf16[512,128]{1,0:T(8,128)(2,1)S(1)}, bf16[512,128]{1,0:T(8,128)(2,1)S(1)}, u32[]{:S(2)}, u32[]{:S(2)}) collective-permute-start(bf16[512,128]{1,0:T(8,128)(2,1)S(1)} %shard_map.96.refs_5_), channel_id=1, source_target_pairs={{0,2},{1,3},{2,0},{3,1},{4,6},{5,7},{6,4},{7,5},{8,9},{9,8},{10,11... | collective-permute-start | bytes 393224 | tf_op jit(solution)/shard_map/ppermute | solution.py:362
  22.4 5.7 %copy-start.4 = (f32[2048]{0:T(1024)S(1)}, f32[2048]{0:T(1024)}, u32[]{:S(2)}) copy-start(f32[2048]{0:T(1024)} %param.8) | copy-start | bytes 24580
  22.7 6.9 %collective-permute-start.6 = (bf16[512,128]{1,0:T(8,128)(2,1)S(1)}, bf16[512,128]{1,0:T(8,128)(2,1)S(1)}, u32[]{:S(2)}, u32[]{:S(2)}) collective-permute-start(bf16[512,128]{1,0:T(8,128)(2,1)S(1)} %get-tuple-element.46), channel_id=1, source_target_pairs={{0,3},{1,2},{2,1},{3,0},{4,7},{5,6},{6,5},{7,4},{8,11},{9,10},{10,... | collective-permute-start | bytes 393224 | tf_op jit(solution)/shard_map/ppermute | solution.py:362
  30.5 7.0 %collective-permute-start.7 = (bf16[544,128]{1,0:T(8,128)(2,1)S(1)}, bf16[544,128]{1,0:T(8,128)(2,1)S(1)}, u32[]{:S(2)}, u32[]{:S(2)}) collective-permute-start(bf16[544,128]{1,0:T(8,128)(2,1)S(1)} %get-tuple-element.55), channel_id=1, source_target_pairs={{0,3},{1,2},{2,1},{3,0},{4,7},{5,6},{6,5},{7,4},{8,11},{9,10},{10,... | collective-permute-start | bytes 417800 | tf_op jit(solution)/shard_map/ppermute | solution.py:362
  32.3 6.1 %collective-permute-start.8 = (bf16[544,128]{1,0:T(8,128)(2,1)S(1)}, bf16[544,128]{1,0:T(8,128)(2,1)S(1)}, u32[]{:S(2)}, u32[]{:S(2)}) collective-permute-start(bf16[544,128]{1,0:T(8,128)(2,1)S(1)} %get-tuple-element.56), channel_id=1, source_target_pairs={{0,1},{1,0},{2,3},{3,2},{4,5},{5,4},{6,7},{7,6},{8,9},{9,8},{10,11... | collective-permute-start | bytes 417800 | tf_op jit(solution)/shard_map/ppermute | solution.py:362
  33.3 5.3 %collective-permute-start.9 = (bf16[544,128]{1,0:T(8,128)(2,1)S(1)}, bf16[544,128]{1,0:T(8,128)(2,1)S(1)}, u32[]{:S(2)}, u32[]{:S(2)}) collective-permute-start(bf16[544,128]{1,0:T(8,128)(2,1)S(1)} %get-tuple-element.57), channel_id=1, source_target_pairs={{0,2},{1,3},{2,0},{3,1},{4,6},{5,7},{6,4},{7,5},{8,10},{9,11},{10,... | collective-permute-start | bytes 417800 | tf_op jit(solution)/shard_map/ppermute | solution.py:362
  38.8 7.5 %collective-permute-start.10 = (bf16[544,128]{1,0:T(8,128)(2,1)S(1)}, bf16[544,128]{1,0:T(8,128)(2,1)S(1)}, u32[]{:S(2)}, u32[]{:S(2)}) collective-permute-start(bf16[544,128]{1,0:T(8,128)(2,1)S(1)} %get-tuple-element.59), channel_id=1, source_target_pairs={{0,4},{1,5},{2,6},{3,7},{4,0},{5,1},{6,2},{7,3},{8,12},{9,13},{10,... | collective-permute-start | bytes 417800 | tf_op jit(solution)/shard_map/ppermute | solution.py:379
  40.6 10.0 %collective-permute-start.15 = (f32[16,128]{1,0:T(8,128)S(1)}, f32[16,128]{1,0:T(8,128)S(1)}, u32[]{:S(2)}, u32[]{:S(2)}) collective-permute-start(f32[16,128]{1,0:T(8,128)S(1)} %get-tuple-element.60.refs_5_), channel_id=1, source_target_pairs={{0,20},{1,21},{2,22},{3,23},{4,16},{5,17},{6,18},{7,19},{8,28},{9,... | collective-permute-start | bytes 24584 | tf_op jit(solution)/shard_map/ppermute | solution.py:399
  42.6 8.0 %collective-permute-start.14 = (f32[16,128]{1,0:T(8,128)S(1)}, f32[16,128]{1,0:T(8,128)S(1)}, u32[]{:S(2)}, u32[]{:S(2)}) collective-permute-start(f32[16,128]{1,0:T(8,128)S(1)} %get-tuple-element.60.refs_5_), channel_id=1, source_target_pairs={{0,16},{1,17},{2,18},{3,19},{4,20},{5,21},{6,22},{7,23},{8,24},{9,... | collective-permute-start | bytes 24584 | tf_op jit(solution)/shard_map/ppermute | solution.py:399
  46.4 6.4 %collective-permute-start.13 = (bf16[512,128]{1,0:T(8,128)(2,1)S(1)}, bf16[512,128]{1,0:T(8,128)(2,1)S(1)}, u32[]{:S(2)}, u32[]{:S(2)}) collective-permute-start(bf16[512,128]{1,0:T(8,128)(2,1)S(1)} %shard_map.103.refs_5_), channel_id=1, source_target_pairs={{0,1},{1,0},{2,3},{3,2},{4,5},{5,4},{6,7},{7,6},{8,9},{9,8},{10,11... | collective-permute-start | bytes 393224 | tf_op jit(solution)/shard_map/ppermute | solution.py:362
  46.7 7.9 %collective-permute-start.11 = (bf16[512,128]{1,0:T(8,128)(2,1)S(1)}, bf16[512,128]{1,0:T(8,128)(2,1)S(1)}, u32[]{:S(2)}, u32[]{:S(2)}) collective-permute-start(bf16[512,128]{1,0:T(8,128)(2,1)S(1)} %shard_map.104.refs_6_), channel_id=1, source_target_pairs={{0,3},{1,2},{2,1},{3,0},{4,7},{5,6},{6,5},{7,4},{8,10},{9,11},{10,... | collective-permute-start | bytes 393224 | tf_op jit(solution)/shard_map/ppermute | solution.py:362
  48.3 6.2 %collective-permute-start.12 = (bf16[512,128]{1,0:T(8,128)(2,1)S(1)}, bf16[512,128]{1,0:T(8,128)(2,1)S(1)}, u32[]{:S(2)}, u32[]{:S(2)}) collective-permute-start(bf16[512,128]{1,0:T(8,128)(2,1)S(1)} %get-tuple-element.61), channel_id=1, source_target_pairs={{0,2},{1,3},{2,0},{3,1},{4,6},{5,7},{6,4},{7,5},{8,11},{9,10},{10,... | collective-permute-start | bytes 393224 | tf_op jit(solution)/shard_map/ppermute | solution.py:362
  50.5 3.5 %collective-permute-start.16 = (f32[16,128]{1,0:T(8,128)S(1)}, f32[16,128]{1,0:T(8,128)S(1)}, u32[]{:S(2)}, u32[]{:S(2)}) collective-permute-start(f32[16,128]{1,0:T(8,128)S(1)} %add_add_fusion.refs_8_), channel_id=1, source_target_pairs={{0,8},{8,0},{16,24},{24,16},{1,9},{9,1},{17,25},{25,17},{2,10},{10... | collective-permute-start | bytes 24584 | tf_op jit(solution)/shard_map/ppermute | solution.py:351

commit v5 on v4

--- a/solution.py
+++ b/solution.py
@@ -32,7 +32,7 @@
 
 
 STATE_ORDERS = (((0, 1, 2, 3), (0, 2, 1, 3)), ((0, 2, 1, 3), (0, 1, 2, 3)))
-GRAD_ORDERS = (((0, 3, 1, 2), (0, 3, 1, 2)), ((0, 1, 3, 2), (0, 1, 2, 3)))
+GRAD_ORDERS = (((0, 3, 1, 2), (0, 3, 1, 2)), ((0, 3, 2, 1), (0, 1, 2, 3)))
 NORM_ORDERS = (STATE_ORDERS[1], GRAD_ORDERS[0])
 
 

time: 55.8 us -> 55 us (0.986)
  waiting for transfers between devices: 19.2 us -> 18.5 us
    ppermute x12, waiting for transfers between devices: 10.8 us -> 10.1 us  [own_and_swapped(): results.append(lax.ppermute(pieces[slot], ('dp', 'seq'), pairs))]
where the time goes in v5:
time: 55 us; the launch traced here: 54.9 us
  starting transfers between devices  23 us (42%)
  waiting for transfers between devices  18.5 us (34%)
  Pallas kernels  12.6 us (23%)
  between operations  0.77 us (1%)
    ppermute x12, starting transfers between devices, own_and_swapped(): results.append(lax.ppermute(pieces[slot], ('dp', 'seq'), pairs))  15.5 us
    pallas_call x16, Pallas kernels, call(): pl.pallas_call(kernel, out_shape=tuple(outs), in_specs=[ins.get(i, VMEM)...  12.6 us
    ppermute x12, waiting for transfers between devices, own_and_swapped(): results.append(lax.ppermute(pieces[slot], ('dp', 'seq'), pairs))  10.1 us
    ppermute x2, waiting for transfers between devices, shifted(): return lax.ppermute(array, 'seq', pairs)  8.4 us
    ppermute x2, starting transfers between devices, shifted(): return lax.ppermute(array, 'seq', pairs)  4.74 us
    ppermute x2, starting transfers between devices, exclusive_scan(): gains.append(lax.ppermute(gains[0], ('dp', 'seq'), pairs))  2.66 us
  transfers between devices with their start and end apart: 17, of which 11 were waited for; matrix products, arithmetic and copies ran while one was open for 0% of the time, Pallas kernels for 16%

profile of v5, /device:TPU:0, one launch (start us, length us, event | category | flops | bytes accessed | tf_op | source)
XLA Modules:
  0.0 54.9 jit_solution(9973925969035622069)
XLA Ops:
  0.7 1.3 %shard_map.93.token_ref = bf16[512,128]{1,0:T(8,128)(2,1)S(1)} custom-call(bf16[128,2048]{1,0:T(8,128)(2,1)} %bitcast.10, bf16[128,2048]{1,0:T(8,128)(2,1)} %bitcast.16), custom_call_target="tpu_custom_call" | custom-call | flops 67108864 | bytes 1179648 | tf_op jit(solution)/shard_map/pallas_call | solution.py:333
  2.0 3.0 %collective-permute-start = (bf16[512,128]{1,0:T(8,128)(2,1)S(1)}, bf16[512,128]{1,0:T(8,128)(2,1)S(1)}, u32[]{:S(2)}, u32[]{:S(2)}) collective-permute-start(bf16[512,128]{1,0:T(8,128)(2,1)S(1)} %shard_map.93.token_ref), channel_id=1, source_target_pairs={{0,1},{1,0},{2,3},{3,2},{4,5},{5,4},{6,7},{7,6},{8,10},{9,11},{10,... | collective-permute-start | bytes 393224 | tf_op jit(solution)/shard_map/ppermute | solution.py:362
  5.0 0.4 shard_map.94
  5.4 1.6 %collective-permute-start.1 = (bf16[512,128]{1,0:T(8,128)(2,1)S(1)}, bf16[512,128]{1,0:T(8,128)(2,1)S(1)}, u32[]{:S(2)}, u32[]{:S(2)}) collective-permute-start(bf16[512,128]{1,0:T(8,128)(2,1)S(1)} %get-tuple-element.40), channel_id=1, source_target_pairs={{0,2},{1,3},{2,0},{3,1},{4,6},{5,7},{6,4},{7,5},{8,9},{9,8},{10,11... | collective-permute-start | bytes 393224 | tf_op jit(solution)/shard_map/ppermute | solution.py:362
  7.1 2.6 %shard_map.92 = (bf16[2048,128]{1,0:T(8,128)(2,1)S(1)}, f32[128,2048]{1,0:T(8,128)S(1)}) custom-call(bf16[128,2048]{1,0:T(8,128)(2,1)S(1)} %bitcast.22, bf16[128,2048]{1,0:T(8,128)(2,1)S(1)} %bitcast.12, bf16[128,2048]{1,0:T(8,128)(2,1)S(1)} %bitcast.18), custom_call_target="tpu_custom_call" | custom-call | flops 134217728 | bytes 3145728 | tf_op jit(solution)/shard_map/pallas_call | solution.py:333
  9.7 2.0 %collective-permute-done.1.refs_2_.refs_3_ = bf16[512,128]{1,0:T(8,128)(2,1)S(1)} collective-permute-done((bf16[512,128]{1,0:T(8,128)(2,1)S(1)}, bf16[512,128]{1,0:T(8,128)(2,1)S(1)}, u32[]{:S(2)}, u32[]{:S(2)}) %collective-permute-start.1) | collective-permute-done | bytes 131104 | tf_op jit(solution)/shard_map/ppermute | solution.py:362
  11.7 1.2 %collective-permute-done.2.refs_3_.refs_4_ = bf16[512,128]{1,0:T(8,128)(2,1)S(1)} collective-permute-done((bf16[512,128]{1,0:T(8,128)(2,1)S(1)}, bf16[512,128]{1,0:T(8,128)(2,1)S(1)}, u32[]{:S(2)}, u32[]{:S(2)}) %collective-permute-start.2) | collective-permute-done | bytes 131104 | tf_op jit(solution)/shard_map/ppermute | solution.py:362
  12.9 3.0 %collective-permute-start.3 = (bf16[512,128]{1,0:T(8,128)(2,1)S(1)}, bf16[512,128]{1,0:T(8,128)(2,1)S(1)}, u32[]{:S(2)}, u32[]{:S(2)}) collective-permute-start(bf16[512,128]{1,0:T(8,128)(2,1)S(1)} %shard_map.95), channel_id=1, source_target_pairs={{0,4},{1,5},{2,6},{3,7},{4,0},{5,1},{6,2},{7,3},{8,12},{9,13},{10,... | collective-permute-start | bytes 393224 | tf_op jit(solution)/shard_map/ppermute | solution.py:379
  15.9 5.3 %collective-permute-done.3.refs_0_ = bf16[512,128]{1,0:T(8,128)(2,1)S(1)} collective-permute-done((bf16[512,128]{1,0:T(8,128)(2,1)S(1)}, bf16[512,128]{1,0:T(8,128)(2,1)S(1)}, u32[]{:S(2)}, u32[]{:S(2)}) %collective-permute-start.3) | collective-permute-done | bytes 131104 | tf_op jit(solution)/shard_map/ppermute | solution.py:379
  21.5 0.9 %collective-permute-start.5 = (bf16[512,128]{1,0:T(8,128)(2,1)S(1)}, bf16[512,128]{1,0:T(8,128)(2,1)S(1)}, u32[]{:S(2)}, u32[]{:S(2)}) collective-permute-start(bf16[512,128]{1,0:T(8,128)(2,1)S(1)} %shard_map.97.refs_5_), channel_id=1, source_target_pairs={{0,1},{1,0},{2,3},{3,2},{4,5},{5,4},{6,7},{7,6},{8,10},{9,11},{10,... | collective-permute-start | bytes 393224 | tf_op jit(solution)/shard_map/ppermute | solution.py:362
  22.4 0.2 shard_map.98
  22.7 2.7 %collective-permute-start.6 = (bf16[512,128]{1,0:T(8,128)(2,1)S(1)}, bf16[512,128]{1,0:T(8,128)(2,1)S(1)}, u32[]{:S(2)}, u32[]{:S(2)}) collective-permute-start(bf16[512,128]{1,0:T(8,128)(2,1)S(1)} %get-tuple-element.46), channel_id=1, source_target_pairs={{0,3},{1,2},{2,1},{3,0},{4,7},{5,6},{6,5},{7,4},{8,11},{9,10},{10,... | collective-permute-start | bytes 393224 | tf_op jit(solution)/shard_map/ppermute | solution.py:362
  25.4 2.7 %collective-permute-done.5.refs_6_.refs_11_ = bf16[512,128]{1,0:T(8,128)(2,1)S(1)} collective-permute-done((bf16[512,128]{1,0:T(8,128)(2,1)S(1)}, bf16[512,128]{1,0:T(8,128)(2,1)S(1)}, u32[]{:S(2)}, u32[]{:S(2)}) %collective-permute-start.5) | collective-permute-done | bytes 131104 | tf_op jit(solution)/shard_map/ppermute | solution.py:362
  28.1 0.4 shard_map.99
  28.6 0.9 %collective-permute-done.6.refs_7_.refs_12_ = bf16[512,128]{1,0:T(8,128)(2,1)S(1)} collective-permute-done((bf16[512,128]{1,0:T(8,128)(2,1)S(1)}, bf16[512,128]{1,0:T(8,128)(2,1)S(1)}, u32[]{:S(2)}, u32[]{:S(2)}) %collective-permute-start.6) | collective-permute-done | bytes 131104 | tf_op jit(solution)/shard_map/ppermute | solution.py:362
  29.5 1.0 %shard_map.100 = (f32[128,512]{1,0:T(8,128)S(1)}, f32[128,128]{1,0:T(8,128)S(1)}, bf16[128,2048]{1,0:T(8,128)(2,1)S(1)}, bf16[544,128]{1,0:T(8,128)(2,1)S(1)}, b...) custom-call(bf16[128,2048]{1,0:T(8,128)(2,1)S(1)} %bitcast.24, ...), custom_call_target="tpu_custom_call" | custom-call | flops 134217728 | bytes 4825088 | tf_op jit(solution)/shard_map/pallas_call | solution.py:333
  30.5 1.8 %collective-permute-start.7 = (bf16[544,128]{1,0:T(8,128)(2,1)S(1)}, bf16[544,128]{1,0:T(8,128)(2,1)S(1)}, u32[]{:S(2)}, u32[]{:S(2)}) collective-permute-start(bf16[544,128]{1,0:T(8,128)(2,1)S(1)} %get-tuple-element.55), channel_id=1, source_target_pairs={{0,3},{1,2},{2,1},{3,0},{4,7},{5,6},{6,5},{7,4},{8,11},{9,10},{10,... | collective-permute-start | bytes 417800 | tf_op jit(solution)/shard_map/ppermute | solution.py:362
  32.3 1.0 %collective-permute-start.8 = (bf16[544,128]{1,0:T(8,128)(2,1)S(1)}, bf16[544,128]{1,0:T(8,128)(2,1)S(1)}, u32[]{:S(2)}, u32[]{:S(2)}) collective-permute-start(bf16[544,128]{1,0:T(8,128)(2,1)S(1)} %get-tuple-element.56), channel_id=1, source_target_pairs={{0,1},{1,0},{2,3},{3,2},{4,5},{5,4},{6,7},{7,6},{8,9},{9,8},{10,11... | collective-permute-start | bytes 417800 | tf_op jit(solution)/shard_map/ppermute | solution.py:362
  33.3 0.7 %collective-permute-start.9 = (bf16[544,128]{1,0:T(8,128)(2,1)S(1)}, bf16[544,128]{1,0:T(8,128)(2,1)S(1)}, u32[]{:S(2)}, u32[]{:S(2)}) collective-permute-start(bf16[544,128]{1,0:T(8,128)(2,1)S(1)} %get-tuple-element.57), channel_id=1, source_target_pairs={{0,2},{1,3},{2,0},{3,1},{4,6},{5,7},{6,4},{7,5},{8,10},{9,11},{10,... | collective-permute-start | bytes 417800 | tf_op jit(solution)/shard_map/ppermute | solution.py:362
  34.1 3.5 %shard_map.101 = (bf16[128,2048]{1,0:T(8,128)(2,1)}, bf16[128,2048]{1,0:T(8,128)(2,1)}, f32[128,2048]{1,0:T(8,128)S(1)}, f32[128,2048]{1,0:T(8,128)S(1)}, f32[8,128]{1,0:T(8,128)S(1)}) custom-call(bf16[128,2048]{1,0:T(8,128)(2,1)S(1)} %bitcast.25, bf16[128,2048]{1,0:T(8,128)(2,1)S(1)} %bitcast.13, bf16[128,2048]{1,0:T(8,128)(2,1)S(1)} %bitcast.19, ...), custom_call_target="tpu_custom_call" | custom-call | flops 335544320 | bytes 7680000 | tf_op jit(solution)/shard_map/pallas_call | solution.py:333
  37.6 0.9 %collective-permute-done.8.refs_2_.refs_3_ = bf16[544,128]{1,0:T(8,128)(2,1)S(1)} collective-permute-done((bf16[544,128]{1,0:T(8,128)(2,1)S(1)}, bf16[544,128]{1,0:T(8,128)(2,1)S(1)}, u32[]{:S(2)}, u32[]{:S(2)}) %collective-permute-start.8) | collective-permute-done | bytes 139296 | tf_op jit(solution)/shard_map/ppermute | solution.py:362
  38.8 1.8 %collective-permute-start.10 = (bf16[544,128]{1,0:T(8,128)(2,1)S(1)}, bf16[544,128]{1,0:T(8,128)(2,1)S(1)}, u32[]{:S(2)}, u32[]{:S(2)}) collective-permute-start(bf16[544,128]{1,0:T(8,128)(2,1)S(1)} %get-tuple-element.59), channel_id=1, source_target_pairs={{0,4},{1,5},{2,6},{3,7},{4,0},{5,1},{6,2},{7,3},{8,12},{9,13},{10,... | collective-permute-start | bytes 417800 | tf_op jit(solution)/shard_map/ppermute | solution.py:379
  40.6 2.0 %collective-permute-start.15 = (f32[16,128]{1,0:T(8,128)S(1)}, f32[16,128]{1,0:T(8,128)S(1)}, u32[]{:S(2)}, u32[]{:S(2)}) collective-permute-start(f32[16,128]{1,0:T(8,128)S(1)} %get-tuple-element.60.refs_5_), channel_id=1, source_target_pairs={{0,20},{1,21},{2,22},{3,23},{4,16},{5,17},{6,18},{7,19},{8,28},{9,... | collective-permute-start | bytes 24584 | tf_op jit(solution)/shard_map/ppermute | solution.py:399
  42.6 0.7 %collective-permute-start.14 = (f32[16,128]{1,0:T(8,128)S(1)}, f32[16,128]{1,0:T(8,128)S(1)}, u32[]{:S(2)}, u32[]{:S(2)}) collective-permute-start(f32[16,128]{1,0:T(8,128)S(1)} %get-tuple-element.60.refs_5_), channel_id=1, source_target_pairs={{0,16},{1,17},{2,18},{3,19},{4,20},{5,21},{6,22},{7,23},{8,24},{9,... | collective-permute-start | bytes 24584 | tf_op jit(solution)/shard_map/ppermute | solution.py:399
  43.2 3.1 %collective-permute-done.10.refs_0_ = bf16[544,128]{1,0:T(8,128)(2,1)S(1)} collective-permute-done((bf16[544,128]{1,0:T(8,128)(2,1)S(1)}, bf16[544,128]{1,0:T(8,128)(2,1)S(1)}, u32[]{:S(2)}, u32[]{:S(2)}) %collective-permute-start.10) | collective-permute-done | bytes 139296 | tf_op jit(solution)/shard_map/ppermute | solution.py:379
  46.5 1.2 %collective-permute-start.13 = (bf16[512,128]{1,0:T(8,128)(2,1)S(1)}, bf16[512,128]{1,0:T(8,128)(2,1)S(1)}, u32[]{:S(2)}, u32[]{:S(2)}) collective-permute-start(bf16[512,128]{1,0:T(8,128)(2,1)S(1)} %shard_map.103.refs_5_), channel_id=1, source_target_pairs={{0,3},{1,2},{2,1},{3,0},{4,7},{5,6},{6,5},{7,4},{8,9},{9,8},{10,11... | collective-permute-start | bytes 393224 | tf_op jit(solution)/shard_map/ppermute | solution.py:362
  47.9 0.3 shard_map.105
  48.1 2.4 %collective-permute-start.12 = (bf16[512,128]{1,0:T(8,128)(2,1)S(1)}, bf16[512,128]{1,0:T(8,128)(2,1)S(1)}, u32[]{:S(2)}, u32[]{:S(2)}) collective-permute-start(bf16[512,128]{1,0:T(8,128)(2,1)S(1)} %get-tuple-element.61), channel_id=1, source_target_pairs={{0,1},{1,0},{2,3},{3,2},{4,5},{5,4},{6,7},{7,6},{8,11},{9,10},{10,... | collective-permute-start | bytes 393224 | tf_op jit(solution)/shard_map/ppermute | solution.py:362
  50.6 1.8 %collective-permute-done.13.refs_5_ = bf16[512,128]{1,0:T(8,128)(2,1)S(1)} collective-permute-done((bf16[512,128]{1,0:T(8,128)(2,1)S(1)}, bf16[512,128]{1,0:T(8,128)(2,1)S(1)}, u32[]{:S(2)}, u32[]{:S(2)}) %collective-permute-start.13) | collective-permute-done | bytes 131104 | tf_op jit(solution)/shard_map/ppermute | solution.py:362
  52.4 1.1 %shard_map.106 = (bf16[128,2048]{1,0:T(8,128)(2,1)}, bf16[128,2048]{1,0:T(8,128)(2,1)}) custom-call(bf16[128,2048]{1,0:T(8,128)(2,1)S(1)} %bitcast.14, bf16[128,2048]{1,0:T(8,128)(2,1)S(1)} %bitcast.20, f32[128,2048]{1,0:T(8,128)S(1)} %get-tuple-element.52.refs_2_, f32[128,2048]{1,0:T(8,128)S(1)} %get-tuple-element.53.refs_3_, ...), custom_call_target="tpu_custom_call" | custom-call | flops 67108864 | bytes 4456448 | tf_op jit(solution)/shard_map/pallas_call | solution.py:333
  53.5 0.3 collective-permute-done.12.refs_5_
  53.8 1.1 %shard_map.107 = (bf16[128,2048]{1,0:T(8,128)(2,1)}, bf16[128,2048]{1,0:T(8,128)(2,1)}, f32[16,128]{1,0:T(8,128)}) custom-call(bf16[128,2048]{1,0:T(8,128)(2,1)S(1)} %bitcast.15, bf16[128,2048]{1,0:T(8,128)(2,1)S(1)} %bitcast.21, f32[128,2048]{1,0:T(8,128)S(1)} %get-tuple-element.52.refs_2_, ...), custom_call_target="tpu_custom_call", output_to_operand_aliasing={{0}: (6, {}), {1}: (7, {})} | custom-call | flops 67108864 | bytes 5529600 | tf_op jit(solution)/shard_map/pallas_call | solution.py:333
  (29 shorter events, 1.3 us)
Async XLA Ops:
  0.6 4.3 %copy-start = (bf16[1,128,2048]{2,1,0:T(8,128)(2,1)S(1)}, bf16[1,128,2048]{2,1,0:T(8,128)(2,1)}, u32[]{:S(2)}) copy-start(bf16[1,128,2048]{2,1,0:T(8,128)(2,1)} %param.6) | copy-start | bytes 1572868
  0.6 4.3 %copy-start.1 = (bf16[1,128,2048]{2,1,0:T(8,128)(2,1)S(1)}, bf16[1,128,2048]{2,1,0:T(8,128)(2,1)}, u32[]{:S(2)}) copy-start(bf16[1,128,2048]{2,1,0:T(8,128)(2,1)} %param.7) | copy-start | bytes 1572868
  2.0 5.1 %copy-start.2 = (bf16[1,128,2048]{2,1,0:T(8,128)(2,1)S(1)}, bf16[1,128,2048]{2,1,0:T(8,128)(2,1)}, u32[]{:S(2)}) copy-start(bf16[1,128,2048]{2,1,0:T(8,128)(2,1)} %param.5) | copy-start | bytes 1572868
  2.0 7.7 %collective-permute-start = (bf16[512,128]{1,0:T(8,128)(2,1)S(1)}, bf16[512,128]{1,0:T(8,128)(2,1)S(1)}, u32[]{:S(2)}, u32[]{:S(2)}) collective-permute-start(bf16[512,128]{1,0:T(8,128)(2,1)S(1)} %shard_map.93.token_ref), channel_id=1, source_target_pairs={{0,1},{1,0},{2,3},{3,2},{4,5},{5,4},{6,7},{7,6},{8,10},{9,11},{10,... | collective-permute-start | bytes 393224 | tf_op jit(solution)/shard_map/ppermute | solution.py:362
  5.4 6.3 %collective-permute-start.1 = (bf16[512,128]{1,0:T(8,128)(2,1)S(1)}, bf16[512,128]{1,0:T(8,128)(2,1)S(1)}, u32[]{:S(2)}, u32[]{:S(2)}) collective-permute-start(bf16[512,128]{1,0:T(8,128)(2,1)S(1)} %get-tuple-element.40), channel_id=1, source_target_pairs={{0,2},{1,3},{2,0},{3,1},{4,6},{5,7},{6,4},{7,5},{8,9},{9,8},{10,11... | collective-permute-start | bytes 393224 | tf_op jit(solution)/shard_map/ppermute | solution.py:362
  7.0 5.9 %collective-permute-start.2 = (bf16[512,128]{1,0:T(8,128)(2,1)S(1)}, bf16[512,128]{1,0:T(8,128)(2,1)S(1)}, u32[]{:S(2)}, u32[]{:S(2)}) collective-permute-start(bf16[512,128]{1,0:T(8,128)(2,1)S(1)} %get-tuple-element.41), channel_id=1, source_target_pairs={{0,3},{1,2},{2,1},{3,0},{4,7},{5,6},{6,5},{7,4},{8,11},{9,10},{10,... | collective-permute-start | bytes 393224 | tf_op jit(solution)/shard_map/ppermute | solution.py:362
  12.9 8.3 %collective-permute-start.3 = (bf16[512,128]{1,0:T(8,128)(2,1)S(1)}, bf16[512,128]{1,0:T(8,128)(2,1)S(1)}, u32[]{:S(2)}, u32[]{:S(2)}) collective-permute-start(bf16[512,128]{1,0:T(8,128)(2,1)S(1)} %shard_map.95), channel_id=1, source_target_pairs={{0,4},{1,5},{2,6},{3,7},{4,0},{5,1},{6,2},{7,3},{8,12},{9,13},{10,... | collective-permute-start | bytes 393224 | tf_op jit(solution)/shard_map/ppermute | solution.py:379
  21.5 6.6 %copy-start.3 = (bf16[1,128,2048]{2,1,0:T(8,128)(2,1)S(1)}, bf16[1,128,2048]{2,1,0:T(8,128)(2,1)}, u32[]{:S(2)}) copy-start(bf16[1,128,2048]{2,1,0:T(8,128)(2,1)} %param.9) | copy-start | bytes 1572868
  21.5 6.5 %collective-permute-start.5 = (bf16[512,128]{1,0:T(8,128)(2,1)S(1)}, bf16[512,128]{1,0:T(8,128)(2,1)S(1)}, u32[]{:S(2)}, u32[]{:S(2)}) collective-permute-start(bf16[512,128]{1,0:T(8,128)(2,1)S(1)} %shard_map.97.refs_5_), channel_id=1, source_target_pairs={{0,1},{1,0},{2,3},{3,2},{4,5},{5,4},{6,7},{7,6},{8,10},{9,11},{10,... | collective-permute-start | bytes 393224 | tf_op jit(solution)/shard_map/ppermute | solution.py:362
  22.4 5.7 %collective-permute-start.4 = (bf16[512,128]{1,0:T(8,128)(2,1)S(1)}, bf16[512,128]{1,0:T(8,128)(2,1)S(1)}, u32[]{:S(2)}, u32[]{:S(2)}) collective-permute-start(bf16[512,128]{1,0:T(8,128)(2,1)S(1)} %shard_map.96.refs_5_), channel_id=1, source_target_pairs={{0,2},{1,3},{2,0},{3,1},{4,6},{5,7},{6,4},{7,5},{8,9},{9,8},{10,11... | collective-permute-start | bytes 393224 | tf_op jit(solution)/shard_map/ppermute | solution.py:362
  22.4 5.7 %copy-start.4 = (f32[2048]{0:T(1024)S(1)}, f32[2048]{0:T(1024)}, u32[]{:S(2)}) copy-start(f32[2048]{0:T(1024)} %param.8) | copy-start | bytes 24580
  22.7 6.9 %collective-permute-start.6 = (bf16[512,128]{1,0:T(8,128)(2,1)S(1)}, bf16[512,128]{1,0:T(8,128)(2,1)S(1)}, u32[]{:S(2)}, u32[]{:S(2)}) collective-permute-start(bf16[512,128]{1,0:T(8,128)(2,1)S(1)} %get-tuple-element.46), channel_id=1, source_target_pairs={{0,3},{1,2},{2,1},{3,0},{4,7},{5,6},{6,5},{7,4},{8,11},{9,10},{10,... | collective-permute-start | bytes 393224 | tf_op jit(solution)/shard_map/ppermute | solution.py:362
  30.5 7.0 %collective-permute-start.7 = (bf16[544,128]{1,0:T(8,128)(2,1)S(1)}, bf16[544,128]{1,0:T(8,128)(2,1)S(1)}, u32[]{:S(2)}, u32[]{:S(2)}) collective-permute-start(bf16[544,128]{1,0:T(8,128)(2,1)S(1)} %get-tuple-element.55), channel_id=1, source_target_pairs={{0,3},{1,2},{2,1},{3,0},{4,7},{5,6},{6,5},{7,4},{8,11},{9,10},{10,... | collective-permute-start | bytes 417800 | tf_op jit(solution)/shard_map/ppermute | solution.py:362
  32.3 6.1 %collective-permute-start.8 = (bf16[544,128]{1,0:T(8,128)(2,1)S(1)}, bf16[544,128]{1,0:T(8,128)(2,1)S(1)}, u32[]{:S(2)}, u32[]{:S(2)}) collective-permute-start(bf16[544,128]{1,0:T(8,128)(2,1)S(1)} %get-tuple-element.56), channel_id=1, source_target_pairs={{0,1},{1,0},{2,3},{3,2},{4,5},{5,4},{6,7},{7,6},{8,9},{9,8},{10,11... | collective-permute-start | bytes 417800 | tf_op jit(solution)/shard_map/ppermute | solution.py:362
  33.3 5.3 %collective-permute-start.9 = (bf16[544,128]{1,0:T(8,128)(2,1)S(1)}, bf16[544,128]{1,0:T(8,128)(2,1)S(1)}, u32[]{:S(2)}, u32[]{:S(2)}) collective-permute-start(bf16[544,128]{1,0:T(8,128)(2,1)S(1)} %get-tuple-element.57), channel_id=1, source_target_pairs={{0,2},{1,3},{2,0},{3,1},{4,6},{5,7},{6,4},{7,5},{8,10},{9,11},{10,... | collective-permute-start | bytes 417800 | tf_op jit(solution)/shard_map/ppermute | solution.py:362
  38.8 7.5 %collective-permute-start.10 = (bf16[544,128]{1,0:T(8,128)(2,1)S(1)}, bf16[544,128]{1,0:T(8,128)(2,1)S(1)}, u32[]{:S(2)}, u32[]{:S(2)}) collective-permute-start(bf16[544,128]{1,0:T(8,128)(2,1)S(1)} %get-tuple-element.59), channel_id=1, source_target_pairs={{0,4},{1,5},{2,6},{3,7},{4,0},{5,1},{6,2},{7,3},{8,12},{9,13},{10,... | collective-permute-start | bytes 417800 | tf_op jit(solution)/shard_map/ppermute | solution.py:379
  40.6 10.0 %collective-permute-start.15 = (f32[16,128]{1,0:T(8,128)S(1)}, f32[16,128]{1,0:T(8,128)S(1)}, u32[]{:S(2)}, u32[]{:S(2)}) collective-permute-start(f32[16,128]{1,0:T(8,128)S(1)} %get-tuple-element.60.refs_5_), channel_id=1, source_target_pairs={{0,20},{1,21},{2,22},{3,23},{4,16},{5,17},{6,18},{7,19},{8,28},{9,... | collective-permute-start | bytes 24584 | tf_op jit(solution)/shard_map/ppermute | solution.py:399
  42.6 8.0 %collective-permute-start.14 = (f32[16,128]{1,0:T(8,128)S(1)}, f32[16,128]{1,0:T(8,128)S(1)}, u32[]{:S(2)}, u32[]{:S(2)}) collective-permute-start(f32[16,128]{1,0:T(8,128)S(1)} %get-tuple-element.60.refs_5_), channel_id=1, source_target_pairs={{0,16},{1,17},{2,18},{3,19},{4,20},{5,21},{6,22},{7,23},{8,24},{9,... | collective-permute-start | bytes 24584 | tf_op jit(solution)/shard_map/ppermute | solution.py:399
  46.5 6.0 %collective-permute-start.13 = (bf16[512,128]{1,0:T(8,128)(2,1)S(1)}, bf16[512,128]{1,0:T(8,128)(2,1)S(1)}, u32[]{:S(2)}, u32[]{:S(2)}) collective-permute-start(bf16[512,128]{1,0:T(8,128)(2,1)S(1)} %shard_map.103.refs_5_), channel_id=1, source_target_pairs={{0,3},{1,2},{2,1},{3,0},{4,7},{5,6},{6,5},{7,4},{8,9},{9,8},{10,11... | collective-permute-start | bytes 393224 | tf_op jit(solution)/shard_map/ppermute | solution.py:362
  47.8 6.0 %collective-permute-start.11 = (bf16[512,128]{1,0:T(8,128)(2,1)S(1)}, bf16[512,128]{1,0:T(8,128)(2,1)S(1)}, u32[]{:S(2)}, u32[]{:S(2)}) collective-permute-start(bf16[512,128]{1,0:T(8,128)(2,1)S(1)} %shard_map.104.refs_6_), channel_id=1, source_target_pairs={{0,2},{1,3},{2,0},{3,1},{4,6},{5,7},{6,4},{7,5},{8,10},{9,11},{10,... | collective-permute-start | bytes 393224 | tf_op jit(solution)/shard_map/ppermute | solution.py:362
  48.1 5.7 %collective-permute-start.12 = (bf16[512,128]{1,0:T(8,128)(2,1)S(1)}, bf16[512,128]{1,0:T(8,128)(2,1)S(1)}, u32[]{:S(2)}, u32[]{:S(2)}) collective-permute-start(bf16[512,128]{1,0:T(8,128)(2,1)S(1)} %get-tuple-element.61), channel_id=1, source_target_pairs={{0,1},{1,0},{2,3},{3,2},{4,5},{5,4},{6,7},{7,6},{8,11},{9,10},{10,... | collective-permute-start | bytes 393224 | tf_op jit(solution)/shard_map/ppermute | solution.py:362
  50.5 3.0 %collective-permute-start.16 = (f32[16,128]{1,0:T(8,128)S(1)}, f32[16,128]{1,0:T(8,128)S(1)}, u32[]{:S(2)}, u32[]{:S(2)}) collective-permute-start(f32[16,128]{1,0:T(8,128)S(1)} %add_add_fusion.refs_8_), channel_id=1, source_target_pairs={{0,8},{8,0},{16,24},{24,16},{1,9},{9,1},{17,25},{25,17},{2,10},{10... | collective-permute-start | bytes 24584 | tf_op jit(solution)/shard_map/ppermute | solution.py:351

commit v6 on v3

--- a/solution.py
+++ b/solution.py
@@ -60,10 +60,16 @@
 def first_state_kernel(head, slot, k_ref, v_ref, piece_ref, k_buffer, v_buffer, arrived):
     width = piece_ref.shape[0]
     source = block_at(partner_of(STATE_ORDERS[0], slot), width)
-    copies = [
-        pltpu.make_async_copy(k_ref.at[:, source], k_buffer, arrived.at[0]),
-        pltpu.make_async_copy(v_ref.at[:, source], v_buffer, arrived.at[1]),
-    ]
+    step = k_buffer.shape[0] // arrived.shape[1]
+    copies = []
+    for i in range(arrived.shape[1]):
+        part = columns(i * step, step)
+        for n, (ref, buffer) in enumerate(((k_ref, k_buffer), (v_ref, v_buffer))):
+            copies.append(
+                pltpu.make_async_copy(
+                    ref.at[part, source], buffer.at[part, :], arrived.at[n, i]
+                )
+            )
     for copy in copies:
         copy.start()
     for copy in copies:
@@ -462,7 +468,7 @@
         [piece],
         [pltpu.with_memory_space_constraint(a, pltpu.HBM) for a in (k, v)],
         1,
-        [pltpu.VMEM((rows, width), HALF)] * 2 + [pltpu.SemaphoreType.DMA((2,))],
+        [pltpu.VMEM((rows, width), HALF)] * 2 + [pltpu.SemaphoreType.DMA((2, 2))],
         ins={0: HBM, 1: HBM},
     )
     slots = (2, 3, 0)

time: 55.1 us -> 55 us (level)
  no operation moved by 1% of the time
where the time goes in v6:
time: 55 us; the launch traced here: 54.9 us
  starting transfers between devices  23 us (42%)
  waiting for transfers between devices  18.4 us (33%)
  Pallas kernels  12.6 us (23%)
  between operations  0.77 us (1%)
    ppermute x12, starting transfers between devices, own_and_swapped(): results.append(lax.ppermute(pieces[slot], ('dp', 'seq'), pairs))  15.5 us
    pallas_call x16, Pallas kernels, call(): pl.pallas_call(kernel, out_shape=tuple(outs), in_specs=[ins.get(i, VMEM)...  12.6 us
    ppermute x12, waiting for transfers between devices, own_and_swapped(): results.append(lax.ppermute(pieces[slot], ('dp', 'seq'), pairs))  10 us
    ppermute x2, waiting for transfers between devices, shifted(): return lax.ppermute(array, 'seq', pairs)  8.39 us
    ppermute x2, starting transfers between devices, shifted(): return lax.ppermute(array, 'seq', pairs)  4.75 us
    ppermute x2, starting transfers between devices, exclusive_scan(): gains.append(lax.ppermute(gains[0], ('dp', 'seq'), pairs))  2.66 us
  transfers between devices with their start and end apart: 17, of which 11 were waited for; matrix products, arithmetic and copies ran while one was open for 0% of the time, Pallas kernels for 16%

profile of v6, /device:TPU:0, one launch (start us, length us, event | category | flops | bytes accessed | tf_op | source)
XLA Modules:
  0.0 54.9 jit_solution(273978717603798650)
XLA Ops:
  0.7 1.3 %shard_map.93.token_ref = bf16[512,128]{1,0:T(8,128)(2,1)S(1)} custom-call(bf16[128,2048]{1,0:T(8,128)(2,1)} %bitcast.10, bf16[128,2048]{1,0:T(8,128)(2,1)} %bitcast.16), custom_call_target="tpu_custom_call" | custom-call | flops 67108864 | bytes 1179648 | tf_op jit(solution)/shard_map/pallas_call | solution.py:339
  2.0 3.0 %collective-permute-start = (bf16[512,128]{1,0:T(8,128)(2,1)S(1)}, bf16[512,128]{1,0:T(8,128)(2,1)S(1)}, u32[]{:S(2)}, u32[]{:S(2)}) collective-permute-start(bf16[512,128]{1,0:T(8,128)(2,1)S(1)} %shard_map.93.token_ref), channel_id=1, source_target_pairs={{0,1},{1,0},{2,3},{3,2},{4,5},{5,4},{6,7},{7,6},{8,10},{9,11},{10,... | collective-permute-start | bytes 393224 | tf_op jit(solution)/shard_map/ppermute | solution.py:368
  5.0 0.4 shard_map.94
  5.3 1.6 %collective-permute-start.1 = (bf16[512,128]{1,0:T(8,128)(2,1)S(1)}, bf16[512,128]{1,0:T(8,128)(2,1)S(1)}, u32[]{:S(2)}, u32[]{:S(2)}) collective-permute-start(bf16[512,128]{1,0:T(8,128)(2,1)S(1)} %get-tuple-element.40), channel_id=1, source_target_pairs={{0,2},{1,3},{2,0},{3,1},{4,6},{5,7},{6,4},{7,5},{8,9},{9,8},{10,11... | collective-permute-start | bytes 393224 | tf_op jit(solution)/shard_map/ppermute | solution.py:368
  7.0 2.6 %shard_map.92 = (bf16[2048,128]{1,0:T(8,128)(2,1)S(1)}, f32[128,2048]{1,0:T(8,128)S(1)}) custom-call(bf16[128,2048]{1,0:T(8,128)(2,1)S(1)} %bitcast.22, bf16[128,2048]{1,0:T(8,128)(2,1)S(1)} %bitcast.12, bf16[128,2048]{1,0:T(8,128)(2,1)S(1)} %bitcast.18), custom_call_target="tpu_custom_call" | custom-call | flops 134217728 | bytes 3145728 | tf_op jit(solution)/shard_map/pallas_call | solution.py:339
  9.7 2.0 %collective-permute-done.1.refs_2_.refs_3_ = bf16[512,128]{1,0:T(8,128)(2,1)S(1)} collective-permute-done((bf16[512,128]{1,0:T(8,128)(2,1)S(1)}, bf16[512,128]{1,0:T(8,128)(2,1)S(1)}, u32[]{:S(2)}, u32[]{:S(2)}) %collective-permute-start.1) | collective-permute-done | bytes 131104 | tf_op jit(solution)/shard_map/ppermute | solution.py:368
  11.6 1.2 %collective-permute-done.2.refs_3_.refs_4_ = bf16[512,128]{1,0:T(8,128)(2,1)S(1)} collective-permute-done((bf16[512,128]{1,0:T(8,128)(2,1)S(1)}, bf16[512,128]{1,0:T(8,128)(2,1)S(1)}, u32[]{:S(2)}, u32[]{:S(2)}) %collective-permute-start.2) | collective-permute-done | bytes 131104 | tf_op jit(solution)/shard_map/ppermute | solution.py:368
  12.9 3.0 %collective-permute-start.3 = (bf16[512,128]{1,0:T(8,128)(2,1)S(1)}, bf16[512,128]{1,0:T(8,128)(2,1)S(1)}, u32[]{:S(2)}, u32[]{:S(2)}) collective-permute-start(bf16[512,128]{1,0:T(8,128)(2,1)S(1)} %shard_map.95), channel_id=1, source_target_pairs={{0,4},{1,5},{2,6},{3,7},{4,0},{5,1},{6,2},{7,3},{8,12},{9,13},{10,... | collective-permute-start | bytes 393224 | tf_op jit(solution)/shard_map/ppermute | solution.py:385
  15.9 5.3 %collective-permute-done.3.refs_0_ = bf16[512,128]{1,0:T(8,128)(2,1)S(1)} collective-permute-done((bf16[512,128]{1,0:T(8,128)(2,1)S(1)}, bf16[512,128]{1,0:T(8,128)(2,1)S(1)}, u32[]{:S(2)}, u32[]{:S(2)}) %collective-permute-start.3) | collective-permute-done | bytes 131104 | tf_op jit(solution)/shard_map/ppermute | solution.py:385
  21.5 0.9 %collective-permute-start.5 = (bf16[512,128]{1,0:T(8,128)(2,1)S(1)}, bf16[512,128]{1,0:T(8,128)(2,1)S(1)}, u32[]{:S(2)}, u32[]{:S(2)}) collective-permute-start(bf16[512,128]{1,0:T(8,128)(2,1)S(1)} %shard_map.97.refs_5_), channel_id=1, source_target_pairs={{0,1},{1,0},{2,3},{3,2},{4,5},{5,4},{6,7},{7,6},{8,10},{9,11},{10,... | collective-permute-start | bytes 393224 | tf_op jit(solution)/shard_map/ppermute | solution.py:368
  22.4 0.2 shard_map.98
  22.6 2.7 %collective-permute-start.6 = (bf16[512,128]{1,0:T(8,128)(2,1)S(1)}, bf16[512,128]{1,0:T(8,128)(2,1)S(1)}, u32[]{:S(2)}, u32[]{:S(2)}) collective-permute-start(bf16[512,128]{1,0:T(8,128)(2,1)S(1)} %get-tuple-element.46), channel_id=1, source_target_pairs={{0,3},{1,2},{2,1},{3,0},{4,7},{5,6},{6,5},{7,4},{8,11},{9,10},{10,... | collective-permute-start | bytes 393224 | tf_op jit(solution)/shard_map/ppermute | solution.py:368
  25.4 2.7 %collective-permute-done.5.refs_6_.refs_11_ = bf16[512,128]{1,0:T(8,128)(2,1)S(1)} collective-permute-done((bf16[512,128]{1,0:T(8,128)(2,1)S(1)}, bf16[512,128]{1,0:T(8,128)(2,1)S(1)}, u32[]{:S(2)}, u32[]{:S(2)}) %collective-permute-start.5) | collective-permute-done | bytes 131104 | tf_op jit(solution)/shard_map/ppermute | solution.py:368
  28.1 0.4 shard_map.99
  28.6 0.9 %collective-permute-done.6.refs_7_.refs_12_ = bf16[512,128]{1,0:T(8,128)(2,1)S(1)} collective-permute-done((bf16[512,128]{1,0:T(8,128)(2,1)S(1)}, bf16[512,128]{1,0:T(8,128)(2,1)S(1)}, u32[]{:S(2)}, u32[]{:S(2)}) %collective-permute-start.6) | collective-permute-done | bytes 131104 | tf_op jit(solution)/shard_map/ppermute | solution.py:368
  29.5 1.0 %shard_map.100 = (f32[128,512]{1,0:T(8,128)S(1)}, f32[128,128]{1,0:T(8,128)S(1)}, bf16[128,2048]{1,0:T(8,128)(2,1)S(1)}, bf16[544,128]{1,0:T(8,128)(2,1)S(1)}, b...) custom-call(bf16[128,2048]{1,0:T(8,128)(2,1)S(1)} %bitcast.24, ...), custom_call_target="tpu_custom_call" | custom-call | flops 134217728 | bytes 4825088 | tf_op jit(solution)/shard_map/pallas_call | solution.py:339
  30.5 1.8 %collective-permute-start.7 = (bf16[544,128]{1,0:T(8,128)(2,1)S(1)}, bf16[544,128]{1,0:T(8,128)(2,1)S(1)}, u32[]{:S(2)}, u32[]{:S(2)}) collective-permute-start(bf16[544,128]{1,0:T(8,128)(2,1)S(1)} %get-tuple-element.55), channel_id=1, source_target_pairs={{0,3},{1,2},{2,1},{3,0},{4,7},{5,6},{6,5},{7,4},{8,11},{9,10},{10,... | collective-permute-start | bytes 417800 | tf_op jit(solution)/shard_map/ppermute | solution.py:368
  32.3 1.0 %collective-permute-start.8 = (bf16[544,128]{1,0:T(8,128)(2,1)S(1)}, bf16[544,128]{1,0:T(8,128)(2,1)S(1)}, u32[]{:S(2)}, u32[]{:S(2)}) collective-permute-start(bf16[544,128]{1,0:T(8,128)(2,1)S(1)} %get-tuple-element.56), channel_id=1, source_target_pairs={{0,1},{1,0},{2,3},{3,2},{4,5},{5,4},{6,7},{7,6},{8,9},{9,8},{10,11... | collective-permute-start | bytes 417800 | tf_op jit(solution)/shard_map/ppermute | solution.py:368
  33.3 0.7 %collective-permute-start.9 = (bf16[544,128]{1,0:T(8,128)(2,1)S(1)}, bf16[544,128]{1,0:T(8,128)(2,1)S(1)}, u32[]{:S(2)}, u32[]{:S(2)}) collective-permute-start(bf16[544,128]{1,0:T(8,128)(2,1)S(1)} %get-tuple-element.57), channel_id=1, source_target_pairs={{0,2},{1,3},{2,0},{3,1},{4,6},{5,7},{6,4},{7,5},{8,10},{9,11},{10,... | collective-permute-start | bytes 417800 | tf_op jit(solution)/shard_map/ppermute | solution.py:368
  34.0 3.5 %shard_map.101 = (bf16[128,2048]{1,0:T(8,128)(2,1)}, bf16[128,2048]{1,0:T(8,128)(2,1)}, f32[128,2048]{1,0:T(8,128)S(1)}, f32[128,2048]{1,0:T(8,128)S(1)}, f32[8,128]{1,0:T(8,128)S(1)}) custom-call(bf16[128,2048]{1,0:T(8,128)(2,1)S(1)} %bitcast.25, bf16[128,2048]{1,0:T(8,128)(2,1)S(1)} %bitcast.13, bf16[128,2048]{1,0:T(8,128)(2,1)S(1)} %bitcast.19, ...), custom_call_target="tpu_custom_call" | custom-call | flops 335544320 | bytes 7680000 | tf_op jit(solution)/shard_map/pallas_call | solution.py:339
  37.5 0.9 %collective-permute-done.8.refs_2_.refs_3_ = bf16[544,128]{1,0:T(8,128)(2,1)S(1)} collective-permute-done((bf16[544,128]{1,0:T(8,128)(2,1)S(1)}, bf16[544,128]{1,0:T(8,128)(2,1)S(1)}, u32[]{:S(2)}, u32[]{:S(2)}) %collective-permute-start.8) | collective-permute-done | bytes 139296 | tf_op jit(solution)/shard_map/ppermute | solution.py:368
  38.8 1.8 %collective-permute-start.10 = (bf16[544,128]{1,0:T(8,128)(2,1)S(1)}, bf16[544,128]{1,0:T(8,128)(2,1)S(1)}, u32[]{:S(2)}, u32[]{:S(2)}) collective-permute-start(bf16[544,128]{1,0:T(8,128)(2,1)S(1)} %get-tuple-element.59), channel_id=1, source_target_pairs={{0,4},{1,5},{2,6},{3,7},{4,0},{5,1},{6,2},{7,3},{8,12},{9,13},{10,... | collective-permute-start | bytes 417800 | tf_op jit(solution)/shard_map/ppermute | solution.py:385
  40.5 2.1 %collective-permute-start.15 = (f32[16,128]{1,0:T(8,128)S(1)}, f32[16,128]{1,0:T(8,128)S(1)}, u32[]{:S(2)}, u32[]{:S(2)}) collective-permute-start(f32[16,128]{1,0:T(8,128)S(1)} %get-tuple-element.60.refs_5_), channel_id=1, source_target_pairs={{0,20},{1,21},{2,22},{3,23},{4,16},{5,17},{6,18},{7,19},{8,28},{9,... | collective-permute-start | bytes 24584 | tf_op jit(solution)/shard_map/ppermute | solution.py:405
  42.6 0.6 %collective-permute-start.14 = (f32[16,128]{1,0:T(8,128)S(1)}, f32[16,128]{1,0:T(8,128)S(1)}, u32[]{:S(2)}, u32[]{:S(2)}) collective-permute-start(f32[16,128]{1,0:T(8,128)S(1)} %get-tuple-element.60.refs_5_), channel_id=1, source_target_pairs={{0,16},{1,17},{2,18},{3,19},{4,20},{5,21},{6,22},{7,23},{8,24},{9,... | collective-permute-start | bytes 24584 | tf_op jit(solution)/shard_map/ppermute | solution.py:405
  43.2 3.1 %collective-permute-done.10.refs_0_ = bf16[544,128]{1,0:T(8,128)(2,1)S(1)} collective-permute-done((bf16[544,128]{1,0:T(8,128)(2,1)S(1)}, bf16[544,128]{1,0:T(8,128)(2,1)S(1)}, u32[]{:S(2)}, u32[]{:S(2)}) %collective-permute-start.10) | collective-permute-done | bytes 139296 | tf_op jit(solution)/shard_map/ppermute | solution.py:385
  46.4 1.2 %collective-permute-start.13 = (bf16[512,128]{1,0:T(8,128)(2,1)S(1)}, bf16[512,128]{1,0:T(8,128)(2,1)S(1)}, u32[]{:S(2)}, u32[]{:S(2)}) collective-permute-start(bf16[512,128]{1,0:T(8,128)(2,1)S(1)} %shard_map.103.refs_5_), channel_id=1, source_target_pairs={{0,3},{1,2},{2,1},{3,0},{4,7},{5,6},{6,5},{7,4},{8,9},{9,8},{10,11... | collective-permute-start | bytes 393224 | tf_op jit(solution)/shard_map/ppermute | solution.py:368
  47.8 0.3 collective-permute-start.11
  48.0 0.3 shard_map.105
  48.3 2.2 %collective-permute-start.12 = (bf16[512,128]{1,0:T(8,128)(2,1)S(1)}, bf16[512,128]{1,0:T(8,128)(2,1)S(1)}, u32[]{:S(2)}, u32[]{:S(2)}) collective-permute-start(bf16[512,128]{1,0:T(8,128)(2,1)S(1)} %get-tuple-element.61), channel_id=1, source_target_pairs={{0,2},{1,3},{2,0},{3,1},{4,6},{5,7},{6,4},{7,5},{8,11},{9,10},{10,... | collective-permute-start | bytes 393224 | tf_op jit(solution)/shard_map/ppermute | solution.py:368
  50.6 1.9 %collective-permute-done.13.refs_5_ = bf16[512,128]{1,0:T(8,128)(2,1)S(1)} collective-permute-done((bf16[512,128]{1,0:T(8,128)(2,1)S(1)}, bf16[512,128]{1,0:T(8,128)(2,1)S(1)}, u32[]{:S(2)}, u32[]{:S(2)}) %collective-permute-start.13) | collective-permute-done | bytes 131104 | tf_op jit(solution)/shard_map/ppermute | solution.py:368
  52.5 1.1 %shard_map.106 = (bf16[128,2048]{1,0:T(8,128)(2,1)}, bf16[128,2048]{1,0:T(8,128)(2,1)}) custom-call(bf16[128,2048]{1,0:T(8,128)(2,1)S(1)} %bitcast.14, bf16[128,2048]{1,0:T(8,128)(2,1)S(1)} %bitcast.20, f32[128,2048]{1,0:T(8,128)S(1)} %get-tuple-element.52.refs_2_, f32[128,2048]{1,0:T(8,128)S(1)} %get-tuple-element.53.refs_3_, ...), custom_call_target="tpu_custom_call" | custom-call | flops 67108864 | bytes 4456448 | tf_op jit(solution)/shard_map/pallas_call | solution.py:339
  53.8 1.1 %shard_map.107 = (bf16[128,2048]{1,0:T(8,128)(2,1)}, bf16[128,2048]{1,0:T(8,128)(2,1)}, f32[16,128]{1,0:T(8,128)}) custom-call(bf16[128,2048]{1,0:T(8,128)(2,1)S(1)} %bitcast.15, bf16[128,2048]{1,0:T(8,128)(2,1)S(1)} %bitcast.21, f32[128,2048]{1,0:T(8,128)S(1)} %get-tuple-element.52.refs_2_, ...), custom_call_target="tpu_custom_call", output_to_operand_aliasing={{0}: (6, {}), {1}: (7, {})} | custom-call | flops 67108864 | bytes 5529600 | tf_op jit(solution)/shard_map/pallas_call | solution.py:339
  (29 shorter events, 1.4 us)
Async XLA Ops:
  0.6 4.3 %copy-start = (bf16[1,128,2048]{2,1,0:T(8,128)(2,1)S(1)}, bf16[1,128,2048]{2,1,0:T(8,128)(2,1)}, u32[]{:S(2)}) copy-start(bf16[1,128,2048]{2,1,0:T(8,128)(2,1)} %param.6) | copy-start | bytes 1572868
  0.6 4.3 %copy-start.1 = (bf16[1,128,2048]{2,1,0:T(8,128)(2,1)S(1)}, bf16[1,128,2048]{2,1,0:T(8,128)(2,1)}, u32[]{:S(2)}) copy-start(bf16[1,128,2048]{2,1,0:T(8,128)(2,1)} %param.7) | copy-start | bytes 1572868
  1.9 5.1 %copy-start.2 = (bf16[1,128,2048]{2,1,0:T(8,128)(2,1)S(1)}, bf16[1,128,2048]{2,1,0:T(8,128)(2,1)}, u32[]{:S(2)}) copy-start(bf16[1,128,2048]{2,1,0:T(8,128)(2,1)} %param.5) | copy-start | bytes 1572868
  2.0 7.7 %collective-permute-start = (bf16[512,128]{1,0:T(8,128)(2,1)S(1)}, bf16[512,128]{1,0:T(8,128)(2,1)S(1)}, u32[]{:S(2)}, u32[]{:S(2)}) collective-permute-start(bf16[512,128]{1,0:T(8,128)(2,1)S(1)} %shard_map.93.token_ref), channel_id=1, source_target_pairs={{0,1},{1,0},{2,3},{3,2},{4,5},{5,4},{6,7},{7,6},{8,10},{9,11},{10,... | collective-permute-start | bytes 393224 | tf_op jit(solution)/shard_map/ppermute | solution.py:368
  5.3 6.3 %collective-permute-start.1 = (bf16[512,128]{1,0:T(8,128)(2,1)S(1)}, bf16[512,128]{1,0:T(8,128)(2,1)S(1)}, u32[]{:S(2)}, u32[]{:S(2)}) collective-permute-start(bf16[512,128]{1,0:T(8,128)(2,1)S(1)} %get-tuple-element.40), channel_id=1, source_target_pairs={{0,2},{1,3},{2,0},{3,1},{4,6},{5,7},{6,4},{7,5},{8,9},{9,8},{10,11... | collective-permute-start | bytes 393224 | tf_op jit(solution)/shard_map/ppermute | solution.py:368
  7.0 5.9 %collective-permute-start.2 = (bf16[512,128]{1,0:T(8,128)(2,1)S(1)}, bf16[512,128]{1,0:T(8,128)(2,1)S(1)}, u32[]{:S(2)}, u32[]{:S(2)}) collective-permute-start(bf16[512,128]{1,0:T(8,128)(2,1)S(1)} %get-tuple-element.41), channel_id=1, source_target_pairs={{0,3},{1,2},{2,1},{3,0},{4,7},{5,6},{6,5},{7,4},{8,11},{9,10},{10,... | collective-permute-start | bytes 393224 | tf_op jit(solution)/shard_map/ppermute | solution.py:368
  12.9 8.3 %collective-permute-start.3 = (bf16[512,128]{1,0:T(8,128)(2,1)S(1)}, bf16[512,128]{1,0:T(8,128)(2,1)S(1)}, u32[]{:S(2)}, u32[]{:S(2)}) collective-permute-start(bf16[512,128]{1,0:T(8,128)(2,1)S(1)} %shard_map.95), channel_id=1, source_target_pairs={{0,4},{1,5},{2,6},{3,7},{4,0},{5,1},{6,2},{7,3},{8,12},{9,13},{10,... | collective-permute-start | bytes 393224 | tf_op jit(solution)/shard_map/ppermute | solution.py:385
  21.5 6.6 %copy-start.3 = (bf16[1,128,2048]{2,1,0:T(8,128)(2,1)S(1)}, bf16[1,128,2048]{2,1,0:T(8,128)(2,1)}, u32[]{:S(2)}) copy-start(bf16[1,128,2048]{2,1,0:T(8,128)(2,1)} %param.9) | copy-start | bytes 1572868
  21.5 6.5 %collective-permute-start.5 = (bf16[512,128]{1,0:T(8,128)(2,1)S(1)}, bf16[512,128]{1,0:T(8,128)(2,1)S(1)}, u32[]{:S(2)}, u32[]{:S(2)}) collective-permute-start(bf16[512,128]{1,0:T(8,128)(2,1)S(1)} %shard_map.97.refs_5_), channel_id=1, source_target_pairs={{0,1},{1,0},{2,3},{3,2},{4,5},{5,4},{6,7},{7,6},{8,10},{9,11},{10,... | collective-permute-start | bytes 393224 | tf_op jit(solution)/shard_map/ppermute | solution.py:368
  22.4 5.7 %collective-permute-start.4 = (bf16[512,128]{1,0:T(8,128)(2,1)S(1)}, bf16[512,128]{1,0:T(8,128)(2,1)S(1)}, u32[]{:S(2)}, u32[]{:S(2)}) collective-permute-start(bf16[512,128]{1,0:T(8,128)(2,1)S(1)} %shard_map.96.refs_5_), channel_id=1, source_target_pairs={{0,2},{1,3},{2,0},{3,1},{4,6},{5,7},{6,4},{7,5},{8,9},{9,8},{10,11... | collective-permute-start | bytes 393224 | tf_op jit(solution)/shard_map/ppermute | solution.py:368
  22.4 5.7 %copy-start.4 = (f32[2048]{0:T(1024)S(1)}, f32[2048]{0:T(1024)}, u32[]{:S(2)}) copy-start(f32[2048]{0:T(1024)} %param.8) | copy-start | bytes 24580
  22.6 6.9 %collective-permute-start.6 = (bf16[512,128]{1,0:T(8,128)(2,1)S(1)}, bf16[512,128]{1,0:T(8,128)(2,1)S(1)}, u32[]{:S(2)}, u32[]{:S(2)}) collective-permute-start(bf16[512,128]{1,0:T(8,128)(2,1)S(1)} %get-tuple-element.46), channel_id=1, source_target_pairs={{0,3},{1,2},{2,1},{3,0},{4,7},{5,6},{6,5},{7,4},{8,11},{9,10},{10,... | collective-permute-start | bytes 393224 | tf_op jit(solution)/shard_map/ppermute | solution.py:368
  30.5 7.0 %collective-permute-start.7 = (bf16[544,128]{1,0:T(8,128)(2,1)S(1)}, bf16[544,128]{1,0:T(8,128)(2,1)S(1)}, u32[]{:S(2)}, u32[]{:S(2)}) collective-permute-start(bf16[544,128]{1,0:T(8,128)(2,1)S(1)} %get-tuple-element.55), channel_id=1, source_target_pairs={{0,3},{1,2},{2,1},{3,0},{4,7},{5,6},{6,5},{7,4},{8,11},{9,10},{10,... | collective-permute-start | bytes 417800 | tf_op jit(solution)/shard_map/ppermute | solution.py:368
  32.3 6.1 %collective-permute-start.8 = (bf16[544,128]{1,0:T(8,128)(2,1)S(1)}, bf16[544,128]{1,0:T(8,128)(2,1)S(1)}, u32[]{:S(2)}, u32[]{:S(2)}) collective-permute-start(bf16[544,128]{1,0:T(8,128)(2,1)S(1)} %get-tuple-element.56), channel_id=1, source_target_pairs={{0,1},{1,0},{2,3},{3,2},{4,5},{5,4},{6,7},{7,6},{8,9},{9,8},{10,11... | collective-permute-start | bytes 417800 | tf_op jit(solution)/shard_map/ppermute | solution.py:368
  33.3 5.3 %collective-permute-start.9 = (bf16[544,128]{1,0:T(8,128)(2,1)S(1)}, bf16[544,128]{1,0:T(8,128)(2,1)S(1)}, u32[]{:S(2)}, u32[]{:S(2)}) collective-permute-start(bf16[544,128]{1,0:T(8,128)(2,1)S(1)} %get-tuple-element.57), channel_id=1, source_target_pairs={{0,2},{1,3},{2,0},{3,1},{4,6},{5,7},{6,4},{7,5},{8,10},{9,11},{10,... | collective-permute-start | bytes 417800 | tf_op jit(solution)/shard_map/ppermute | solution.py:368
  38.8 7.5 %collective-permute-start.10 = (bf16[544,128]{1,0:T(8,128)(2,1)S(1)}, bf16[544,128]{1,0:T(8,128)(2,1)S(1)}, u32[]{:S(2)}, u32[]{:S(2)}) collective-permute-start(bf16[544,128]{1,0:T(8,128)(2,1)S(1)} %get-tuple-element.59), channel_id=1, source_target_pairs={{0,4},{1,5},{2,6},{3,7},{4,0},{5,1},{6,2},{7,3},{8,12},{9,13},{10,... | collective-permute-start | bytes 417800 | tf_op jit(solution)/shard_map/ppermute | solution.py:385
  40.5 10.0 %collective-permute-start.15 = (f32[16,128]{1,0:T(8,128)S(1)}, f32[16,128]{1,0:T(8,128)S(1)}, u32[]{:S(2)}, u32[]{:S(2)}) collective-permute-start(f32[16,128]{1,0:T(8,128)S(1)} %get-tuple-element.60.refs_5_), channel_id=1, source_target_pairs={{0,20},{1,21},{2,22},{3,23},{4,16},{5,17},{6,18},{7,19},{8,28},{9,... | collective-permute-start | bytes 24584 | tf_op jit(solution)/shard_map/ppermute | solution.py:405
  42.6 7.9 %collective-permute-start.14 = (f32[16,128]{1,0:T(8,128)S(1)}, f32[16,128]{1,0:T(8,128)S(1)}, u32[]{:S(2)}, u32[]{:S(2)}) collective-permute-start(f32[16,128]{1,0:T(8,128)S(1)} %get-tuple-element.60.refs_5_), channel_id=1, source_target_pairs={{0,16},{1,17},{2,18},{3,19},{4,20},{5,21},{6,22},{7,23},{8,24},{9,... | collective-permute-start | bytes 24584 | tf_op jit(solution)/shard_map/ppermute | solution.py:405
  46.4 6.0 %collective-permute-start.13 = (bf16[512,128]{1,0:T(8,128)(2,1)S(1)}, bf16[512,128]{1,0:T(8,128)(2,1)S(1)}, u32[]{:S(2)}, u32[]{:S(2)}) collective-permute-start(bf16[512,128]{1,0:T(8,128)(2,1)S(1)} %shard_map.103.refs_5_), channel_id=1, source_target_pairs={{0,3},{1,2},{2,1},{3,0},{4,7},{5,6},{6,5},{7,4},{8,9},{9,8},{10,11... | collective-permute-start | bytes 393224 | tf_op jit(solution)/shard_map/ppermute | solution.py:368
  47.8 6.0 %collective-permute-start.11 = (bf16[512,128]{1,0:T(8,128)(2,1)S(1)}, bf16[512,128]{1,0:T(8,128)(2,1)S(1)}, u32[]{:S(2)}, u32[]{:S(2)}) collective-permute-start(bf16[512,128]{1,0:T(8,128)(2,1)S(1)} %shard_map.104.refs_6_), channel_id=1, source_target_pairs={{0,1},{1,0},{2,3},{3,2},{4,5},{5,4},{6,7},{7,6},{8,10},{9,11},{10,... | collective-permute-start | bytes 393224 | tf_op jit(solution)/shard_map/ppermute | solution.py:368
  48.3 5.3 %collective-permute-start.12 = (bf16[512,128]{1,0:T(8,128)(2,1)S(1)}, bf16[512,128]{1,0:T(8,128)(2,1)S(1)}, u32[]{:S(2)}, u32[]{:S(2)}) collective-permute-start(bf16[512,128]{1,0:T(8,128)(2,1)S(1)} %get-tuple-element.61), channel_id=1, source_target_pairs={{0,2},{1,3},{2,0},{3,1},{4,6},{5,7},{6,4},{7,5},{8,11},{9,10},{10,... | collective-permute-start | bytes 393224 | tf_op jit(solution)/shard_map/ppermute | solution.py:368
  50.5 3.0 %collective-permute-start.16 = (f32[16,128]{1,0:T(8,128)S(1)}, f32[16,128]{1,0:T(8,128)S(1)}, u32[]{:S(2)}, u32[]{:S(2)}) collective-permute-start(f32[16,128]{1,0:T(8,128)S(1)} %add_add_fusion.refs_8_), channel_id=1, source_target_pairs={{0,8},{8,0},{16,24},{24,16},{1,9},{9,1},{17,25},{25,17},{2,10},{10... | collective-permute-start | bytes 24584 | tf_op jit(solution)/shard_map/ppermute | solution.py:357

commit v7 on v3

--- a/solution.py
+++ b/solution.py
@@ -500,7 +500,7 @@
     gains = [gain_grad, swap(gain_grad, "dp", 1)]
     inputs = [k, v, key_part, value_part]
     outs = []
-    for slots in ((0, 1), (2, 3)):
+    for slots in ((0,), (1, 2, 3)):
         last = group - 1 in slots
         at = len(inputs) + len(slots)
         results = call(

time: 55.1 us -> 55.2 us (level)
  transfers between devices with their start and end apart: 17 -> 17, of which waited for: 11 -> 12; matrix products, arithmetic and copies ran while one was open for 0% -> 0% of each run, Pallas kernels for 16% -> 16%
where the time goes in v7:
time: 55.2 us; the launch traced here: 55.1 us
  starting transfers between devices  23 us (42%)
  waiting for transfers between devices  18.6 us (34%)
  Pallas kernels  12.7 us (23%)
  between operations  0.76 us (1%)
    ppermute x12, starting transfers between devices, own_and_swapped(): results.append(lax.ppermute(pieces[slot], ('dp', 'seq'), pairs))  15.5 us
    pallas_call x16, Pallas kernels, call(): pl.pallas_call(kernel, out_shape=tuple(outs), in_specs=[ins.get(i, VMEM)...  12.7 us
    ppermute x12, waiting for transfers between devices, own_and_swapped(): results.append(lax.ppermute(pieces[slot], ('dp', 'seq'), pairs))  10 us
    ppermute x2, waiting for transfers between devices, shifted(): return lax.ppermute(array, 'seq', pairs)  8.4 us
    ppermute x2, starting transfers between devices, shifted(): return lax.ppermute(array, 'seq', pairs)  4.74 us
    ppermute x2, starting transfers between devices, exclusive_scan(): gains.append(lax.ppermute(gains[0], ('dp', 'seq'), pairs))  2.66 us
  transfers between devices with their start and end apart: 17, of which 12 were waited for; matrix products, arithmetic and copies ran while one was open for 0% of the time, Pallas kernels for 16%

profile of v7, /device:TPU:0, one launch (start us, length us, event | category | flops | bytes accessed | tf_op | source)
XLA Modules:
  0.0 55.1 jit_solution(1523881654188184804)
XLA Ops:
  0.7 1.3 %shard_map.93.token_ref = bf16[512,128]{1,0:T(8,128)(2,1)S(1)} custom-call(bf16[128,2048]{1,0:T(8,128)(2,1)} %bitcast.10, bf16[128,2048]{1,0:T(8,128)(2,1)} %bitcast.16), custom_call_target="tpu_custom_call" | custom-call | flops 67108864 | bytes 1179648 | tf_op jit(solution)/shard_map/pallas_call | solution.py:333
  2.0 3.0 %collective-permute-start = (bf16[512,128]{1,0:T(8,128)(2,1)S(1)}, bf16[512,128]{1,0:T(8,128)(2,1)S(1)}, u32[]{:S(2)}, u32[]{:S(2)}) collective-permute-start(bf16[512,128]{1,0:T(8,128)(2,1)S(1)} %shard_map.93.token_ref), channel_id=1, source_target_pairs={{0,1},{1,0},{2,3},{3,2},{4,5},{5,4},{6,7},{7,6},{8,10},{9,11},{10,... | collective-permute-start | bytes 393224 | tf_op jit(solution)/shard_map/ppermute | solution.py:362
  5.0 0.4 shard_map.94
  5.4 1.6 %collective-permute-start.1 = (bf16[512,128]{1,0:T(8,128)(2,1)S(1)}, bf16[512,128]{1,0:T(8,128)(2,1)S(1)}, u32[]{:S(2)}, u32[]{:S(2)}) collective-permute-start(bf16[512,128]{1,0:T(8,128)(2,1)S(1)} %get-tuple-element.40), channel_id=1, source_target_pairs={{0,2},{1,3},{2,0},{3,1},{4,6},{5,7},{6,4},{7,5},{8,9},{9,8},{10,11... | collective-permute-start | bytes 393224 | tf_op jit(solution)/shard_map/ppermute | solution.py:362
  7.1 2.6 %shard_map.92 = (bf16[2048,128]{1,0:T(8,128)(2,1)S(1)}, f32[128,2048]{1,0:T(8,128)S(1)}) custom-call(bf16[128,2048]{1,0:T(8,128)(2,1)S(1)} %bitcast.22, bf16[128,2048]{1,0:T(8,128)(2,1)S(1)} %bitcast.12, bf16[128,2048]{1,0:T(8,128)(2,1)S(1)} %bitcast.18), custom_call_target="tpu_custom_call" | custom-call | flops 134217728 | bytes 3145728 | tf_op jit(solution)/shard_map/pallas_call | solution.py:333
  9.7 2.0 %collective-permute-done.1.refs_2_.refs_3_ = bf16[512,128]{1,0:T(8,128)(2,1)S(1)} collective-permute-done((bf16[512,128]{1,0:T(8,128)(2,1)S(1)}, bf16[512,128]{1,0:T(8,128)(2,1)S(1)}, u32[]{:S(2)}, u32[]{:S(2)}) %collective-permute-start.1) | collective-permute-done | bytes 131104 | tf_op jit(solution)/shard_map/ppermute | solution.py:362
  11.7 1.2 %collective-permute-done.2.refs_3_.refs_4_ = bf16[512,128]{1,0:T(8,128)(2,1)S(1)} collective-permute-done((bf16[512,128]{1,0:T(8,128)(2,1)S(1)}, bf16[512,128]{1,0:T(8,128)(2,1)S(1)}, u32[]{:S(2)}, u32[]{:S(2)}) %collective-permute-start.2) | collective-permute-done | bytes 131104 | tf_op jit(solution)/shard_map/ppermute | solution.py:362
  12.9 3.0 %collective-permute-start.3 = (bf16[512,128]{1,0:T(8,128)(2,1)S(1)}, bf16[512,128]{1,0:T(8,128)(2,1)S(1)}, u32[]{:S(2)}, u32[]{:S(2)}) collective-permute-start(bf16[512,128]{1,0:T(8,128)(2,1)S(1)} %shard_map.95), channel_id=1, source_target_pairs={{0,4},{1,5},{2,6},{3,7},{4,0},{5,1},{6,2},{7,3},{8,12},{9,13},{10,... | collective-permute-start | bytes 393224 | tf_op jit(solution)/shard_map/ppermute | solution.py:379
  15.9 5.3 %collective-permute-done.3.refs_0_ = bf16[512,128]{1,0:T(8,128)(2,1)S(1)} collective-permute-done((bf16[512,128]{1,0:T(8,128)(2,1)S(1)}, bf16[512,128]{1,0:T(8,128)(2,1)S(1)}, u32[]{:S(2)}, u32[]{:S(2)}) %collective-permute-start.3) | collective-permute-done | bytes 131104 | tf_op jit(solution)/shard_map/ppermute | solution.py:379
  21.5 0.9 %collective-permute-start.5 = (bf16[512,128]{1,0:T(8,128)(2,1)S(1)}, bf16[512,128]{1,0:T(8,128)(2,1)S(1)}, u32[]{:S(2)}, u32[]{:S(2)}) collective-permute-start(bf16[512,128]{1,0:T(8,128)(2,1)S(1)} %shard_map.97.refs_5_), channel_id=1, source_target_pairs={{0,1},{1,0},{2,3},{3,2},{4,5},{5,4},{6,7},{7,6},{8,10},{9,11},{10,... | collective-permute-start | bytes 393224 | tf_op jit(solution)/shard_map/ppermute | solution.py:362
  22.7 2.7 %collective-permute-start.6 = (bf16[512,128]{1,0:T(8,128)(2,1)S(1)}, bf16[512,128]{1,0:T(8,128)(2,1)S(1)}, u32[]{:S(2)}, u32[]{:S(2)}) collective-permute-start(bf16[512,128]{1,0:T(8,128)(2,1)S(1)} %get-tuple-element.46), channel_id=1, source_target_pairs={{0,3},{1,2},{2,1},{3,0},{4,7},{5,6},{6,5},{7,4},{8,11},{9,10},{10,... | collective-permute-start | bytes 393224 | tf_op jit(solution)/shard_map/ppermute | solution.py:362
  25.4 2.7 %collective-permute-done.5.refs_6_.refs_11_ = bf16[512,128]{1,0:T(8,128)(2,1)S(1)} collective-permute-done((bf16[512,128]{1,0:T(8,128)(2,1)S(1)}, bf16[512,128]{1,0:T(8,128)(2,1)S(1)}, u32[]{:S(2)}, u32[]{:S(2)}) %collective-permute-start.5) | collective-permute-done | bytes 131104 | tf_op jit(solution)/shard_map/ppermute | solution.py:362
  28.1 0.4 shard_map.99
  28.6 0.9 %collective-permute-done.6.refs_7_.refs_12_ = bf16[512,128]{1,0:T(8,128)(2,1)S(1)} collective-permute-done((bf16[512,128]{1,0:T(8,128)(2,1)S(1)}, bf16[512,128]{1,0:T(8,128)(2,1)S(1)}, u32[]{:S(2)}, u32[]{:S(2)}) %collective-permute-start.6) | collective-permute-done | bytes 131104 | tf_op jit(solution)/shard_map/ppermute | solution.py:362
  29.5 1.0 %shard_map.100 = (f32[128,512]{1,0:T(8,128)S(1)}, f32[128,128]{1,0:T(8,128)S(1)}, bf16[128,2048]{1,0:T(8,128)(2,1)S(1)}, bf16[544,128]{1,0:T(8,128)(2,1)S(1)}, b...) custom-call(bf16[128,2048]{1,0:T(8,128)(2,1)S(1)} %bitcast.24, ...), custom_call_target="tpu_custom_call" | custom-call | flops 134217728 | bytes 4825088 | tf_op jit(solution)/shard_map/pallas_call | solution.py:333
  30.5 1.8 %collective-permute-start.7 = (bf16[544,128]{1,0:T(8,128)(2,1)S(1)}, bf16[544,128]{1,0:T(8,128)(2,1)S(1)}, u32[]{:S(2)}, u32[]{:S(2)}) collective-permute-start(bf16[544,128]{1,0:T(8,128)(2,1)S(1)} %get-tuple-element.55), channel_id=1, source_target_pairs={{0,3},{1,2},{2,1},{3,0},{4,7},{5,6},{6,5},{7,4},{8,11},{9,10},{10,... | collective-permute-start | bytes 417800 | tf_op jit(solution)/shard_map/ppermute | solution.py:362
  32.3 1.0 %collective-permute-start.8 = (bf16[544,128]{1,0:T(8,128)(2,1)S(1)}, bf16[544,128]{1,0:T(8,128)(2,1)S(1)}, u32[]{:S(2)}, u32[]{:S(2)}) collective-permute-start(bf16[544,128]{1,0:T(8,128)(2,1)S(1)} %get-tuple-element.56), channel_id=1, source_target_pairs={{0,1},{1,0},{2,3},{3,2},{4,5},{5,4},{6,7},{7,6},{8,9},{9,8},{10,11... | collective-permute-start | bytes 417800 | tf_op jit(solution)/shard_map/ppermute | solution.py:362
  33.3 0.7 %collective-permute-start.9 = (bf16[544,128]{1,0:T(8,128)(2,1)S(1)}, bf16[544,128]{1,0:T(8,128)(2,1)S(1)}, u32[]{:S(2)}, u32[]{:S(2)}) collective-permute-start(bf16[544,128]{1,0:T(8,128)(2,1)S(1)} %get-tuple-element.57), channel_id=1, source_target_pairs={{0,2},{1,3},{2,0},{3,1},{4,6},{5,7},{6,4},{7,5},{8,10},{9,11},{10,... | collective-permute-start | bytes 417800 | tf_op jit(solution)/shard_map/ppermute | solution.py:362
  34.1 3.5 %shard_map.101 = (bf16[128,2048]{1,0:T(8,128)(2,1)}, bf16[128,2048]{1,0:T(8,128)(2,1)}, f32[128,2048]{1,0:T(8,128)S(1)}, f32[128,2048]{1,0:T(8,128)S(1)}, f32[8,128]{1,0:T(8,128)S(1)}) custom-call(bf16[128,2048]{1,0:T(8,128)(2,1)S(1)} %bitcast.25, bf16[128,2048]{1,0:T(8,128)(2,1)S(1)} %bitcast.13, bf16[128,2048]{1,0:T(8,128)(2,1)S(1)} %bitcast.19, ...), custom_call_target="tpu_custom_call" | custom-call | flops 335544320 | bytes 7680000 | tf_op jit(solution)/shard_map/pallas_call | solution.py:333
  37.6 0.9 %collective-permute-done.8.refs_2_.refs_3_ = bf16[544,128]{1,0:T(8,128)(2,1)S(1)} collective-permute-done((bf16[544,128]{1,0:T(8,128)(2,1)S(1)}, bf16[544,128]{1,0:T(8,128)(2,1)S(1)}, u32[]{:S(2)}, u32[]{:S(2)}) %collective-permute-start.8) | collective-permute-done | bytes 139296 | tf_op jit(solution)/shard_map/ppermute | solution.py:362
  38.8 1.8 %collective-permute-start.10 = (bf16[544,128]{1,0:T(8,128)(2,1)S(1)}, bf16[544,128]{1,0:T(8,128)(2,1)S(1)}, u32[]{:S(2)}, u32[]{:S(2)}) collective-permute-start(bf16[544,128]{1,0:T(8,128)(2,1)S(1)} %get-tuple-element.59), channel_id=1, source_target_pairs={{0,4},{1,5},{2,6},{3,7},{4,0},{5,1},{6,2},{7,3},{8,12},{9,13},{10,... | collective-permute-start | bytes 417800 | tf_op jit(solution)/shard_map/ppermute | solution.py:379
  40.6 2.0 %collective-permute-start.15 = (f32[16,128]{1,0:T(8,128)S(1)}, f32[16,128]{1,0:T(8,128)S(1)}, u32[]{:S(2)}, u32[]{:S(2)}) collective-permute-start(f32[16,128]{1,0:T(8,128)S(1)} %get-tuple-element.60.refs_5_), channel_id=1, source_target_pairs={{0,20},{1,21},{2,22},{3,23},{4,16},{5,17},{6,18},{7,19},{8,28},{9,... | collective-permute-start | bytes 24584 | tf_op jit(solution)/shard_map/ppermute | solution.py:399
  42.6 0.7 %collective-permute-start.14 = (f32[16,128]{1,0:T(8,128)S(1)}, f32[16,128]{1,0:T(8,128)S(1)}, u32[]{:S(2)}, u32[]{:S(2)}) collective-permute-start(f32[16,128]{1,0:T(8,128)S(1)} %get-tuple-element.60.refs_5_), channel_id=1, source_target_pairs={{0,16},{1,17},{2,18},{3,19},{4,20},{5,21},{6,22},{7,23},{8,24},{9,... | collective-permute-start | bytes 24584 | tf_op jit(solution)/shard_map/ppermute | solution.py:399
  43.2 3.1 %collective-permute-done.10.refs_0_ = bf16[544,128]{1,0:T(8,128)(2,1)S(1)} collective-permute-done((bf16[544,128]{1,0:T(8,128)(2,1)S(1)}, bf16[544,128]{1,0:T(8,128)(2,1)S(1)}, u32[]{:S(2)}, u32[]{:S(2)}) %collective-permute-start.10) | collective-permute-done | bytes 139296 | tf_op jit(solution)/shard_map/ppermute | solution.py:379
  46.5 1.2 %collective-permute-start.11 = (bf16[512,128]{1,0:T(8,128)(2,1)S(1)}, bf16[512,128]{1,0:T(8,128)(2,1)S(1)}, u32[]{:S(2)}, u32[]{:S(2)}) collective-permute-start(bf16[512,128]{1,0:T(8,128)(2,1)S(1)} %shard_map.103.refs_5_), channel_id=1, source_target_pairs={{0,3},{1,2},{2,1},{3,0},{4,7},{5,6},{6,5},{7,4},{8,9},{9,8},{10,11... | collective-permute-start | bytes 393224 | tf_op jit(solution)/shard_map/ppermute | solution.py:362
  47.8 0.3 collective-permute-start.12
  48.1 0.3 shard_map.105
  48.3 2.2 %collective-permute-start.13 = (bf16[512,128]{1,0:T(8,128)(2,1)S(1)}, bf16[512,128]{1,0:T(8,128)(2,1)S(1)}, u32[]{:S(2)}, u32[]{:S(2)}) collective-permute-start(bf16[512,128]{1,0:T(8,128)(2,1)S(1)} %get-tuple-element.61), channel_id=1, source_target_pairs={{0,2},{1,3},{2,0},{3,1},{4,6},{5,7},{6,4},{7,5},{8,11},{9,10},{10,... | collective-permute-start | bytes 393224 | tf_op jit(solution)/shard_map/ppermute | solution.py:362
  50.6 1.0 %shard_map.106 = (bf16[128,2048]{1,0:T(8,128)(2,1)}, bf16[128,2048]{1,0:T(8,128)(2,1)}) custom-call(bf16[128,2048]{1,0:T(8,128)(2,1)S(1)} %bitcast.14, bf16[128,2048]{1,0:T(8,128)(2,1)S(1)} %bitcast.20, f32[128,2048]{1,0:T(8,128)S(1)} %get-tuple-element.52.refs_2_, f32[128,2048]{1,0:T(8,128)S(1)} %get-tuple-element.53.refs_3_, ...), custom_call_target="tpu_custom_call" | custom-call | flops 67108864 | bytes 4325376 | tf_op jit(solution)/shard_map/pallas_call | solution.py:333
  51.8 1.7 %collective-permute-done.13.refs_6_ = bf16[512,128]{1,0:T(8,128)(2,1)S(1)} collective-permute-done((bf16[512,128]{1,0:T(8,128)(2,1)S(1)}, bf16[512,128]{1,0:T(8,128)(2,1)S(1)}, u32[]{:S(2)}, u32[]{:S(2)}) %collective-permute-start.13) | collective-permute-done | bytes 131104 | tf_op jit(solution)/shard_map/ppermute | solution.py:362
  53.5 0.3 collective-permute-done.12.refs_5_
  53.8 1.3 %shard_map.107 = (bf16[128,2048]{1,0:T(8,128)(2,1)}, bf16[128,2048]{1,0:T(8,128)(2,1)}, f32[16,128]{1,0:T(8,128)}) custom-call(bf16[128,2048]{1,0:T(8,128)(2,1)S(1)} %bitcast.15, bf16[128,2048]{1,0:T(8,128)(2,1)S(1)} %bitcast.21, f32[128,2048]{1,0:T(8,128)S(1)} %get-tuple-element.52.refs_2_, ...), custom_call_target="tpu_custom_call", output_to_operand_aliasing={{0}: (7, {}), {1}: (8, {})} | custom-call | flops 67108864 | bytes 5660672 | tf_op jit(solution)/shard_map/pallas_call | solution.py:333
  (29 shorter events, 1.7 us)
Async XLA Ops:
  0.6 4.3 %copy-start = (bf16[1,128,2048]{2,1,0:T(8,128)(2,1)S(1)}, bf16[1,128,2048]{2,1,0:T(8,128)(2,1)}, u32[]{:S(2)}) copy-start(bf16[1,128,2048]{2,1,0:T(8,128)(2,1)} %param.6) | copy-start | bytes 1572868
  0.6 4.3 %copy-start.1 = (bf16[1,128,2048]{2,1,0:T(8,128)(2,1)S(1)}, bf16[1,128,2048]{2,1,0:T(8,128)(2,1)}, u32[]{:S(2)}) copy-start(bf16[1,128,2048]{2,1,0:T(8,128)(2,1)} %param.7) | copy-start | bytes 1572868
  2.0 5.1 %copy-start.2 = (bf16[1,128,2048]{2,1,0:T(8,128)(2,1)S(1)}, bf16[1,128,2048]{2,1,0:T(8,128)(2,1)}, u32[]{:S(2)}) copy-start(bf16[1,128,2048]{2,1,0:T(8,128)(2,1)} %param.5) | copy-start | bytes 1572868
  2.0 7.7 %collective-permute-start = (bf16[512,128]{1,0:T(8,128)(2,1)S(1)}, bf16[512,128]{1,0:T(8,128)(2,1)S(1)}, u32[]{:S(2)}, u32[]{:S(2)}) collective-permute-start(bf16[512,128]{1,0:T(8,128)(2,1)S(1)} %shard_map.93.token_ref), channel_id=1, source_target_pairs={{0,1},{1,0},{2,3},{3,2},{4,5},{5,4},{6,7},{7,6},{8,10},{9,11},{10,... | collective-permute-start | bytes 393224 | tf_op jit(solution)/shard_map/ppermute | solution.py:362
  5.4 6.3 %collective-permute-start.1 = (bf16[512,128]{1,0:T(8,128)(2,1)S(1)}, bf16[512,128]{1,0:T(8,128)(2,1)S(1)}, u32[]{:S(2)}, u32[]{:S(2)}) collective-permute-start(bf16[512,128]{1,0:T(8,128)(2,1)S(1)} %get-tuple-element.40), channel_id=1, source_target_pairs={{0,2},{1,3},{2,0},{3,1},{4,6},{5,7},{6,4},{7,5},{8,9},{9,8},{10,11... | collective-permute-start | bytes 393224 | tf_op jit(solution)/shard_map/ppermute | solution.py:362
  7.0 5.9 %collective-permute-start.2 = (bf16[512,128]{1,0:T(8,128)(2,1)S(1)}, bf16[512,128]{1,0:T(8,128)(2,1)S(1)}, u32[]{:S(2)}, u32[]{:S(2)}) collective-permute-start(bf16[512,128]{1,0:T(8,128)(2,1)S(1)} %get-tuple-element.41), channel_id=1, source_target_pairs={{0,3},{1,2},{2,1},{3,0},{4,7},{5,6},{6,5},{7,4},{8,11},{9,10},{10,... | collective-permute-start | bytes 393224 | tf_op jit(solution)/shard_map/ppermute | solution.py:362
  12.9 8.3 %collective-permute-start.3 = (bf16[512,128]{1,0:T(8,128)(2,1)S(1)}, bf16[512,128]{1,0:T(8,128)(2,1)S(1)}, u32[]{:S(2)}, u32[]{:S(2)}) collective-permute-start(bf16[512,128]{1,0:T(8,128)(2,1)S(1)} %shard_map.95), channel_id=1, source_target_pairs={{0,4},{1,5},{2,6},{3,7},{4,0},{5,1},{6,2},{7,3},{8,12},{9,13},{10,... | collective-permute-start | bytes 393224 | tf_op jit(solution)/shard_map/ppermute | solution.py:379
  21.5 6.6 %copy-start.3 = (bf16[1,128,2048]{2,1,0:T(8,128)(2,1)S(1)}, bf16[1,128,2048]{2,1,0:T(8,128)(2,1)}, u32[]{:S(2)}) copy-start(bf16[1,128,2048]{2,1,0:T(8,128)(2,1)} %param.9) | copy-start | bytes 1572868
  21.5 6.5 %collective-permute-start.5 = (bf16[512,128]{1,0:T(8,128)(2,1)S(1)}, bf16[512,128]{1,0:T(8,128)(2,1)S(1)}, u32[]{:S(2)}, u32[]{:S(2)}) collective-permute-start(bf16[512,128]{1,0:T(8,128)(2,1)S(1)} %shard_map.97.refs_5_), channel_id=1, source_target_pairs={{0,1},{1,0},{2,3},{3,2},{4,5},{5,4},{6,7},{7,6},{8,10},{9,11},{10,... | collective-permute-start | bytes 393224 | tf_op jit(solution)/shard_map/ppermute | solution.py:362
  22.4 5.7 %collective-permute-start.4 = (bf16[512,128]{1,0:T(8,128)(2,1)S(1)}, bf16[512,128]{1,0:T(8,128)(2,1)S(1)}, u32[]{:S(2)}, u32[]{:S(2)}) collective-permute-start(bf16[512,128]{1,0:T(8,128)(2,1)S(1)} %shard_map.96.refs_5_), channel_id=1, source_target_pairs={{0,2},{1,3},{2,0},{3,1},{4,6},{5,7},{6,4},{7,5},{8,9},{9,8},{10,11... | collective-permute-start | bytes 393224 | tf_op jit(solution)/shard_map/ppermute | solution.py:362
  22.4 5.7 %copy-start.4 = (f32[2048]{0:T(1024)S(1)}, f32[2048]{0:T(1024)}, u32[]{:S(2)}) copy-start(f32[2048]{0:T(1024)} %param.8) | copy-start | bytes 24580
  22.7 6.9 %collective-permute-start.6 = (bf16[512,128]{1,0:T(8,128)(2,1)S(1)}, bf16[512,128]{1,0:T(8,128)(2,1)S(1)}, u32[]{:S(2)}, u32[]{:S(2)}) collective-permute-start(bf16[512,128]{1,0:T(8,128)(2,1)S(1)} %get-tuple-element.46), channel_id=1, source_target_pairs={{0,3},{1,2},{2,1},{3,0},{4,7},{5,6},{6,5},{7,4},{8,11},{9,10},{10,... | collective-permute-start | bytes 393224 | tf_op jit(solution)/shard_map/ppermute | solution.py:362
  30.5 7.0 %collective-permute-start.7 = (bf16[544,128]{1,0:T(8,128)(2,1)S(1)}, bf16[544,128]{1,0:T(8,128)(2,1)S(1)}, u32[]{:S(2)}, u32[]{:S(2)}) collective-permute-start(bf16[544,128]{1,0:T(8,128)(2,1)S(1)} %get-tuple-element.55), channel_id=1, source_target_pairs={{0,3},{1,2},{2,1},{3,0},{4,7},{5,6},{6,5},{7,4},{8,11},{9,10},{10,... | collective-permute-start | bytes 417800 | tf_op jit(solution)/shard_map/ppermute | solution.py:362
  32.3 6.1 %collective-permute-start.8 = (bf16[544,128]{1,0:T(8,128)(2,1)S(1)}, bf16[544,128]{1,0:T(8,128)(2,1)S(1)}, u32[]{:S(2)}, u32[]{:S(2)}) collective-permute-start(bf16[544,128]{1,0:T(8,128)(2,1)S(1)} %get-tuple-element.56), channel_id=1, source_target_pairs={{0,1},{1,0},{2,3},{3,2},{4,5},{5,4},{6,7},{7,6},{8,9},{9,8},{10,11... | collective-permute-start | bytes 417800 | tf_op jit(solution)/shard_map/ppermute | solution.py:362
  33.3 5.3 %collective-permute-start.9 = (bf16[544,128]{1,0:T(8,128)(2,1)S(1)}, bf16[544,128]{1,0:T(8,128)(2,1)S(1)}, u32[]{:S(2)}, u32[]{:S(2)}) collective-permute-start(bf16[544,128]{1,0:T(8,128)(2,1)S(1)} %get-tuple-element.57), channel_id=1, source_target_pairs={{0,2},{1,3},{2,0},{3,1},{4,6},{5,7},{6,4},{7,5},{8,10},{9,11},{10,... | collective-permute-start | bytes 417800 | tf_op jit(solution)/shard_map/ppermute | solution.py:362
  38.8 7.5 %collective-permute-start.10 = (bf16[544,128]{1,0:T(8,128)(2,1)S(1)}, bf16[544,128]{1,0:T(8,128)(2,1)S(1)}, u32[]{:S(2)}, u32[]{:S(2)}) collective-permute-start(bf16[544,128]{1,0:T(8,128)(2,1)S(1)} %get-tuple-element.59), channel_id=1, source_target_pairs={{0,4},{1,5},{2,6},{3,7},{4,0},{5,1},{6,2},{7,3},{8,12},{9,13},{10,... | collective-permute-start | bytes 417800 | tf_op jit(solution)/shard_map/ppermute | solution.py:379
  40.6 10.0 %collective-permute-start.15 = (f32[16,128]{1,0:T(8,128)S(1)}, f32[16,128]{1,0:T(8,128)S(1)}, u32[]{:S(2)}, u32[]{:S(2)}) collective-permute-start(f32[16,128]{1,0:T(8,128)S(1)} %get-tuple-element.60.refs_5_), channel_id=1, source_target_pairs={{0,20},{1,21},{2,22},{3,23},{4,16},{5,17},{6,18},{7,19},{8,28},{9,... | collective-permute-start | bytes 24584 | tf_op jit(solution)/shard_map/ppermute | solution.py:399
  42.6 8.0 %collective-permute-start.14 = (f32[16,128]{1,0:T(8,128)S(1)}, f32[16,128]{1,0:T(8,128)S(1)}, u32[]{:S(2)}, u32[]{:S(2)}) collective-permute-start(f32[16,128]{1,0:T(8,128)S(1)} %get-tuple-element.60.refs_5_), channel_id=1, source_target_pairs={{0,16},{1,17},{2,18},{3,19},{4,20},{5,21},{6,22},{7,23},{8,24},{9,... | collective-permute-start | bytes 24584 | tf_op jit(solution)/shard_map/ppermute | solution.py:399
  46.5 7.3 %collective-permute-start.11 = (bf16[512,128]{1,0:T(8,128)(2,1)S(1)}, bf16[512,128]{1,0:T(8,128)(2,1)S(1)}, u32[]{:S(2)}, u32[]{:S(2)}) collective-permute-start(bf16[512,128]{1,0:T(8,128)(2,1)S(1)} %shard_map.103.refs_5_), channel_id=1, source_target_pairs={{0,3},{1,2},{2,1},{3,0},{4,7},{5,6},{6,5},{7,4},{8,9},{9,8},{10,11... | collective-permute-start | bytes 393224 | tf_op jit(solution)/shard_map/ppermute | solution.py:362
  47.8 6.0 %collective-permute-start.12 = (bf16[512,128]{1,0:T(8,128)(2,1)S(1)}, bf16[512,128]{1,0:T(8,128)(2,1)S(1)}, u32[]{:S(2)}, u32[]{:S(2)}) collective-permute-start(bf16[512,128]{1,0:T(8,128)(2,1)S(1)} %shard_map.104.refs_6_), channel_id=1, source_target_pairs={{0,1},{1,0},{2,3},{3,2},{4,5},{5,4},{6,7},{7,6},{8,10},{9,11},{10,... | collective-permute-start | bytes 393224 | tf_op jit(solution)/shard_map/ppermute | solution.py:362
  48.3 5.2 %collective-permute-start.13 = (bf16[512,128]{1,0:T(8,128)(2,1)S(1)}, bf16[512,128]{1,0:T(8,128)(2,1)S(1)}, u32[]{:S(2)}, u32[]{:S(2)}) collective-permute-start(bf16[512,128]{1,0:T(8,128)(2,1)S(1)} %get-tuple-element.61), channel_id=1, source_target_pairs={{0,2},{1,3},{2,0},{3,1},{4,6},{5,7},{6,4},{7,5},{8,11},{9,10},{10,... | collective-permute-start | bytes 393224 | tf_op jit(solution)/shard_map/ppermute | solution.py:362
  50.6 1.2 %collective-permute-start.16 = (f32[16,128]{1,0:T(8,128)S(1)}, f32[16,128]{1,0:T(8,128)S(1)}, u32[]{:S(2)}, u32[]{:S(2)}) collective-permute-start(f32[16,128]{1,0:T(8,128)S(1)} %add_add_fusion.refs_9_), channel_id=1, source_target_pairs={{0,8},{8,0},{16,24},{24,16},{1,9},{9,1},{17,25},{25,17},{2,10},{10... | collective-permute-start | bytes 24584 | tf_op jit(solution)/shard_map/ppermute | solution.py:351

commit v8 on v7

--- a/solution.py
+++ b/solution.py
@@ -500,7 +500,7 @@
     gains = [gain_grad, swap(gain_grad, "dp", 1)]
     inputs = [k, v, key_part, value_part]
     outs = []
-    for slots in ((0,), (1, 2, 3)):
+    for slots in ((0,), (1,), (2, 3)):
         last = group - 1 in slots
         at = len(inputs) + len(slots)
         results = call(

time: 55.2 us -> 55.1 us (level)
  waiting for transfers between devices: 18.6 us -> 17.6 us
  Pallas kernels: 12.7 us -> 13.5 us
    pallas_call x16 -> x17, Pallas kernels: 12.7 us -> 13.5 us  [call(): pl.pallas_call(kernel, out_shape=tuple(outs), in_specs=[ins.get(i, VMEM)...]
    ppermute x12, waiting for transfers between devices: 10 us -> 9.21 us  [own_and_swapped(): results.append(lax.ppermute(pieces[slot], ('dp', 'seq'), pairs))]
  transfers between devices with their start and end apart: 17 -> 17, of which waited for: 12 -> 11; matrix products, arithmetic and copies ran while one was open for 0% -> 0% of each run, Pallas kernels for 16% -> 17%
where the time goes in v8:
time: 55.1 us; the launch traced here: 54.9 us
  starting transfers between devices  23 us (42%)
  waiting for transfers between devices  17.6 us (32%)
  Pallas kernels  13.5 us (25%)
  between operations  0.77 us (1%)
    ppermute x12, starting transfers between devices, own_and_swapped(): results.append(lax.ppermute(pieces[slot], ('dp', 'seq'), pairs))  15.5 us
    pallas_call x17, Pallas kernels, call(): pl.pallas_call(kernel, out_shape=tuple(outs), in_specs=[ins.get(i, VMEM)...  13.5 us
    ppermute x12, waiting for transfers between devices, own_and_swapped(): results.append(lax.ppermute(pieces[slot], ('dp', 'seq'), pairs))  9.21 us
    ppermute x2, waiting for transfers between devices, shifted(): return lax.ppermute(array, 'seq', pairs)  8.4 us
    ppermute x2, starting transfers between devices, shifted(): return lax.ppermute(array, 'seq', pairs)  4.74 us
    ppermute x2, starting transfers between devices, exclusive_scan(): gains.append(lax.ppermute(gains[0], ('dp', 'seq'), pairs))  2.66 us
  transfers between devices with their start and end apart: 17, of which 11 were waited for; matrix products, arithmetic and copies ran while one was open for 0% of the time, Pallas kernels for 17%

profile of v8, /device:TPU:0, one launch (start us, length us, event | category | flops | bytes accessed | tf_op | source)
XLA Modules:
  0.0 54.9 jit_solution(1690374271006421342)
XLA Ops:
  0.7 1.3 %shard_map.93.token_ref = bf16[512,128]{1,0:T(8,128)(2,1)S(1)} custom-call(bf16[128,2048]{1,0:T(8,128)(2,1)} %bitcast.10, bf16[128,2048]{1,0:T(8,128)(2,1)} %bitcast.17), custom_call_target="tpu_custom_call" | custom-call | flops 67108864 | bytes 1179648 | tf_op jit(solution)/shard_map/pallas_call | solution.py:333
  2.0 3.0 %collective-permute-start = (bf16[512,128]{1,0:T(8,128)(2,1)S(1)}, bf16[512,128]{1,0:T(8,128)(2,1)S(1)}, u32[]{:S(2)}, u32[]{:S(2)}) collective-permute-start(bf16[512,128]{1,0:T(8,128)(2,1)S(1)} %shard_map.93.token_ref), channel_id=1, source_target_pairs={{0,1},{1,0},{2,3},{3,2},{4,5},{5,4},{6,7},{7,6},{8,10},{9,11},{10,... | collective-permute-start | bytes 393224 | tf_op jit(solution)/shard_map/ppermute | solution.py:362
  5.0 0.4 shard_map.94
  5.4 1.6 %collective-permute-start.1 = (bf16[512,128]{1,0:T(8,128)(2,1)S(1)}, bf16[512,128]{1,0:T(8,128)(2,1)S(1)}, u32[]{:S(2)}, u32[]{:S(2)}) collective-permute-start(bf16[512,128]{1,0:T(8,128)(2,1)S(1)} %get-tuple-element.42), channel_id=1, source_target_pairs={{0,2},{1,3},{2,0},{3,1},{4,6},{5,7},{6,4},{7,5},{8,9},{9,8},{10,11... | collective-permute-start | bytes 393224 | tf_op jit(solution)/shard_map/ppermute | solution.py:362
  7.1 2.6 %shard_map.92 = (bf16[2048,128]{1,0:T(8,128)(2,1)S(1)}, f32[128,2048]{1,0:T(8,128)S(1)}) custom-call(bf16[128,2048]{1,0:T(8,128)(2,1)S(1)} %bitcast.24, bf16[128,2048]{1,0:T(8,128)(2,1)S(1)} %bitcast.12, bf16[128,2048]{1,0:T(8,128)(2,1)S(1)} %bitcast.19), custom_call_target="tpu_custom_call" | custom-call | flops 134217728 | bytes 3145728 | tf_op jit(solution)/shard_map/pallas_call | solution.py:333
  9.7 2.0 %collective-permute-done.1.refs_2_.refs_3_ = bf16[512,128]{1,0:T(8,128)(2,1)S(1)} collective-permute-done((bf16[512,128]{1,0:T(8,128)(2,1)S(1)}, bf16[512,128]{1,0:T(8,128)(2,1)S(1)}, u32[]{:S(2)}, u32[]{:S(2)}) %collective-permute-start.1) | collective-permute-done | bytes 131104 | tf_op jit(solution)/shard_map/ppermute | solution.py:362
  11.7 1.2 %collective-permute-done.2.refs_3_.refs_4_ = bf16[512,128]{1,0:T(8,128)(2,1)S(1)} collective-permute-done((bf16[512,128]{1,0:T(8,128)(2,1)S(1)}, bf16[512,128]{1,0:T(8,128)(2,1)S(1)}, u32[]{:S(2)}, u32[]{:S(2)}) %collective-permute-start.2) | collective-permute-done | bytes 131104 | tf_op jit(solution)/shard_map/ppermute | solution.py:362
  12.9 3.0 %collective-permute-start.3 = (bf16[512,128]{1,0:T(8,128)(2,1)S(1)}, bf16[512,128]{1,0:T(8,128)(2,1)S(1)}, u32[]{:S(2)}, u32[]{:S(2)}) collective-permute-start(bf16[512,128]{1,0:T(8,128)(2,1)S(1)} %shard_map.95), channel_id=1, source_target_pairs={{0,4},{1,5},{2,6},{3,7},{4,0},{5,1},{6,2},{7,3},{8,12},{9,13},{10,... | collective-permute-start | bytes 393224 | tf_op jit(solution)/shard_map/ppermute | solution.py:379
  15.9 5.3 %collective-permute-done.3.refs_0_ = bf16[512,128]{1,0:T(8,128)(2,1)S(1)} collective-permute-done((bf16[512,128]{1,0:T(8,128)(2,1)S(1)}, bf16[512,128]{1,0:T(8,128)(2,1)S(1)}, u32[]{:S(2)}, u32[]{:S(2)}) %collective-permute-start.3) | collective-permute-done | bytes 131104 | tf_op jit(solution)/shard_map/ppermute | solution.py:379
  21.5 0.9 %collective-permute-start.5 = (bf16[512,128]{1,0:T(8,128)(2,1)S(1)}, bf16[512,128]{1,0:T(8,128)(2,1)S(1)}, u32[]{:S(2)}, u32[]{:S(2)}) collective-permute-start(bf16[512,128]{1,0:T(8,128)(2,1)S(1)} %shard_map.97.refs_5_), channel_id=1, source_target_pairs={{0,1},{1,0},{2,3},{3,2},{4,5},{5,4},{6,7},{7,6},{8,10},{9,11},{10,... | collective-permute-start | bytes 393224 | tf_op jit(solution)/shard_map/ppermute | solution.py:362
  22.7 2.7 %collective-permute-start.6 = (bf16[512,128]{1,0:T(8,128)(2,1)S(1)}, bf16[512,128]{1,0:T(8,128)(2,1)S(1)}, u32[]{:S(2)}, u32[]{:S(2)}) collective-permute-start(bf16[512,128]{1,0:T(8,128)(2,1)S(1)} %get-tuple-element.48), channel_id=1, source_target_pairs={{0,3},{1,2},{2,1},{3,0},{4,7},{5,6},{6,5},{7,4},{8,11},{9,10},{10,... | collective-permute-start | bytes 393224 | tf_op jit(solution)/shard_map/ppermute | solution.py:362
  25.4 2.7 %collective-permute-done.5.refs_6_.refs_11_ = bf16[512,128]{1,0:T(8,128)(2,1)S(1)} collective-permute-done((bf16[512,128]{1,0:T(8,128)(2,1)S(1)}, bf16[512,128]{1,0:T(8,128)(2,1)S(1)}, u32[]{:S(2)}, u32[]{:S(2)}) %collective-permute-start.5) | collective-permute-done | bytes 131104 | tf_op jit(solution)/shard_map/ppermute | solution.py:362
  28.1 0.4 shard_map.99
  28.6 0.9 %collective-permute-done.6.refs_7_.refs_12_ = bf16[512,128]{1,0:T(8,128)(2,1)S(1)} collective-permute-done((bf16[512,128]{1,0:T(8,128)(2,1)S(1)}, bf16[512,128]{1,0:T(8,128)(2,1)S(1)}, u32[]{:S(2)}, u32[]{:S(2)}) %collective-permute-start.6) | collective-permute-done | bytes 131104 | tf_op jit(solution)/shard_map/ppermute | solution.py:362
  29.5 1.0 %shard_map.100 = (f32[128,512]{1,0:T(8,128)S(1)}, f32[128,128]{1,0:T(8,128)S(1)}, bf16[128,2048]{1,0:T(8,128)(2,1)S(1)}, bf16[544,128]{1,0:T(8,128)(2,1)S(1)}, b...) custom-call(bf16[128,2048]{1,0:T(8,128)(2,1)S(1)} %bitcast.26, ...), custom_call_target="tpu_custom_call" | custom-call | flops 134217728 | bytes 4825088 | tf_op jit(solution)/shard_map/pallas_call | solution.py:333
  30.5 1.8 %collective-permute-start.7 = (bf16[544,128]{1,0:T(8,128)(2,1)S(1)}, bf16[544,128]{1,0:T(8,128)(2,1)S(1)}, u32[]{:S(2)}, u32[]{:S(2)}) collective-permute-start(bf16[544,128]{1,0:T(8,128)(2,1)S(1)} %get-tuple-element.57), channel_id=1, source_target_pairs={{0,3},{1,2},{2,1},{3,0},{4,7},{5,6},{6,5},{7,4},{8,11},{9,10},{10,... | collective-permute-start | bytes 417800 | tf_op jit(solution)/shard_map/ppermute | solution.py:362
  32.3 1.0 %collective-permute-start.8 = (bf16[544,128]{1,0:T(8,128)(2,1)S(1)}, bf16[544,128]{1,0:T(8,128)(2,1)S(1)}, u32[]{:S(2)}, u32[]{:S(2)}) collective-permute-start(bf16[544,128]{1,0:T(8,128)(2,1)S(1)} %get-tuple-element.58), channel_id=1, source_target_pairs={{0,1},{1,0},{2,3},{3,2},{4,5},{5,4},{6,7},{7,6},{8,9},{9,8},{10,11... | collective-permute-start | bytes 417800 | tf_op jit(solution)/shard_map/ppermute | solution.py:362
  33.3 0.7 %collective-permute-start.9 = (bf16[544,128]{1,0:T(8,128)(2,1)S(1)}, bf16[544,128]{1,0:T(8,128)(2,1)S(1)}, u32[]{:S(2)}, u32[]{:S(2)}) collective-permute-start(bf16[544,128]{1,0:T(8,128)(2,1)S(1)} %get-tuple-element.59), channel_id=1, source_target_pairs={{0,2},{1,3},{2,0},{3,1},{4,6},{5,7},{6,4},{7,5},{8,10},{9,11},{10,... | collective-permute-start | bytes 417800 | tf_op jit(solution)/shard_map/ppermute | solution.py:362
  34.1 3.5 %shard_map.101 = (bf16[128,2048]{1,0:T(8,128)(2,1)}, bf16[128,2048]{1,0:T(8,128)(2,1)}, f32[128,2048]{1,0:T(8,128)S(1)}, f32[128,2048]{1,0:T(8,128)S(1)}, f32[8,128]{1,0:T(8,128)S(1)}) custom-call(bf16[128,2048]{1,0:T(8,128)(2,1)S(1)} %bitcast.27, bf16[128,2048]{1,0:T(8,128)(2,1)S(1)} %bitcast.13, bf16[128,2048]{1,0:T(8,128)(2,1)S(1)} %bitcast.20, ...), custom_call_target="tpu_custom_call" | custom-call | flops 335544320 | bytes 7680000 | tf_op jit(solution)/shard_map/pallas_call | solution.py:333
  37.6 0.9 %collective-permute-done.8.refs_2_.refs_3_ = bf16[544,128]{1,0:T(8,128)(2,1)S(1)} collective-permute-done((bf16[544,128]{1,0:T(8,128)(2,1)S(1)}, bf16[544,128]{1,0:T(8,128)(2,1)S(1)}, u32[]{:S(2)}, u32[]{:S(2)}) %collective-permute-start.8) | collective-permute-done | bytes 139296 | tf_op jit(solution)/shard_map/ppermute | solution.py:362
  38.8 1.8 %collective-permute-start.10 = (bf16[544,128]{1,0:T(8,128)(2,1)S(1)}, bf16[544,128]{1,0:T(8,128)(2,1)S(1)}, u32[]{:S(2)}, u32[]{:S(2)}) collective-permute-start(bf16[544,128]{1,0:T(8,128)(2,1)S(1)} %get-tuple-element.61), channel_id=1, source_target_pairs={{0,4},{1,5},{2,6},{3,7},{4,0},{5,1},{6,2},{7,3},{8,12},{9,13},{10,... | collective-permute-start | bytes 417800 | tf_op jit(solution)/shard_map/ppermute | solution.py:379
  40.6 2.0 %collective-permute-start.15 = (f32[16,128]{1,0:T(8,128)S(1)}, f32[16,128]{1,0:T(8,128)S(1)}, u32[]{:S(2)}, u32[]{:S(2)}) collective-permute-start(f32[16,128]{1,0:T(8,128)S(1)} %get-tuple-element.62.refs_5_), channel_id=1, source_target_pairs={{0,20},{1,21},{2,22},{3,23},{4,16},{5,17},{6,18},{7,19},{8,28},{9,... | collective-permute-start | bytes 24584 | tf_op jit(solution)/shard_map/ppermute | solution.py:399
  42.6 0.7 %collective-permute-start.14 = (f32[16,128]{1,0:T(8,128)S(1)}, f32[16,128]{1,0:T(8,128)S(1)}, u32[]{:S(2)}, u32[]{:S(2)}) collective-permute-start(f32[16,128]{1,0:T(8,128)S(1)} %get-tuple-element.62.refs_5_), channel_id=1, source_target_pairs={{0,16},{1,17},{2,18},{3,19},{4,20},{5,21},{6,22},{7,23},{8,24},{9,... | collective-permute-start | bytes 24584 | tf_op jit(solution)/shard_map/ppermute | solution.py:399
  43.2 3.1 %collective-permute-done.10.refs_0_ = bf16[544,128]{1,0:T(8,128)(2,1)S(1)} collective-permute-done((bf16[544,128]{1,0:T(8,128)(2,1)S(1)}, bf16[544,128]{1,0:T(8,128)(2,1)S(1)}, u32[]{:S(2)}, u32[]{:S(2)}) %collective-permute-start.10) | collective-permute-done | bytes 139296 | tf_op jit(solution)/shard_map/ppermute | solution.py:379
  46.5 1.2 %collective-permute-start.13 = (bf16[512,128]{1,0:T(8,128)(2,1)S(1)}, bf16[512,128]{1,0:T(8,128)(2,1)S(1)}, u32[]{:S(2)}, u32[]{:S(2)}) collective-permute-start(bf16[512,128]{1,0:T(8,128)(2,1)S(1)} %shard_map.103.refs_5_), channel_id=1, source_target_pairs={{0,3},{1,2},{2,1},{3,0},{4,7},{5,6},{6,5},{7,4},{8,9},{9,8},{10,11... | collective-permute-start | bytes 393224 | tf_op jit(solution)/shard_map/ppermute | solution.py:362
  47.8 0.3 collective-permute-start.11
  48.3 2.2 %collective-permute-start.12 = (bf16[512,128]{1,0:T(8,128)(2,1)S(1)}, bf16[512,128]{1,0:T(8,128)(2,1)S(1)}, u32[]{:S(2)}, u32[]{:S(2)}) collective-permute-start(bf16[512,128]{1,0:T(8,128)(2,1)S(1)} %get-tuple-element.63), channel_id=1, source_target_pairs={{0,2},{1,3},{2,0},{3,1},{4,6},{5,7},{6,4},{7,5},{8,11},{9,10},{10,... | collective-permute-start | bytes 393224 | tf_op jit(solution)/shard_map/ppermute | solution.py:362
  50.6 1.0 %shard_map.106 = (bf16[128,2048]{1,0:T(8,128)(2,1)}, bf16[128,2048]{1,0:T(8,128)(2,1)}) custom-call(bf16[128,2048]{1,0:T(8,128)(2,1)S(1)} %bitcast.14, bf16[128,2048]{1,0:T(8,128)(2,1)S(1)} %bitcast.21, f32[128,2048]{1,0:T(8,128)S(1)} %get-tuple-element.54.refs_2_, f32[128,2048]{1,0:T(8,128)S(1)} %get-tuple-element.55.refs_3_, ...), custom_call_target="tpu_custom_call" | custom-call | flops 67108864 | bytes 4325376 | tf_op jit(solution)/shard_map/pallas_call | solution.py:333
  51.6 0.9 %collective-permute-done.13.refs_4_ = bf16[512,128]{1,0:T(8,128)(2,1)S(1)} collective-permute-done((bf16[512,128]{1,0:T(8,128)(2,1)S(1)}, bf16[512,128]{1,0:T(8,128)(2,1)S(1)}, u32[]{:S(2)}, u32[]{:S(2)}) %collective-permute-start.13) | collective-permute-done | bytes 131104 | tf_op jit(solution)/shard_map/ppermute | solution.py:362
  52.5 1.0 %shard_map.107 = (bf16[128,2048]{1,0:T(8,128)(2,1)}, bf16[128,2048]{1,0:T(8,128)(2,1)}) custom-call(bf16[128,2048]{1,0:T(8,128)(2,1)S(1)} %bitcast.15, bf16[128,2048]{1,0:T(8,128)(2,1)S(1)} %bitcast.22, f32[128,2048]{1,0:T(8,128)S(1)} %get-tuple-element.54.refs_2_, ...), custom_call_target="tpu_custom_call", output_to_operand_aliasing={{0}: (5, {}), {1}: (6, {})} | custom-call | flops 67108864 | bytes 5373952 | tf_op jit(solution)/shard_map/pallas_call | solution.py:333
  53.5 0.3 collective-permute-done.11.refs_4_
  53.8 1.1 %shard_map.108 = (bf16[128,2048]{1,0:T(8,128)(2,1)}, bf16[128,2048]{1,0:T(8,128)(2,1)}, f32[16,128]{1,0:T(8,128)}) custom-call(bf16[128,2048]{1,0:T(8,128)(2,1)S(1)} %bitcast.16, bf16[128,2048]{1,0:T(8,128)(2,1)S(1)} %bitcast.23, f32[128,2048]{1,0:T(8,128)S(1)} %get-tuple-element.54.refs_2_, ...), custom_call_target="tpu_custom_call", output_to_operand_aliasing={{0}: (6, {}), {1}: (7, {})} | custom-call | flops 67108864 | bytes 5529600 | tf_op jit(solution)/shard_map/pallas_call | solution.py:333
  (30 shorter events, 1.7 us)
Async XLA Ops:
  0.6 4.3 %copy-start = (bf16[1,128,2048]{2,1,0:T(8,128)(2,1)S(1)}, bf16[1,128,2048]{2,1,0:T(8,128)(2,1)}, u32[]{:S(2)}) copy-start(bf16[1,128,2048]{2,1,0:T(8,128)(2,1)} %param.6) | copy-start | bytes 1572868
  0.6 4.3 %copy-start.1 = (bf16[1,128,2048]{2,1,0:T(8,128)(2,1)S(1)}, bf16[1,128,2048]{2,1,0:T(8,128)(2,1)}, u32[]{:S(2)}) copy-start(bf16[1,128,2048]{2,1,0:T(8,128)(2,1)} %param.7) | copy-start | bytes 1572868
  2.0 5.1 %copy-start.2 = (bf16[1,128,2048]{2,1,0:T(8,128)(2,1)S(1)}, bf16[1,128,2048]{2,1,0:T(8,128)(2,1)}, u32[]{:S(2)}) copy-start(bf16[1,128,2048]{2,1,0:T(8,128)(2,1)} %param.5) | copy-start | bytes 1572868
  2.0 7.7 %collective-permute-start = (bf16[512,128]{1,0:T(8,128)(2,1)S(1)}, bf16[512,128]{1,0:T(8,128)(2,1)S(1)}, u32[]{:S(2)}, u32[]{:S(2)}) collective-permute-start(bf16[512,128]{1,0:T(8,128)(2,1)S(1)} %shard_map.93.token_ref), channel_id=1, source_target_pairs={{0,1},{1,0},{2,3},{3,2},{4,5},{5,4},{6,7},{7,6},{8,10},{9,11},{10,... | collective-permute-start | bytes 393224 | tf_op jit(solution)/shard_map/ppermute | solution.py:362
  5.4 6.3 %collective-permute-start.1 = (bf16[512,128]{1,0:T(8,128)(2,1)S(1)}, bf16[512,128]{1,0:T(8,128)(2,1)S(1)}, u32[]{:S(2)}, u32[]{:S(2)}) collective-permute-start(bf16[512,128]{1,0:T(8,128)(2,1)S(1)} %get-tuple-element.42), channel_id=1, source_target_pairs={{0,2},{1,3},{2,0},{3,1},{4,6},{5,7},{6,4},{7,5},{8,9},{9,8},{10,11... | collective-permute-start | bytes 393224 | tf_op jit(solution)/shard_map/ppermute | solution.py:362
  7.0 5.9 %collective-permute-start.2 = (bf16[512,128]{1,0:T(8,128)(2,1)S(1)}, bf16[512,128]{1,0:T(8,128)(2,1)S(1)}, u32[]{:S(2)}, u32[]{:S(2)}) collective-permute-start(bf16[512,128]{1,0:T(8,128)(2,1)S(1)} %get-tuple-element.43), channel_id=1, source_target_pairs={{0,3},{1,2},{2,1},{3,0},{4,7},{5,6},{6,5},{7,4},{8,11},{9,10},{10,... | collective-permute-start | bytes 393224 | tf_op jit(solution)/shard_map/ppermute | solution.py:362
  12.9 8.3 %collective-permute-start.3 = (bf16[512,128]{1,0:T(8,128)(2,1)S(1)}, bf16[512,128]{1,0:T(8,128)(2,1)S(1)}, u32[]{:S(2)}, u32[]{:S(2)}) collective-permute-start(bf16[512,128]{1,0:T(8,128)(2,1)S(1)} %shard_map.95), channel_id=1, source_target_pairs={{0,4},{1,5},{2,6},{3,7},{4,0},{5,1},{6,2},{7,3},{8,12},{9,13},{10,... | collective-permute-start | bytes 393224 | tf_op jit(solution)/shard_map/ppermute | solution.py:379
  21.5 6.6 %copy-start.3 = (bf16[1,128,2048]{2,1,0:T(8,128)(2,1)S(1)}, bf16[1,128,2048]{2,1,0:T(8,128)(2,1)}, u32[]{:S(2)}) copy-start(bf16[1,128,2048]{2,1,0:T(8,128)(2,1)} %param.9) | copy-start | bytes 1572868
  21.5 6.5 %collective-permute-start.5 = (bf16[512,128]{1,0:T(8,128)(2,1)S(1)}, bf16[512,128]{1,0:T(8,128)(2,1)S(1)}, u32[]{:S(2)}, u32[]{:S(2)}) collective-permute-start(bf16[512,128]{1,0:T(8,128)(2,1)S(1)} %shard_map.97.refs_5_), channel_id=1, source_target_pairs={{0,1},{1,0},{2,3},{3,2},{4,5},{5,4},{6,7},{7,6},{8,10},{9,11},{10,... | collective-permute-start | bytes 393224 | tf_op jit(solution)/shard_map/ppermute | solution.py:362
  22.4 5.7 %collective-permute-start.4 = (bf16[512,128]{1,0:T(8,128)(2,1)S(1)}, bf16[512,128]{1,0:T(8,128)(2,1)S(1)}, u32[]{:S(2)}, u32[]{:S(2)}) collective-permute-start(bf16[512,128]{1,0:T(8,128)(2,1)S(1)} %shard_map.96.refs_5_), channel_id=1, source_target_pairs={{0,2},{1,3},{2,0},{3,1},{4,6},{5,7},{6,4},{7,5},{8,9},{9,8},{10,11... | collective-permute-start | bytes 393224 | tf_op jit(solution)/shard_map/ppermute | solution.py:362
  22.4 5.7 %copy-start.4 = (f32[2048]{0:T(1024)S(1)}, f32[2048]{0:T(1024)}, u32[]{:S(2)}) copy-start(f32[2048]{0:T(1024)} %param.8) | copy-start | bytes 24580
  22.7 6.9 %collective-permute-start.6 = (bf16[512,128]{1,0:T(8,128)(2,1)S(1)}, bf16[512,128]{1,0:T(8,128)(2,1)S(1)}, u32[]{:S(2)}, u32[]{:S(2)}) collective-permute-start(bf16[512,128]{1,0:T(8,128)(2,1)S(1)} %get-tuple-element.48), channel_id=1, source_target_pairs={{0,3},{1,2},{2,1},{3,0},{4,7},{5,6},{6,5},{7,4},{8,11},{9,10},{10,... | collective-permute-start | bytes 393224 | tf_op jit(solution)/shard_map/ppermute | solution.py:362
  30.5 7.0 %collective-permute-start.7 = (bf16[544,128]{1,0:T(8,128)(2,1)S(1)}, bf16[544,128]{1,0:T(8,128)(2,1)S(1)}, u32[]{:S(2)}, u32[]{:S(2)}) collective-permute-start(bf16[544,128]{1,0:T(8,128)(2,1)S(1)} %get-tuple-element.57), channel_id=1, source_target_pairs={{0,3},{1,2},{2,1},{3,0},{4,7},{5,6},{6,5},{7,4},{8,11},{9,10},{10,... | collective-permute-start | bytes 417800 | tf_op jit(solution)/shard_map/ppermute | solution.py:362
  32.3 6.1 %collective-permute-start.8 = (bf16[544,128]{1,0:T(8,128)(2,1)S(1)}, bf16[544,128]{1,0:T(8,128)(2,1)S(1)}, u32[]{:S(2)}, u32[]{:S(2)}) collective-permute-start(bf16[544,128]{1,0:T(8,128)(2,1)S(1)} %get-tuple-element.58), channel_id=1, source_target_pairs={{0,1},{1,0},{2,3},{3,2},{4,5},{5,4},{6,7},{7,6},{8,9},{9,8},{10,11... | collective-permute-start | bytes 417800 | tf_op jit(solution)/shard_map/ppermute | solution.py:362
  33.3 5.3 %collective-permute-start.9 = (bf16[544,128]{1,0:T(8,128)(2,1)S(1)}, bf16[544,128]{1,0:T(8,128)(2,1)S(1)}, u32[]{:S(2)}, u32[]{:S(2)}) collective-permute-start(bf16[544,128]{1,0:T(8,128)(2,1)S(1)} %get-tuple-element.59), channel_id=1, source_target_pairs={{0,2},{1,3},{2,0},{3,1},{4,6},{5,7},{6,4},{7,5},{8,10},{9,11},{10,... | collective-permute-start | bytes 417800 | tf_op jit(solution)/shard_map/ppermute | solution.py:362
  38.8 7.5 %collective-permute-start.10 = (bf16[544,128]{1,0:T(8,128)(2,1)S(1)}, bf16[544,128]{1,0:T(8,128)(2,1)S(1)}, u32[]{:S(2)}, u32[]{:S(2)}) collective-permute-start(bf16[544,128]{1,0:T(8,128)(2,1)S(1)} %get-tuple-element.61), channel_id=1, source_target_pairs={{0,4},{1,5},{2,6},{3,7},{4,0},{5,1},{6,2},{7,3},{8,12},{9,13},{10,... | collective-permute-start | bytes 417800 | tf_op jit(solution)/shard_map/ppermute | solution.py:379
  40.6 10.0 %collective-permute-start.15 = (f32[16,128]{1,0:T(8,128)S(1)}, f32[16,128]{1,0:T(8,128)S(1)}, u32[]{:S(2)}, u32[]{:S(2)}) collective-permute-start(f32[16,128]{1,0:T(8,128)S(1)} %get-tuple-element.62.refs_5_), channel_id=1, source_target_pairs={{0,20},{1,21},{2,22},{3,23},{4,16},{5,17},{6,18},{7,19},{8,28},{9,... | collective-permute-start | bytes 24584 | tf_op jit(solution)/shard_map/ppermute | solution.py:399
  42.6 8.0 %collective-permute-start.14 = (f32[16,128]{1,0:T(8,128)S(1)}, f32[16,128]{1,0:T(8,128)S(1)}, u32[]{:S(2)}, u32[]{:S(2)}) collective-permute-start(f32[16,128]{1,0:T(8,128)S(1)} %get-tuple-element.62.refs_5_), channel_id=1, source_target_pairs={{0,16},{1,17},{2,18},{3,19},{4,20},{5,21},{6,22},{7,23},{8,24},{9,... | collective-permute-start | bytes 24584 | tf_op jit(solution)/shard_map/ppermute | solution.py:399
  46.5 6.0 %collective-permute-start.13 = (bf16[512,128]{1,0:T(8,128)(2,1)S(1)}, bf16[512,128]{1,0:T(8,128)(2,1)S(1)}, u32[]{:S(2)}, u32[]{:S(2)}) collective-permute-start(bf16[512,128]{1,0:T(8,128)(2,1)S(1)} %shard_map.103.refs_5_), channel_id=1, source_target_pairs={{0,3},{1,2},{2,1},{3,0},{4,7},{5,6},{6,5},{7,4},{8,9},{9,8},{10,11... | collective-permute-start | bytes 393224 | tf_op jit(solution)/shard_map/ppermute | solution.py:362
  47.8 6.0 %collective-permute-start.11 = (bf16[512,128]{1,0:T(8,128)(2,1)S(1)}, bf16[512,128]{1,0:T(8,128)(2,1)S(1)}, u32[]{:S(2)}, u32[]{:S(2)}) collective-permute-start(bf16[512,128]{1,0:T(8,128)(2,1)S(1)} %shard_map.104.refs_6_), channel_id=1, source_target_pairs={{0,1},{1,0},{2,3},{3,2},{4,5},{5,4},{6,7},{7,6},{8,10},{9,11},{10,... | collective-permute-start | bytes 393224 | tf_op jit(solution)/shard_map/ppermute | solution.py:362
  48.3 5.2 %collective-permute-start.12 = (bf16[512,128]{1,0:T(8,128)(2,1)S(1)}, bf16[512,128]{1,0:T(8,128)(2,1)S(1)}, u32[]{:S(2)}, u32[]{:S(2)}) collective-permute-start(bf16[512,128]{1,0:T(8,128)(2,1)S(1)} %get-tuple-element.63), channel_id=1, source_target_pairs={{0,2},{1,3},{2,0},{3,1},{4,6},{5,7},{6,4},{7,5},{8,11},{9,10},{10,... | collective-permute-start | bytes 393224 | tf_op jit(solution)/shard_map/ppermute | solution.py:362
  50.6 2.9 %collective-permute-start.16 = (f32[16,128]{1,0:T(8,128)S(1)}, f32[16,128]{1,0:T(8,128)S(1)}, u32[]{:S(2)}, u32[]{:S(2)}) collective-permute-start(f32[16,128]{1,0:T(8,128)S(1)} %add_add_fusion.refs_8_), channel_id=1, source_target_pairs={{0,8},{8,0},{16,24},{24,16},{1,9},{9,1},{17,25},{25,17},{2,10},{10... | collective-permute-start | bytes 24584 | tf_op jit(solution)/shard_map/ppermute | solution.py:351
